TPU v7x, 256 devices: a whole 4x4x8 slice. The times are simulated.
256 devices in a mesh: row: 32 (over z_lo, y, core), col: 8 (over z_hi, x).
Axes of the slice: x: 4, y: 4, z: 8 (z_hi: 2, z_lo: 4; z = z_hi * 4 + z_lo), core: 2. Of those that a mesh axis runs over, the one named last changes fastest.
Arguments:
- right_sides: bfloat16 [16384, 128, 128], P(('col', 'row')), may hold values from -6 to 6
- col_factors: bfloat16 [2, 16384, 128, 128], P(None, ('col', 'row')), may hold values from -0.5 to 0.5
- col_ranks: int32 [2, 16384], P(None, ('col', 'row')), may hold values from 64 to 128
- block_order: int32 [256, 64], P(('col', 'row')), may hold values from 0 to 63, each once within a row
- mid_factors: bfloat16 [8, 2048, 128, 128], P('col', 'row'), may hold values from -0.5 to 0.5
- mid_ranks: int32 [8, 2048], P('col', 'row'), may hold values from 64 to 128
- row_factors: bfloat16 [2048, 128, 128], P('row'), may hold values from -0.5 to 0.5
- row_ranks: int32 [2048], P('row'), may hold values from 64 to 128
Outputs:
- product: bfloat16 [2048, 128, 128], P(('row', 'col'))
Inputs may be any that keep to these rules, and one draw needn't show every extreme that they name: Each row of block_order is a permutation of 0 to 63.
All inputs are finite; a program needn't handle non-finite values.
Results may differ from a plain program's by a relative error of at most 0.014.
Values may be sent and summed in bfloat16 or wider, within the bound.
No kernel may reach another device: no remote copies, remote signals or barrier semaphores. Data moves between devices by JAX's collectives and lax.ppermute only.
A program may use at most 64 MiB of HBM per device.

v0:
```python
import jax
import jax.numpy as jnp
from jax import lax
from jax.sharding import PartitionSpec as P


def rank_mask(factors, ranks):
    keep = lax.broadcasted_iota(jnp.int32, (1, factors.shape[-1]), 1) < ranks[..., None]
    return jnp.where(keep[..., None, :], factors, jnp.zeros((), factors.dtype))


def level(blocks, factors, ranks):
    return jnp.einsum(
        "nrk,nkj->nrj", blocks, rank_mask(factors, ranks), preferred_element_type=jnp.float32
    )


def pair_halves(blocks):
    block_count = blocks.shape[0]
    side_count = blocks.shape[1]
    block_width = blocks.shape[2]
    parts = blocks.reshape(block_count // 2, 2, side_count, 2, block_width // 2)
    return parts.transpose(0, 3, 2, 1, 4).reshape(block_count, side_count, block_width)


def shards(
    right_sides, col_factors, col_ranks, block_order, mid_factors, mid_ranks, row_factors, row_ranks
):
    first = pair_halves(level(right_sides, col_factors[0], col_ranks[0])).astype(jnp.bfloat16)
    middle = level(first, col_factors[1], col_ranks[1]).astype(jnp.bfloat16)
    regrouped = lax.all_to_all(
        jnp.take(middle, block_order[0], axis=0), "row", split_axis=0, concat_axis=0, tiled=True
    )
    inner = pair_halves(level(regrouped, mid_factors[0], mid_ranks[0])).astype(jnp.bfloat16)
    partial_value = level(inner, row_factors, row_ranks)
    return lax.psum_scatter(partial_value, "col", scatter_dimension=0, tiled=True).astype(
        jnp.bfloat16
    )


def solution(mesh):
    in_specs = (
        P(("col", "row"), None, None),
        P(None, ("col", "row"), None, None),
        P(None, ("col", "row")),
        P(("col", "row"), None),
        P("col", "row", None, None),
        P("col", "row"),
        P("row", None, None),
        P("row"),
    )
    out_specs = P(("row", "col"), None, None)
    return jax.shard_map(shards, mesh=mesh, in_specs=in_specs, out_specs=out_specs, check_vma=False)
```

profile of v0, /device:TPU:38, one launch (start us, length us, event | category | flops | bytes accessed | tf_op | source)
XLA Modules:
  0.0 223.2 jit_solution(12771876566022111913)
XLA Ops:
  6.5 0.0 copy-start
  6.5 0.8 fusion.18
  7.3 0.7 compare_and_fusion
  8.0 0.8 slice_bitcast_fusion
  8.8 0.1 iota_compare_fusion.2
  8.9 3.2 %fusion.11 = bf16[64,128,128]{2,1,0:T(8,128)(2,1)S(1)} fusion(bf16[64,128,128]{2,1,0:T(8,128)(2,1)S(1)} %copy-done, bf16[2,64,128,128]{3,2,1,0:T(8,128)(2,1)} %param.9, pred[64,128]{1,0:T(8,128)(4,1)S(1)} %get-tuple-element.8), kind=kOutput, calls=%fused_computation.16 | convolution fusion | flops 270532608 | bytes 6299648 | tf_op jit(solution)/shard_map/nrk,nkj->nrj/dot_general | solution.py:13
  12.1 0.3 copy.13
  12.4 1.9 copy-done.4
  14.3 2.2 fusion.12
  16.5 3.7 %gather_fusion = bf16[64,128,128]{2,1,0:T(8,128)(2,1)} fusion(bf16[64,128,128]{2,1,0:T(8,128)(2,1)} %fusion.12, s32[1024]{0:T(1024)S(1)} %pad_clamp_fusion), kind=kCustom, calls=%fused_computation | custom fusion | bytes 4194560 | tf_op jit(solution)/shard_map/jit(_take)/gather | solution.py:32
  20.2 3.2 %broadcast_select_fusion = bf16[64,128,128]{2,1,0:T(8,128)(2,1)} fusion(bf16[64,128,128]{2,1,0:T(8,128)(2,1)} %gather_fusion, pred[64]{0:T(512)(128)(4,1)S(1)} %compare_and_fusion), kind=kLoop, calls=%fused_computation.11 | loop fusion | flops 1048576 | bytes 4194368 | tf_op jit(solution)/shard_map/jit(_take)/select_n | solution.py:32
  23.4 9.0 %all-to-all-start = ((bf16[64,128,128]{2,1,0:T(8,128)(2,1)}), bf16[64,128,128]{2,1,0:T(8,128)(2,1)}, u32[]{:S(2)}, u32[]{:S(2)}) async-start(bf16[64,128,128]{2,1,0:T(8,128)(2,1)} %broadcast_select_fusion), calls=%async_computation | async-start | bytes 4194304 | tf_op jit(solution)/shard_map/all_to_all | solution.py:31
  32.4 0.0 reduce-scatter.2.cloned.1.call-start
  32.4 0.1 iota_compare_fusion.1
  32.5 0.0 copy-done.3
  32.5 0.1 iota_compare_fusion
  32.6 46.4 %all-to-all-done = bf16[64,128,128]{2,1,0:T(8,128)(2,1)} async-done(((bf16[64,128,128]{2,1,0:T(8,128)(2,1)}), bf16[64,128,128]{2,1,0:T(8,128)(2,1)}, u32[]{:S(2)}, u32[]{:S(2)}) %all-to-all-start) | async-done | bytes 2097184 | tf_op jit(solution)/shard_map/all_to_all | solution.py:31
  79.0 3.8 %fusion.13 = bf16[64,128,128]{1,2,0:T(8,128)(2,1)S(1)} fusion(bf16[64,128,128]{2,1,0:T(8,128)(2,1)} %all-to-all-done, bf16[1,64,128,128]{3,2,1,0:T(8,128)(2,1)} %param.12, pred[64,128]{1,0:T(8,128)(4,1)S(1)} %iota_compare_fusion.1), kind=kOutput, calls=%fused_computation.18 | convolution fusion | flops 270532608 | bytes 6299648 | tf_op jit(solution)/shard_map/nrk,nkj->nrj/dot_general | solution.py:13
  82.8 0.2 copy.15
  83.0 1.4 copy-done.1
  84.4 2.8 %fusion.3 = f32[64,128,128]{2,1,0:T(8,128)} fusion(bf16[64,128,128]{1,2,0:T(8,128)(2,1)S(1)} %bitcast.40, bf16[64,128,128]{2,1,0:T(8,128)(2,1)S(1)} %copy-done.1, pred[64,128]{1,0:T(8,128)(4,1)S(1)} %iota_compare_fusion), kind=kOutput, calls=%fused_computation.7 | convolution fusion | flops 269484032 | bytes 8396800 | tf_op jit(solution)/shard_map/nrk,nkj->nrj/dot_general | solution.py:13
  87.2 0.0 reduce-scatter.2.cloned.1.call-update
  87.2 127.3 %reduce-scatter.2.cloned.1.call-done = f32[8,128,128]{2,1,0:T(8,128)} async-done(((f32[64,128,128]{2,1,0:T(8,128)}), f32[8,128,128]{2,1,0:T(8,128)}) %reduce-scatter.2.cloned.1.call-update) | async-done | bytes 524304 | tf_op jit(solution)/shard_map/reduce_scatter | solution.py:36
  214.5 1.8 convert_element_type.43
  (7 shorter events, 0.0 us)
Async XLA Ops:
  6.5 2.3 %copy-start = (bf16[64,128,128]{2,1,0:T(8,128)(2,1)S(1)}, bf16[64,128,128]{2,1,0:T(8,128)(2,1)}, u32[]{:S(2)}) copy-start(bf16[64,128,128]{2,1,0:T(8,128)(2,1)} %param.8) | copy-start | bytes 6291460
  12.1 2.2 copy-start.4
  23.4 9.0 %copy-start.2 = (s32[1,64]{1,0:T(1,128)S(1)}, s32[1,64]{1,0:T(1,128)}, u32[]{:S(2)}) copy-start(s32[1,64]{1,0:T(1,128)} %param.13) | copy-start | bytes 772
  23.4 9.1 %copy-start.3 = (s32[64]{0:T(128)S(1)}, s32[64]{0:T(128)}, u32[]{:S(2)}) copy-start(s32[64]{0:T(128)} %param.15) | copy-start | bytes 772
  23.4 55.6 %all-to-all-start = ((bf16[64,128,128]{2,1,0:T(8,128)(2,1)}), bf16[64,128,128]{2,1,0:T(8,128)(2,1)}, u32[]{:S(2)}, u32[]{:S(2)}) async-start(bf16[64,128,128]{2,1,0:T(8,128)(2,1)} %broadcast_select_fusion), calls=%async_computation | async-start | bytes 4194304 | tf_op jit(solution)/shard_map/all_to_all | solution.py:31
  32.4 182.2 %reduce-scatter.2.cloned.1.call-start = ((), (), s32[]{:S(2)}) async-start(), calls=%async_computation.2 | async-start | bytes 4718592 | tf_op jit(solution)/shard_map/reduce_scatter | solution.py:36
  82.8 1.6 copy-start.1
Sparse Core Ops, SparseCore 0:
  87.3 127.1 reduce-scatter.1
where the time goes:
time: 225 us; the launch traced here: 223 us
  waiting for transfers between devices  174 us (77%)
  between operations  13.5 us (6%)
  matrix products  12.1 us (5%)
  starting transfers between devices  9.02 us (4%)
  local copies, waits for them, and re-layouts  8.25 us (4%)
  other arithmetic  6.65 us (3%)
    reduce_scatter x1, waiting for transfers between devices, shards(): lax.psum_scatter(partial_value, 'col', scatter_dimension=0, tiled=True)  127 us
    all_to_all x1, waiting for transfers between devices, shards(): lax.all_to_all(jnp.take(middle, block_order[0], axis=0), 'row', split_axi...  46.4 us
    dot_general x4, matrix products, level(): jnp.einsum('nrk,nkj->nrj', blocks, rank_mask(factors, ranks), preferred_e...  12.1 us
    all_to_all x1, starting transfers between devices, shards(): lax.all_to_all(jnp.take(middle, block_order[0], axis=0), 'row', split_axi...  8.98 us
  transfers between devices with their start and end apart: 2, of which 2 were waited for; matrix products, arithmetic and copies ran while one was open for 0% of the time, Pallas kernels for 0%

commit v1 on v0

v1 whole, which is shorter than its diff:
```python
import functools

import jax
import jax.numpy as jnp
from jax import lax
from jax.experimental import pallas as pl
from jax.experimental.pallas import tpu as pltpu
from jax.sharding import PartitionSpec as P

BW = 128
HALF = BW // 2
R = 128
PB = 64
STEP = 8
N_X = 4
N_Z = 2
OWN = 8
CHUNKS = (64, 64)


def masked_dot(blocks, factors, rank):
    product = jnp.dot(blocks, factors, preferred_element_type=jnp.float32)
    lane = lax.broadcasted_iota(jnp.int32, product.shape, 1)
    return jnp.where(lane < rank, product, 0.0)


def pair(even, odd):
    lane = lax.broadcasted_iota(jnp.int32, even.shape, 1)
    front = jnp.where(lane < HALF, even, pltpu.roll(odd, HALF, 1))
    back = jnp.where(lane < HALF, pltpu.roll(even, HALF, 1), odd)
    return front.astype(jnp.bfloat16), back.astype(jnp.bfloat16)


def col_kernel(start, rows, order_ref, rank_ref, z_ref, w_ref, out_ref, place_ref):
    step = pl.program_id(0)

    @pl.when(step == 0)
    def _():
        def put(k, carry):
            place_ref[order_ref[k]] = k
            return carry

        lax.fori_loop(0, PB, put, 0)

    for j in range(0, STEP, 2):
        b = step * STEP + j
        even = masked_dot(z_ref[j, start : start + rows], w_ref[0, j], rank_ref[0, b])
        odd = masked_dot(z_ref[j + 1, start : start + rows], w_ref[0, j + 1], rank_ref[0, b + 1])
        for i, block in enumerate(pair(even, odd)):
            middle = masked_dot(block, w_ref[1, j + i], rank_ref[1, b + i])
            out_ref[place_ref[b + i]] = middle.astype(jnp.bfloat16)


def col_levels(start, rows, order, ranks, right_sides, factors):
    return pl.pallas_call(
        functools.partial(col_kernel, start, rows),
        out_shape=jax.ShapeDtypeStruct((PB, rows, BW), jnp.bfloat16),
        grid_spec=pltpu.PrefetchScalarGridSpec(
            num_scalar_prefetch=2,
            grid=(PB // STEP,),
            in_specs=[
                pl.BlockSpec((STEP, R, BW), lambda g, *_: (g, 0, 0)),
                pl.BlockSpec((2, STEP, BW, BW), lambda g, *_: (0, g, 0, 0)),
            ],
            out_specs=pl.BlockSpec((PB, rows, BW), lambda g, *_: (0, 0, 0)),
            scratch_shapes=[pltpu.SMEM((PB,), jnp.int32)],
        ),
        cost_estimate=pl.CostEstimate(
            flops=4 * PB * rows * BW * BW, bytes_accessed=8 * 2**20, transcendentals=0
        ),
        name="col_levels",
    )(order, ranks, right_sides, factors)


def mid_kernel(x_ref, rank_ref, z_ref, w_ref, *out_refs):
    d, h = pl.program_id(0), pl.program_id(1)
    base = (h * N_X + lax.rem(x_ref[0] + d, N_X)) * STEP
    done = []
    for j in range(0, STEP, 2):
        even = masked_dot(z_ref[j], w_ref[j], rank_ref[base + j])
        odd = masked_dot(z_ref[j + 1], w_ref[j + 1], rank_ref[base + j + 1])
        done.extend(pair(even, odd))
    for k, out_ref in enumerate(out_refs):

        @pl.when(d == k)
        def _():
            for j, block in enumerate(done):
                out_ref[h * STEP + j] = block


def mid_level(rows, x, ranks, blocks, factors):
    def at(d, h, x_ref, rank_ref):
        return (h * N_X + lax.rem(x_ref[0] + d, N_X), 0, 0)

    piece = (N_Z * STEP, rows, BW)
    return pl.pallas_call(
        mid_kernel,
        out_shape=[jax.ShapeDtypeStruct(piece, jnp.bfloat16)] * N_X,
        grid_spec=pltpu.PrefetchScalarGridSpec(
            num_scalar_prefetch=2,
            grid=(N_X, N_Z),
            in_specs=[
                pl.BlockSpec((STEP, rows, BW), at),
                pl.BlockSpec((STEP, BW, BW), at),
            ],
            out_specs=[pl.BlockSpec(piece, lambda d, h, *_: (0, 0, 0))] * N_X,
        ),
        cost_estimate=pl.CostEstimate(
            flops=2 * PB * rows * BW * BW, bytes_accessed=6 * 2**20, transcendentals=0
        ),
        name="mid_level",
    )(x, ranks, blocks, factors)


def total_of(refs):
    total = refs[0][...].astype(jnp.float32)
    for ref in refs[1:]:
        total = total + ref[...].astype(jnp.float32)
    return total


def sum_kernel(z_ref, *refs):
    refs[-1][...] = total_of(refs[:-1]).astype(jnp.bfloat16)


def sum_other(rows, z, parts):
    return pl.pallas_call(
        sum_kernel,
        out_shape=jax.ShapeDtypeStruct((STEP, rows, BW), jnp.bfloat16),
        grid_spec=pltpu.PrefetchScalarGridSpec(
            num_scalar_prefetch=1,
            grid=(1,),
            in_specs=[pl.BlockSpec((STEP, rows, BW), lambda g, z_ref: (1 - z_ref[0], 0, 0))] * N_X,
            out_specs=pl.BlockSpec((STEP, rows, BW), lambda g, z_ref: (0, 0, 0)),
        ),
        cost_estimate=pl.CostEstimate(
            flops=4 * STEP * rows * BW, bytes_accessed=10 * STEP * rows * BW, transcendentals=0
        ),
        name="sum_other",
    )(z, *parts)


def row_kernel(chunks, me_ref, rank_ref, w_ref, *refs):
    out_ref = refs[-1]
    base = me_ref[0] * OWN
    start = 0
    for n, rows in enumerate(chunks):
        own = refs[n * (N_X + 1) : (n + 1) * (N_X + 1)]
        total = total_of(own).astype(jnp.bfloat16)
        for j in range(OWN):
            product = masked_dot(total[j], w_ref[j], rank_ref[base + j])
            out_ref[j, start : start + rows] = product.astype(jnp.bfloat16)
        start += rows


def row_level(chunks, me, ranks, factors, parts):
    in_specs = [pl.BlockSpec((OWN, BW, BW), lambda g, me_ref, *_: (me_ref[0], 0, 0))]
    for rows in chunks:
        half = pl.BlockSpec(
            (OWN, rows, BW), lambda g, me_ref, *_: (lax.div(me_ref[0], N_X), 0, 0)
        )
        in_specs += [half] * N_X + [pl.BlockSpec((OWN, rows, BW), lambda g, *_: (0, 0, 0))]
    return pl.pallas_call(
        functools.partial(row_kernel, chunks),
        out_shape=jax.ShapeDtypeStruct((OWN, R, BW), jnp.bfloat16),
        grid_spec=pltpu.PrefetchScalarGridSpec(
            num_scalar_prefetch=2,
            grid=(1,),
            in_specs=in_specs,
            out_specs=pl.BlockSpec((OWN, R, BW), lambda g, *_: (0, 0, 0)),
        ),
        cost_estimate=pl.CostEstimate(
            flops=2 * OWN * R * BW * BW, bytes_accessed=2**20, transcendentals=0
        ),
        name="row_level",
    )(me, ranks, factors, *parts)


def around_x(value, d):
    pairs = [(z * N_X + x, z * N_X + (x + d) % N_X) for z in range(N_Z) for x in range(N_X)]
    return lax.ppermute(value, "col", pairs)


def across_z(value):
    half = N_X * N_Z // 2
    return lax.ppermute(value, "col", [(i, (i + half) % (2 * half)) for i in range(2 * half)])


def shards(
    right_sides, col_factors, col_ranks, block_order, mid_factors, mid_ranks, row_factors, row_ranks
):
    me = lax.axis_index("col").astype(jnp.int32)
    x = lax.rem(me, N_X).reshape(1)
    z = lax.div(me, N_X).reshape(1)
    start = 0
    middles = []
    for rows in CHUNKS:
        middles.append(
            col_levels(start, rows, block_order[0], col_ranks, right_sides, col_factors)
        )
        start += rows
    parts = []
    for rows, middle in zip(CHUNKS, middles):
        regrouped = lax.all_to_all(middle, "row", split_axis=0, concat_axis=0, tiled=True)
        inner = mid_level(rows, x, mid_ranks[0], regrouped, mid_factors[0])
        near = [inner[0]] + [around_x(inner[d], d) for d in range(1, N_X)]
        far = across_z(sum_other(rows, z, near))
        parts += near + [far]
    return row_level(CHUNKS, me.reshape(1), row_ranks, row_factors, parts)


def solution(mesh):
    in_specs = (
        P(("col", "row"), None, None),
        P(None, ("col", "row"), None, None),
        P(None, ("col", "row")),
        P(("col", "row"), None),
        P("col", "row", None, None),
        P("col", "row"),
        P("row", None, None),
        P("row"),
    )
    out_specs = P(("row", "col"), None, None)
    return jax.shard_map(shards, mesh=mesh, in_specs=in_specs, out_specs=out_specs, check_vma=False)
```

time: 225 us -> 123 us (0.55)
  waiting for transfers between devices: 174 us -> 44.4 us
  Pallas kernels: 0 us -> 43.9 us
  starting transfers between devices: 9.02 us -> 29.9 us
  between operations: 13.5 us -> 0.08 us
  matrix products: 12.1 us -> 0 us
  other arithmetic: 6.65 us -> 0 us
  local copies, waits for them, and re-layouts: 8.25 us -> 3.19 us
    reduce_scatter x1 -> x0, waiting for transfers between devices: 127 us -> none  [shards(): lax.psum_scatter(partial_value, 'col', scatter_dimension=0, tiled=True)]
    pallas_call x0 -> x7, Pallas kernels: none -> 43.9 us  [the longest x2 22.3 us: col_levels(): pl.pallas_call(functools.partial(col_kernel, start, rows), out_shape=jax....]
    all_to_all x1 -> x2, waiting for transfers between devices: 46.4 us -> 29.5 us  [shards(): lax.all_to_all(middle, 'row', split_axis=0, concat_axis=0, tiled=True)]
    ppermute x0 -> x8, waiting for transfers between devices: none -> 14.8 us  [the longest x2 7.94 us: across_z(): lax.ppermute(value, 'col', [(i, (i + half) % (2 * half)) for i in range(2...]
    ppermute x0 -> x8, starting transfers between devices: none -> 14.8 us  [the longest x2 8.98 us: across_z(): lax.ppermute(value, 'col', [(i, (i + half) % (2 * half)) for i in range(2...]
    dot_general x4 -> x0, matrix products: 12.1 us -> none  [level(): jnp.einsum('nrk,nkj->nrj', blocks, rank_mask(factors, ranks), preferred_e...]
    all_to_all x1 -> x2, starting transfers between devices: 8.98 us -> 15.1 us  [shards(): lax.all_to_all(middle, 'row', split_axis=0, concat_axis=0, tiled=True)]
    select_n x2 -> x0, other arithmetic: 3.97 us -> none  [shards(): jnp.take(middle, block_order[0], axis=0)]
  transfers between devices with their start and end apart: 2 -> 10, of which waited for: 2 -> 5; matrix products, arithmetic and copies ran while one was open for 0% -> 0% of each run, Pallas kernels for 0% -> 24%
where the time goes in v1:
time: 123 us; the launch traced here: 121 us
  waiting for transfers between devices  44.4 us (36%)
  Pallas kernels  43.9 us (36%)
  starting transfers between devices  29.9 us (24%)
  local copies, waits for them, and re-layouts  3.19 us (3%)
    all_to_all x2, waiting for transfers between devices, shards(): lax.all_to_all(middle, 'row', split_axis=0, concat_axis=0, tiled=True)  29.5 us
    pallas_call x2, Pallas kernels, col_levels(): pl.pallas_call(functools.partial(col_kernel, start, rows), out_shape=jax....  22.3 us
    all_to_all x2, starting transfers between devices, shards(): lax.all_to_all(middle, 'row', split_axis=0, concat_axis=0, tiled=True)  15.1 us
    pallas_call x2, Pallas kernels, mid_level(): pl.pallas_call(mid_kernel, out_shape=[jax.ShapeDtypeStruct(piece, jnp.bfl...  14.8 us
    ppermute x2, starting transfers between devices, across_z(): lax.ppermute(value, 'col', [(i, (i + half) % (2 * half)) for i in range(2...  8.98 us
    ppermute x2, waiting for transfers between devices, across_z(): lax.ppermute(value, 'col', [(i, (i + half) % (2 * half)) for i in range(2...  7.94 us
    ppermute x6, waiting for transfers between devices, around_x(): return lax.ppermute(value, 'col', pairs)  6.9 us
    ppermute x6, starting transfers between devices, around_x(): return lax.ppermute(value, 'col', pairs)  5.8 us
  transfers between devices with their start and end apart: 10, of which 5 were waited for; matrix products, arithmetic and copies ran while one was open for 0% of the time, Pallas kernels for 24%

profile of v1, /device:TPU:38, one launch (start us, length us, event | category | flops | bytes accessed | tf_op | source)
XLA Modules:
  0.0 121.4 jit_solution(13096143695866164413)
XLA Ops:
  0.0 11.1 %col_levels.3 = bf16[64,64,128]{2,1,0:T(8,128)(2,1)} custom-call(s32[64]{0:T(128)} %bitcast.8, s32[2,64]{1,0:T(2,128)} %rank_ref.4, bf16[64,128,128]{2,1,0:T(8,128)(2,1)} %z_ref.3, bf16[2,64,128,128]{3,2,1,0:T(8,128)(2,1)} %w_ref.4), custom_call_target="tpu_custom_call" | custom-call | flops 268435456 | bytes 8388608 | tf_op jit(solution)/shard_map/col_levels/pallas_call | solution.py:55
  11.1 8.8 %all-to-all-start.1 = ((bf16[64,64,128]{2,1,0:T(8,128)(2,1)}), bf16[64,64,128]{2,1,0:T(8,128)(2,1)S(1)}, u32[]{:S(2)}, u32[]{:S(2)}) async-start(bf16[64,64,128]{2,1,0:T(8,128)(2,1)} %col_levels.3), calls=%async_computation.1 | async-start | bytes 2097152 | tf_op jit(solution)/shard_map/all_to_all | solution.py:204
  19.9 11.2 %col_levels.2 = bf16[64,64,128]{2,1,0:T(8,128)(2,1)} custom-call(s32[64]{0:T(128)} %bitcast.9, s32[2,64]{1,0:T(2,128)} %rank_ref.4, bf16[64,128,128]{2,1,0:T(8,128)(2,1)} %z_ref.3, bf16[2,64,128,128]{3,2,1,0:T(8,128)(2,1)} %w_ref.4), custom_call_target="tpu_custom_call" | custom-call | flops 268435456 | bytes 8388608 | tf_op jit(solution)/shard_map/col_levels/pallas_call | solution.py:55
  31.1 14.4 %all-to-all-done.1.z_ref = bf16[64,64,128]{2,1,0:T(8,128)(2,1)S(1)} async-done(((bf16[64,64,128]{2,1,0:T(8,128)(2,1)}), bf16[64,64,128]{2,1,0:T(8,128)(2,1)S(1)}, u32[]{:S(2)}, u32[]{:S(2)}) %all-to-all-start.1) | async-done | bytes 1048608 | tf_op jit(solution)/shard_map/all_to_all | solution.py:204
  45.5 6.3 %all-to-all-start = ((bf16[64,64,128]{2,1,0:T(8,128)(2,1)}), bf16[64,64,128]{2,1,0:T(8,128)(2,1)S(1)}, u32[]{:S(2)}, u32[]{:S(2)}) async-start(bf16[64,64,128]{2,1,0:T(8,128)(2,1)} %col_levels.2), calls=%async_computation | async-start | bytes 2097152 | tf_op jit(solution)/shard_map/all_to_all | solution.py:204
  51.8 7.4 %mid_level.3 = (bf16[16,64,128]{2,1,0:T(8,128)(2,1)}, bf16[16,64,128]{2,1,0:T(8,128)(2,1)}, bf16[16,64,128]{2,1,0:T(8,128)(2,1)}, bf16[16,64,128]{2,1,0:T(8,128)(2,1)}) custom-call(s32[1]{0:T(128)} %bitcast.1.x_ref, s32[64]{0:T(128)} %bitcast.10, bf16[64,64,128]{2,1,0:T(8,128)(2,1)} %copy-done.1, bf16[64,128,128]{2,1,0:T(8,128)(2,1)} %bitcast.6), custom_call_target="tpu_custom_call" | custom-call | flops 134217728 | bytes 6291456 | tf_op jit(solution)/shard_map/mid_level/pallas_call | solution.py:96
  59.2 0.5 collective-permute-start.4
  59.7 2.4 %collective-permute-start.5 = (bf16[16,64,128]{2,1,0:T(8,128)(2,1)}, bf16[16,64,128]{2,1,0:T(8,128)(2,1)S(1)}, u32[]{:S(2)}, u32[]{:S(2)}) collective-permute-start(bf16[16,64,128]{2,1,0:T(8,128)(2,1)} %get-tuple-element.19), channel_id=1, source_target_pairs={{0,2},{1,3},{2,0},{3,1},{4,6},{5,7},{6,4},{7,5},{8,10},{9,11},{10,... | collective-permute-start | bytes 786440 | tf_op jit(solution)/shard_map/ppermute | solution.py:181
  62.1 15.2 %all-to-all-done.z_ref = bf16[64,64,128]{2,1,0:T(8,128)(2,1)S(1)} async-done(((bf16[64,64,128]{2,1,0:T(8,128)(2,1)}), bf16[64,64,128]{2,1,0:T(8,128)(2,1)S(1)}, u32[]{:S(2)}, u32[]{:S(2)}) %all-to-all-start) | async-done | bytes 1048608 | tf_op jit(solution)/shard_map/all_to_all | solution.py:204
  77.3 1.0 copy-done
  78.3 7.4 %mid_level.2 = (bf16[16,64,128]{2,1,0:T(8,128)(2,1)}, bf16[16,64,128]{2,1,0:T(8,128)(2,1)}, bf16[16,64,128]{2,1,0:T(8,128)(2,1)}, bf16[16,64,128]{2,1,0:T(8,128)(2,1)}) custom-call(s32[1]{0:T(128)} %bitcast.1.x_ref, s32[64]{0:T(128)} %bitcast.11, bf16[64,64,128]{2,1,0:T(8,128)(2,1)} %copy-done, bf16[64,128,128]{2,1,0:T(8,128)(2,1)} %bitcast.7), custom_call_target="tpu_custom_call" | custom-call | flops 134217728 | bytes 6291456 | tf_op jit(solution)/shard_map/mid_level/pallas_call | solution.py:96
  85.7 0.5 collective-permute-start
  86.2 2.4 %collective-permute-start.1 = (bf16[16,64,128]{2,1,0:T(8,128)(2,1)}, bf16[16,64,128]{2,1,0:T(8,128)(2,1)S(1)}, u32[]{:S(2)}, u32[]{:S(2)}) collective-permute-start(bf16[16,64,128]{2,1,0:T(8,128)(2,1)} %get-tuple-element.15), channel_id=1, source_target_pairs={{0,2},{1,3},{2,0},{3,1},{4,6},{5,7},{6,4},{7,5},{8,10},{9,11},{10,... | collective-permute-start | bytes 786440 | tf_op jit(solution)/shard_map/ppermute | solution.py:181
  88.6 0.6 copy-done.2
  89.5 1.8 %sum_other.3 = bf16[8,64,128]{2,1,0:T(8,128)(2,1)} custom-call(s32[1]{0:T(128)} %bitcast.5.z_ref, bf16[16,64,128]{2,1,0:T(8,128)(2,1)} %get-tuple-element.17.refs_0_.refs_5_, bf16[16,64,128]{2,1,0:T(8,128)(2,1)} %copy-done.2, bf16[16,64,128]{2,1,0:T(8,128)(2,1)} %copy-done.3, bf16[16,64,128]{2,1,0:T(8,128)(2,1)} %copy-done.4), custom_call_target="tpu_custom_call" | custom-call | flops 262144 | bytes 655360 | tf_op jit(solution)/shard_map/sum_other/pallas_call | solution.py:127
  91.3 4.5 %collective-permute-start.7 = (bf16[8,64,128]{2,1,0:T(8,128)(2,1)}, bf16[8,64,128]{2,1,0:T(8,128)(2,1)S(1)}, u32[]{:S(2)}, u32[]{:S(2)}) collective-permute-start(bf16[8,64,128]{2,1,0:T(8,128)(2,1)} %sum_other.3), channel_id=1, source_target_pairs={{0,4},{1,5},{2,6},{3,7},{4,0},{5,1},{6,2},{7,3},{8,12},{9,13},{10,... | collective-permute-start | bytes 393224 | tf_op jit(solution)/shard_map/ppermute | solution.py:186
  95.8 1.2 %collective-permute-done.1.refs_2_ = bf16[16,64,128]{2,1,0:T(8,128)(2,1)S(1)} collective-permute-done((bf16[16,64,128]{2,1,0:T(8,128)(2,1)}, bf16[16,64,128]{2,1,0:T(8,128)(2,1)S(1)}, u32[]{:S(2)}, u32[]{:S(2)}) %collective-permute-start.1) | collective-permute-done | bytes 262176 | tf_op jit(solution)/shard_map/ppermute | solution.py:181
  97.0 5.7 %collective-permute-done.2.refs_3_ = bf16[16,64,128]{2,1,0:T(8,128)(2,1)S(1)} collective-permute-done((bf16[16,64,128]{2,1,0:T(8,128)(2,1)}, bf16[16,64,128]{2,1,0:T(8,128)(2,1)S(1)}, u32[]{:S(2)}, u32[]{:S(2)}) %collective-permute-start.2) | collective-permute-done | bytes 262176 | tf_op jit(solution)/shard_map/ppermute | solution.py:181
  102.7 0.7 copy-done.7
  103.4 1.8 %sum_other.2 = bf16[8,64,128]{2,1,0:T(8,128)(2,1)} custom-call(s32[1]{0:T(128)} %bitcast.5.z_ref, bf16[16,64,128]{2,1,0:T(8,128)(2,1)} %get-tuple-element.13.refs_0_, bf16[16,64,128]{2,1,0:T(8,128)(2,1)} %copy-done.5, bf16[16,64,128]{2,1,0:T(8,128)(2,1)} %copy-done.6, bf16[16,64,128]{2,1,0:T(8,128)(2,1)} %copy-done.7), custom_call_target="tpu_custom_call" | custom-call | flops 262144 | bytes 655360 | tf_op jit(solution)/shard_map/sum_other/pallas_call | solution.py:127
  105.2 4.5 %collective-permute-start.3 = (bf16[8,64,128]{2,1,0:T(8,128)(2,1)}, bf16[8,64,128]{2,1,0:T(8,128)(2,1)S(1)}, u32[]{:S(2)}, u32[]{:S(2)}) collective-permute-start(bf16[8,64,128]{2,1,0:T(8,128)(2,1)} %sum_other.2), channel_id=1, source_target_pairs={{0,4},{1,5},{2,6},{3,7},{4,0},{5,1},{6,2},{7,3},{8,12},{9,13},{10,... | collective-permute-start | bytes 393224 | tf_op jit(solution)/shard_map/ppermute | solution.py:186
  109.7 7.9 %collective-permute-done.3.refs_4_ = bf16[8,64,128]{2,1,0:T(8,128)(2,1)S(1)} collective-permute-done((bf16[8,64,128]{2,1,0:T(8,128)(2,1)}, bf16[8,64,128]{2,1,0:T(8,128)(2,1)S(1)}, u32[]{:S(2)}, u32[]{:S(2)}) %collective-permute-start.3) | collective-permute-done | bytes 131104 | tf_op jit(solution)/shard_map/ppermute | solution.py:186
  117.6 0.6 copy-done.9
  118.3 3.1 %row_level.1 = bf16[8,128,128]{2,1,0:T(8,128)(2,1)} custom-call(s32[1]{0:T(128)} %bitcast.me_ref, s32[64]{0:T(128)} %rank_ref.5, bf16[64,128,128]{2,1,0:T(8,128)(2,1)} %w_ref.5, bf16[16,64,128]{2,1,0:T(8,128)(2,1)} %get-tuple-element.13.refs_0_, bf16[16,64,128]{2,1,0:T(8,128)(2,1)} %copy-done.5, bf16[16,64,128]{2,1,0:T(8,128)(2,1)} %copy-done.6, ...), custom_call_target="tpu_custom_call" | custom-call | flops 33554432 | bytes 1048576 | tf_op jit(solution)/shard_map/row_level/pallas_call | solution.py:163
  (23 shorter events, 0.2 us)
Async XLA Ops:
  11.1 34.3 %all-to-all-start.1 = ((bf16[64,64,128]{2,1,0:T(8,128)(2,1)}), bf16[64,64,128]{2,1,0:T(8,128)(2,1)S(1)}, u32[]{:S(2)}, u32[]{:S(2)}) async-start(bf16[64,64,128]{2,1,0:T(8,128)(2,1)} %col_levels.3), calls=%async_computation.1 | async-start | bytes 2097152 | tf_op jit(solution)/shard_map/all_to_all | solution.py:204
  45.5 6.3 %copy-start.1 = (bf16[64,64,128]{2,1,0:T(8,128)(2,1)}, bf16[64,64,128]{2,1,0:T(8,128)(2,1)S(1)}, u32[]{:S(2)}) copy-start(bf16[64,64,128]{2,1,0:T(8,128)(2,1)S(1)} %all-to-all-done.1.z_ref) | copy-start | bytes 3145732
  45.5 31.8 %all-to-all-start = ((bf16[64,64,128]{2,1,0:T(8,128)(2,1)}), bf16[64,64,128]{2,1,0:T(8,128)(2,1)S(1)}, u32[]{:S(2)}, u32[]{:S(2)}) async-start(bf16[64,64,128]{2,1,0:T(8,128)(2,1)} %col_levels.2), calls=%async_computation | async-start | bytes 2097152 | tf_op jit(solution)/shard_map/all_to_all | solution.py:204
  59.2 29.4 %collective-permute-start.4 = (bf16[16,64,128]{2,1,0:T(8,128)(2,1)}, bf16[16,64,128]{2,1,0:T(8,128)(2,1)S(1)}, u32[]{:S(2)}, u32[]{:S(2)}) collective-permute-start(bf16[16,64,128]{2,1,0:T(8,128)(2,1)} %get-tuple-element.18), channel_id=1, source_target_pairs={{0,1},{1,2},{2,3},{3,0},{4,5},{5,6},{6,7},{7,4},{8,9},{9,10},{10,1... | collective-permute-start | bytes 786440 | tf_op jit(solution)/shard_map/ppermute | solution.py:181
  59.7 28.9 %collective-permute-start.5 = (bf16[16,64,128]{2,1,0:T(8,128)(2,1)}, bf16[16,64,128]{2,1,0:T(8,128)(2,1)S(1)}, u32[]{:S(2)}, u32[]{:S(2)}) collective-permute-start(bf16[16,64,128]{2,1,0:T(8,128)(2,1)} %get-tuple-element.19), channel_id=1, source_target_pairs={{0,2},{1,3},{2,0},{3,1},{4,6},{5,7},{6,4},{7,5},{8,10},{9,11},{10,... | collective-permute-start | bytes 786440 | tf_op jit(solution)/shard_map/ppermute | solution.py:181
  62.1 26.5 %collective-permute-start.6 = (bf16[16,64,128]{2,1,0:T(8,128)(2,1)}, bf16[16,64,128]{2,1,0:T(8,128)(2,1)S(1)}, u32[]{:S(2)}, u32[]{:S(2)}) collective-permute-start(bf16[16,64,128]{2,1,0:T(8,128)(2,1)} %get-tuple-element.20), channel_id=1, source_target_pairs={{0,3},{1,0},{2,1},{3,2},{4,7},{5,4},{6,5},{7,6},{8,11},{9,8},{10,9... | collective-permute-start | bytes 786440 | tf_op jit(solution)/shard_map/ppermute | solution.py:181
  77.3 1.0 copy-start
  85.7 10.1 %collective-permute-start = (bf16[16,64,128]{2,1,0:T(8,128)(2,1)}, bf16[16,64,128]{2,1,0:T(8,128)(2,1)S(1)}, u32[]{:S(2)}, u32[]{:S(2)}) collective-permute-start(bf16[16,64,128]{2,1,0:T(8,128)(2,1)} %get-tuple-element.14), channel_id=1, source_target_pairs={{0,1},{1,2},{2,3},{3,0},{4,5},{5,6},{6,7},{7,4},{8,9},{9,10},{10,1... | collective-permute-start | bytes 786440 | tf_op jit(solution)/shard_map/ppermute | solution.py:181
  86.2 10.9 %collective-permute-start.1 = (bf16[16,64,128]{2,1,0:T(8,128)(2,1)}, bf16[16,64,128]{2,1,0:T(8,128)(2,1)S(1)}, u32[]{:S(2)}, u32[]{:S(2)}) collective-permute-start(bf16[16,64,128]{2,1,0:T(8,128)(2,1)} %get-tuple-element.15), channel_id=1, source_target_pairs={{0,2},{1,3},{2,0},{3,1},{4,6},{5,7},{6,4},{7,5},{8,10},{9,11},{10,... | collective-permute-start | bytes 786440 | tf_op jit(solution)/shard_map/ppermute | solution.py:181
  88.6 0.7 copy-start.2
  88.6 14.1 %collective-permute-start.2 = (bf16[16,64,128]{2,1,0:T(8,128)(2,1)}, bf16[16,64,128]{2,1,0:T(8,128)(2,1)S(1)}, u32[]{:S(2)}, u32[]{:S(2)}) collective-permute-start(bf16[16,64,128]{2,1,0:T(8,128)(2,1)} %get-tuple-element.16), channel_id=1, source_target_pairs={{0,3},{1,0},{2,1},{3,2},{4,7},{5,4},{6,5},{7,6},{8,11},{9,8},{10,9... | collective-permute-start | bytes 786440 | tf_op jit(solution)/shard_map/ppermute | solution.py:181
  88.6 0.8 copy-start.3
  88.6 0.8 copy-start.4
  91.3 18.4 %collective-permute-start.7 = (bf16[8,64,128]{2,1,0:T(8,128)(2,1)}, bf16[8,64,128]{2,1,0:T(8,128)(2,1)S(1)}, u32[]{:S(2)}, u32[]{:S(2)}) collective-permute-start(bf16[8,64,128]{2,1,0:T(8,128)(2,1)} %sum_other.3), channel_id=1, source_target_pairs={{0,4},{1,5},{2,6},{3,7},{4,0},{5,1},{6,2},{7,3},{8,12},{9,13},{10,... | collective-permute-start | bytes 393224 | tf_op jit(solution)/shard_map/ppermute | solution.py:186
  95.8 6.9 %copy-start.5 = (bf16[16,64,128]{2,1,0:T(8,128)(2,1)}, bf16[16,64,128]{2,1,0:T(8,128)(2,1)S(1)}, u32[]{:S(2)}) copy-start(bf16[16,64,128]{2,1,0:T(8,128)(2,1)S(1)} %collective-permute-done.refs_1_) | copy-start | bytes 786436
  97.0 5.7 %copy-start.6 = (bf16[16,64,128]{2,1,0:T(8,128)(2,1)}, bf16[16,64,128]{2,1,0:T(8,128)(2,1)S(1)}, u32[]{:S(2)}) copy-start(bf16[16,64,128]{2,1,0:T(8,128)(2,1)S(1)} %collective-permute-done.1.refs_2_) | copy-start | bytes 786436
  102.7 0.7 copy-start.7
  105.2 12.4 %collective-permute-start.3 = (bf16[8,64,128]{2,1,0:T(8,128)(2,1)}, bf16[8,64,128]{2,1,0:T(8,128)(2,1)S(1)}, u32[]{:S(2)}, u32[]{:S(2)}) collective-permute-start(bf16[8,64,128]{2,1,0:T(8,128)(2,1)} %sum_other.2), channel_id=1, source_target_pairs={{0,4},{1,5},{2,6},{3,7},{4,0},{5,1},{6,2},{7,3},{8,12},{9,13},{10,... | collective-permute-start | bytes 393224 | tf_op jit(solution)/shard_map/ppermute | solution.py:186
  109.7 7.9 %copy-start.8 = (bf16[8,64,128]{2,1,0:T(8,128)(2,1)}, bf16[8,64,128]{2,1,0:T(8,128)(2,1)S(1)}, u32[]{:S(2)}) copy-start(bf16[8,64,128]{2,1,0:T(8,128)(2,1)S(1)} %collective-permute-done.7.refs_9_) | copy-start | bytes 393220
  117.6 0.7 copy-start.9

commit v2 on v0

v2 whole, which is shorter than its diff:
```python
import functools

import jax
import jax.numpy as jnp
from jax import lax
from jax.experimental import pallas as pl
from jax.experimental.pallas import tpu as pltpu
from jax.sharding import PartitionSpec as P

BW = 128
HALF = BW // 2
R = 128
PB = 64
STEP = 8
N_X = 4
N_Z = 2
OWN = 8
CHUNKS = (64, 64)
BF16 = jnp.bfloat16
ANY = pl.BlockSpec(memory_space=pl.ANY)
SMEM = pl.BlockSpec(memory_space=pltpu.SMEM)
VMEM = pl.BlockSpec(memory_space=pltpu.VMEM)
SMALL = pltpu.CompilerParams(vmem_limit_bytes=12 * 2**20)


def masked_dot(blocks, factors, rank):
    product = jnp.dot(blocks, factors, preferred_element_type=jnp.float32)
    lane = lax.broadcasted_iota(jnp.int32, product.shape, 1)
    return jnp.where(lane < rank, product, 0.0)


def pair(even, odd):
    lane = lax.broadcasted_iota(jnp.int32, even.shape, 1)
    front = jnp.where(lane < HALF, even, pltpu.roll(odd, HALF, 1))
    back = jnp.where(lane < HALF, pltpu.roll(even, HALF, 1), odd)
    return front.astype(BF16), back.astype(BF16)


def col_kernel(order_ref, rank_ref, z_ref, w_ref, *refs):
    n = len(CHUNKS)
    out_refs, (z_buf, w_buf, place_ref, sems) = refs[:n], refs[n:]
    copies = []
    for g in range(PB // STEP):
        part = pl.ds(g * STEP, STEP)
        copies.append(
            [
                pltpu.make_async_copy(z_ref.at[part], z_buf.at[part], sems.at[0, g]),
                pltpu.make_async_copy(w_ref.at[0, part], w_buf.at[0, part], sems.at[1, g]),
                pltpu.make_async_copy(w_ref.at[1, part], w_buf.at[1, part], sems.at[2, g]),
            ]
        )
        for copy in copies[-1]:
            copy.start()
    for k in range(PB):
        place_ref[order_ref[k]] = k
    for g in range(PB // STEP):
        for copy in copies[g]:
            copy.wait()
        blocks = range(g * STEP, (g + 1) * STEP)
        first = [masked_dot(z_buf[b], w_buf[0, b], rank_ref[0, b]) for b in blocks]
        paired = []
        for j in range(0, STEP, 2):
            paired.extend(pair(first[j], first[j + 1]))
        for b, block in zip(blocks, paired):
            middle = masked_dot(block, w_buf[1, b], rank_ref[1, b]).astype(BF16)
            start = 0
            for rows, out_ref in zip(CHUNKS, out_refs):
                out_ref[place_ref[b]] = middle[start : start + rows]
                start += rows


def col_levels(order, ranks, right_sides, factors):
    return pl.pallas_call(
        col_kernel,
        out_shape=[jax.ShapeDtypeStruct((PB, rows, BW), BF16) for rows in CHUNKS],
        in_specs=[SMEM, SMEM, ANY, ANY],
        out_specs=[VMEM] * len(CHUNKS),
        scratch_shapes=[
            pltpu.VMEM((PB, R, BW), BF16),
            pltpu.VMEM((2, PB, BW, BW), BF16),
            pltpu.SMEM((PB,), jnp.int32),
            pltpu.SemaphoreType.DMA((3, PB // STEP)),
        ],
        cost_estimate=pl.CostEstimate(
            flops=4 * PB * R * BW * BW, bytes_accessed=8 * 2**20, transcendentals=0
        ),
        name="col_levels",
    )(order, ranks, right_sides, factors)


def mid_kernel(offsets, x_ref, rank_ref, z_ref, w_ref, *out_refs):
    for d, out_ref in zip(offsets, out_refs):
        for h in range(N_Z):
            base = (h * N_X + lax.rem(x_ref[0] + d, N_X)) * STEP
            for j in range(STEP):
                inner = masked_dot(z_ref[base + j], w_ref[base + j], rank_ref[base + j])
                out_ref[h * STEP + j] = inner.astype(BF16)


def mid_level(rows, offsets, x, ranks, blocks, factors):
    n = len(offsets)
    count = n * N_Z * STEP
    return pl.pallas_call(
        functools.partial(mid_kernel, offsets),
        out_shape=[jax.ShapeDtypeStruct((N_Z * STEP, rows, BW), BF16)] * n,
        in_specs=[SMEM, SMEM, VMEM, VMEM],
        out_specs=[VMEM] * n,
        compiler_params=SMALL,
        cost_estimate=pl.CostEstimate(
            flops=2 * count * rows * BW * BW,
            bytes_accessed=count * (4 * rows + 2 * BW) * BW,
            transcendentals=0,
        ),
        name="mid_level",
    )(x, ranks, blocks, factors)


def total_of(refs, half):
    total = refs[0][half].astype(jnp.float32)
    for ref in refs[1:]:
        total = total + ref[half].astype(jnp.float32)
    return total


def sum_kernel(z_ref, *refs):
    half = pl.ds((1 - z_ref[0]) * STEP, STEP)
    refs[N_X][...] = total_of(refs[:N_X], half).astype(BF16)


def sum_other(rows, z, parts):
    return pl.pallas_call(
        sum_kernel,
        out_shape=jax.ShapeDtypeStruct((STEP, rows, BW), BF16),
        in_specs=[SMEM] + [VMEM] * N_X,
        out_specs=VMEM,
        compiler_params=SMALL,
        cost_estimate=pl.CostEstimate(
            flops=4 * STEP * rows * BW, bytes_accessed=10 * STEP * rows * BW, transcendentals=0
        ),
        name="sum_other",
    )(z, *parts)


def row_kernel(me_ref, rank_ref, w_ref, *refs):
    out_ref = refs[-1]
    base = me_ref[0] * OWN
    half = pl.ds(lax.div(me_ref[0], N_X) * STEP, STEP)
    start = 0
    for n, rows in enumerate(CHUNKS):
        near = refs[n * (N_X + 1) : n * (N_X + 1) + N_X]
        far = refs[n * (N_X + 1) + N_X]
        total = total_of(near, half) + far[...].astype(jnp.float32)
        for j in range(0, OWN, 2):
            for i, block in enumerate(pair(total[j], total[j + 1])):
                product = masked_dot(block, w_ref[base + j + i], rank_ref[base + j + i])
                out_ref[j + i, start : start + rows] = product.astype(BF16)
        start += rows


def row_level(me, ranks, factors, parts):
    return pl.pallas_call(
        row_kernel,
        out_shape=jax.ShapeDtypeStruct((OWN, R, BW), BF16),
        in_specs=[SMEM, SMEM, VMEM] + [VMEM] * len(parts),
        out_specs=VMEM,
        compiler_params=SMALL,
        cost_estimate=pl.CostEstimate(
            flops=2 * OWN * R * BW * BW, bytes_accessed=2**20, transcendentals=0
        ),
        name="row_level",
    )(me, ranks, factors, *parts)


def around_x(value, d):
    pairs = [(z * N_X + x, z * N_X + (x + d) % N_X) for z in range(N_Z) for x in range(N_X)]
    return lax.ppermute(value, "col", pairs)


def across_z(value):
    half = N_X * N_Z // 2
    return lax.ppermute(value, "col", [(i, (i + half) % (2 * half)) for i in range(2 * half)])


def shards(
    right_sides, col_factors, col_ranks, block_order, mid_factors, mid_ranks, row_factors, row_ranks
):
    me = lax.axis_index("col").astype(jnp.int32)
    x = lax.rem(me, N_X).reshape(1)
    z = lax.div(me, N_X).reshape(1)
    middles = col_levels(block_order[0], col_ranks, right_sides, col_factors)
    parts = []
    before = None
    for rows, middle in zip(CHUNKS, middles):
        regrouped = lax.all_to_all(middle, "row", split_axis=0, concat_axis=0, tiled=True)
        if before is not None:
            regrouped, before = lax.optimization_barrier((regrouped, before))
            parts.append(across_z(before))
        sent = mid_level(rows, (2, 1, 3), x, mid_ranks[0], regrouped, mid_factors[0])
        kept = mid_level(rows, (0,), x, mid_ranks[0], regrouped, mid_factors[0])
        near = list(kept) + [around_x(piece, d) for piece, d in zip(sent, (2, 1, 3))]
        before = sum_other(rows, z, near)
        parts += near
    parts.append(across_z(before))
    return row_level(me.reshape(1), row_ranks, row_factors, parts)


def solution(mesh):
    in_specs = (
        P(("col", "row"), None, None),
        P(None, ("col", "row"), None, None),
        P(None, ("col", "row")),
        P(("col", "row"), None),
        P("col", "row", None, None),
        P("col", "row"),
        P("row", None, None),
        P("row"),
    )
    out_specs = P(("row", "col"), None, None)
    return jax.shard_map(shards, mesh=mesh, in_specs=in_specs, out_specs=out_specs, check_vma=False)
```

time: 225 us -> 106 us (0.47)
  waiting for transfers between devices: 174 us -> 30.9 us
  blocking collectives: 0 us -> 34.6 us
  Pallas kernels: 0 us -> 14.8 us
  starting transfers between devices: 9.02 us -> 22.5 us
  between operations: 13.5 us -> 0.09 us
  matrix products: 12.1 us -> 0 us
  other arithmetic: 6.65 us -> 0 us
  local copies, waits for them, and re-layouts: 8.25 us -> 2.46 us
    reduce_scatter x1 -> x0, waiting for transfers between devices: 127 us -> none  [shards(): lax.psum_scatter(partial_value, 'col', scatter_dimension=0, tiled=True)]
    all_to_all x1, waiting for transfers between devices: 46.4 us -> 5.49 us  [shards(): lax.all_to_all(middle, 'row', split_axis=0, concat_axis=0, tiled=True)]
    all_to_all x0 -> x1, blocking collectives: none -> 34.6 us  [shards(): lax.all_to_all(middle, 'row', split_axis=0, concat_axis=0, tiled=True)]
    ppermute x0 -> x8, waiting for transfers between devices: none -> 25.4 us  [the longest x6 17.7 us: around_x(): return lax.ppermute(value, 'col', pairs)]
    ppermute x0 -> x8, starting transfers between devices: none -> 16.3 us  [the longest x2 9.1 us: across_z(): lax.ppermute(value, 'col', [(i, (i + half) % (2 * half)) for i in range(2...]
    pallas_call x0 -> x8, Pallas kernels: none -> 14.8 us  [the longest x1 6.84 us: col_levels(): pl.pallas_call(col_kernel, out_shape=[jax.ShapeDtypeStruct((PB, rows, BW)...]
    dot_general x4 -> x0, matrix products: 12.1 us -> none  [level(): jnp.einsum('nrk,nkj->nrj', blocks, rank_mask(factors, ranks), preferred_e...]
    select_n x2 -> x0, other arithmetic: 3.97 us -> none  [shards(): jnp.take(middle, block_order[0], axis=0)]
  transfers between devices with their start and end apart: 2 -> 9, of which waited for: 2 -> 8; matrix products, arithmetic and copies ran while one was open for 0% -> 0% of each run, Pallas kernels for 0% -> 4%
where the time goes in v2:
time: 106 us; the launch traced here: 105 us
  blocking collectives  34.6 us (33%)
  waiting for transfers between devices  30.9 us (29%)
  starting transfers between devices  22.5 us (21%)
  Pallas kernels  14.8 us (14%)
  local copies, waits for them, and re-layouts  2.46 us (2%)
    all_to_all x1, blocking collectives, shards(): lax.all_to_all(middle, 'row', split_axis=0, concat_axis=0, tiled=True)  34.6 us
    ppermute x6, waiting for transfers between devices, around_x(): return lax.ppermute(value, 'col', pairs)  17.7 us
    ppermute x2, starting transfers between devices, across_z(): lax.ppermute(value, 'col', [(i, (i + half) % (2 * half)) for i in range(2...  9.1 us
    ppermute x2, waiting for transfers between devices, across_z(): lax.ppermute(value, 'col', [(i, (i + half) % (2 * half)) for i in range(2...  7.69 us
    ppermute x6, starting transfers between devices, around_x(): return lax.ppermute(value, 'col', pairs)  7.15 us
    pallas_call x1, Pallas kernels, col_levels(): pl.pallas_call(col_kernel, out_shape=[jax.ShapeDtypeStruct((PB, rows, BW)...  6.84 us
    all_to_all x1, starting transfers between devices, shards(): lax.all_to_all(middle, 'row', split_axis=0, concat_axis=0, tiled=True)  6.28 us
    all_to_all x1, waiting for transfers between devices, shards(): lax.all_to_all(middle, 'row', split_axis=0, concat_axis=0, tiled=True)  5.49 us
  transfers between devices with their start and end apart: 9, of which 8 were waited for; matrix products, arithmetic and copies ran while one was open for 0% of the time, Pallas kernels for 4%

profile of v2, /device:TPU:38, one launch (start us, length us, event | category | flops | bytes accessed | tf_op | source)
XLA Modules:
  0.0 105.3 jit_solution(1003147485307508487)
XLA Ops:
  0.0 6.8 %col_levels.1 = (bf16[64,64,128]{2,1,0:T(8,128)(2,1)}, bf16[64,64,128]{2,1,0:T(8,128)(2,1)}) custom-call(s32[64]{0:T(128)} %bitcast.14, s32[2,64]{1,0:T(2,128)} %rank_ref.2, bf16[64,128,128]{2,1,0:T(8,128)(2,1)} %z_ref.1, bf16[2,64,128,128]{3,2,1,0:T(8,128)(2,1)} %w_ref.2), custom_call_target="tpu_custom_call" | custom-call | flops 536870912 | bytes 8388608 | tf_op jit(solution)/shard_map/col_levels/pallas_call | solution.py:73
  6.9 34.6 %all_to_all.10.z_ref = bf16[64,64,128]{2,1,0:T(8,128)(2,1)} all-to-all(bf16[64,64,128]{2,1,0:T(8,128)(2,1)} %get-tuple-element.15), channel_id=1, replica_groups=mesh['row'=32,'col'=8] {'row'}, dimensions={0} | all-to-all | bytes 2097152 | tf_op jit(solution)/shard_map/all_to_all | solution.py:194
  41.4 6.3 %all-to-all-start.1 = ((bf16[64,64,128]{2,1,0:T(8,128)(2,1)}), bf16[64,64,128]{2,1,0:T(8,128)(2,1)S(1)}, u32[]{:S(2)}, u32[]{:S(2)}) async-start(bf16[64,64,128]{2,1,0:T(8,128)(2,1)} %get-tuple-element.19), calls=%async_computation.1 | async-start | bytes 2097152 | tf_op jit(solution)/shard_map/all_to_all | solution.py:194
  47.8 1.2 %copy-done.1 = bf16[64,64,128]{2,1,0:T(8,128)(2,1)S(1)} copy-done((bf16[64,64,128]{2,1,0:T(8,128)(2,1)S(1)}, bf16[64,64,128]{2,1,0:T(8,128)(2,1)}, u32[]{:S(2)}) %copy-start.1) | copy-done | bytes 1048600
  49.0 1.8 %mid_level.5 = (bf16[16,64,128]{2,1,0:T(8,128)(2,1)}, bf16[16,64,128]{2,1,0:T(8,128)(2,1)}, bf16[16,64,128]{2,1,0:T(8,128)(2,1)}) custom-call(s32[1]{0:T(128)} %bitcast.1.x_ref, s32[64]{0:T(128)S(1)} %bitcast.10, bf16[64,64,128]{2,1,0:T(8,128)(2,1)S(1)} %copy-done.1, bf16[64,128,128]{2,1,0:T(8,128)(2,1)S(1)} %bitcast.6), custom_call_target="tpu_custom_call" | custom-call | flops 100663296 | bytes 3145728 | tf_op jit(solution)/shard_map/mid_level/pallas_call | solution.py:103
  50.8 1.4 %collective-permute-start = (bf16[16,64,128]{2,1,0:T(8,128)(2,1)}, bf16[16,64,128]{2,1,0:T(8,128)(2,1)}, u32[]{:S(2)}, u32[]{:S(2)}) collective-permute-start(bf16[16,64,128]{2,1,0:T(8,128)(2,1)} %get-tuple-element.16), channel_id=1, source_target_pairs={{0,2},{1,3},{2,0},{3,1},{4,6},{5,7},{6,4},{7,5},{8,10},{9,11},{10,... | collective-permute-start | bytes 786440 | tf_op jit(solution)/shard_map/ppermute | solution.py:176
  52.2 2.1 %collective-permute-start.1 = (bf16[16,64,128]{2,1,0:T(8,128)(2,1)}, bf16[16,64,128]{2,1,0:T(8,128)(2,1)}, u32[]{:S(2)}, u32[]{:S(2)}) collective-permute-start(bf16[16,64,128]{2,1,0:T(8,128)(2,1)} %get-tuple-element.17), channel_id=1, source_target_pairs={{0,1},{1,2},{2,3},{3,0},{4,5},{5,6},{6,7},{7,4},{8,9},{9,10},{10,1... | collective-permute-start | bytes 786440 | tf_op jit(solution)/shard_map/ppermute | solution.py:176
  54.3 1.2 %copy-done.2 = bf16[64,64,128]{2,1,0:T(8,128)(2,1)S(1)} copy-done((bf16[64,64,128]{2,1,0:T(8,128)(2,1)S(1)}, bf16[64,64,128]{2,1,0:T(8,128)(2,1)}, u32[]{:S(2)}) %copy-start.2) | copy-done | bytes 1048600
  56.4 5.4 %collective-permute-done.refs_1_ = bf16[16,64,128]{2,1,0:T(8,128)(2,1)} collective-permute-done((bf16[16,64,128]{2,1,0:T(8,128)(2,1)}, bf16[16,64,128]{2,1,0:T(8,128)(2,1)}, u32[]{:S(2)}, u32[]{:S(2)}) %collective-permute-start) | collective-permute-done | bytes 262176 | tf_op jit(solution)/shard_map/ppermute | solution.py:176
  61.8 2.7 %collective-permute-done.1.refs_2_ = bf16[16,64,128]{2,1,0:T(8,128)(2,1)} collective-permute-done((bf16[16,64,128]{2,1,0:T(8,128)(2,1)}, bf16[16,64,128]{2,1,0:T(8,128)(2,1)}, u32[]{:S(2)}, u32[]{:S(2)}) %collective-permute-start.1) | collective-permute-done | bytes 262176 | tf_op jit(solution)/shard_map/ppermute | solution.py:176
  64.5 2.1 %collective-permute-done.2.refs_3_ = bf16[16,64,128]{2,1,0:T(8,128)(2,1)} collective-permute-done((bf16[16,64,128]{2,1,0:T(8,128)(2,1)}, bf16[16,64,128]{2,1,0:T(8,128)(2,1)}, u32[]{:S(2)}, u32[]{:S(2)}) %collective-permute-start.2) | collective-permute-done | bytes 262176 | tf_op jit(solution)/shard_map/ppermute | solution.py:176
  66.6 1.2 %sum_other.2 = bf16[8,64,128]{2,1,0:T(8,128)(2,1)S(1)} custom-call(s32[1]{0:T(128)} %bitcast.5.z_ref, bf16[16,64,128]{2,1,0:T(8,128)(2,1)S(1)} %mid_level.4.refs_0_, bf16[16,64,128]{2,1,0:T(8,128)(2,1)} %collective-permute-done.refs_1_, bf16[16,64,128]{2,1,0:T(8,128)(2,1)} %collective-permute-done.1.refs_2_, bf16[16,64,128]{2,1,0:T(8,128)(2,1)} %collective-permute-done.2.refs_3_), custom_call_target="tpu_custom_call" | custom-call | flops 262144 | bytes 655360 | tf_op jit(solution)/shard_map/sum_other/pallas_call | solution.py:131
  67.8 5.5 %all-to-all-done.1.z_ref = bf16[64,64,128]{2,1,0:T(8,128)(2,1)S(1)} async-done(((bf16[64,64,128]{2,1,0:T(8,128)(2,1)}), bf16[64,64,128]{2,1,0:T(8,128)(2,1)S(1)}, u32[]{:S(2)}, u32[]{:S(2)}) %all-to-all-start.1) | async-done | bytes 1048608 | tf_op jit(solution)/shard_map/all_to_all | solution.py:194
  73.2 1.1 %mid_level.7 = (bf16[16,64,128]{2,1,0:T(8,128)(2,1)S(1)}, bf16[16,64,128]{2,1,0:T(8,128)(2,1)S(1)}, bf16[16,64,128]{2,1,0:T(8,128)(2,1)S(1)}) custom-call(s32[1]{0:T(128)} %bitcast.1.x_ref, s32[64]{0:T(128)S(1)} %bitcast.12, bf16[64,64,128]{2,1,0:T(8,128)(2,1)S(1)} %all-to-all-done.1.z_ref, bf16[64,128,128]{2,1,0:T(8,128)(2,1)S(1)} %bitcast.8), custom_call_target="tpu_custom_call" | custom-call | flops 100663296 | bytes 3145728 | tf_op jit(solution)/shard_map/mid_level/pallas_call | solution.py:103
  74.3 1.5 %collective-permute-start.4 = (bf16[16,64,128]{2,1,0:T(8,128)(2,1)S(1)}, bf16[16,64,128]{2,1,0:T(8,128)(2,1)S(1)}, u32[]{:S(2)}, u32[]{:S(2)}) collective-permute-start(bf16[16,64,128]{2,1,0:T(8,128)(2,1)S(1)} %get-tuple-element.22), channel_id=1, source_target_pairs={{0,2},{1,3},{2,0},{3,1},{4,6},{5,7},{6,4},{7,5},{8,10},{9,11},{10,... | collective-permute-start | bytes 786440 | tf_op jit(solution)/shard_map/ppermute | solution.py:176
  75.8 2.1 %collective-permute-start.5 = (bf16[16,64,128]{2,1,0:T(8,128)(2,1)S(1)}, bf16[16,64,128]{2,1,0:T(8,128)(2,1)S(1)}, u32[]{:S(2)}, u32[]{:S(2)}) collective-permute-start(bf16[16,64,128]{2,1,0:T(8,128)(2,1)S(1)} %get-tuple-element.23), channel_id=1, source_target_pairs={{0,1},{1,2},{2,3},{3,0},{4,5},{5,6},{6,7},{7,4},{8,9},{9,10},{10,1... | collective-permute-start | bytes 786440 | tf_op jit(solution)/shard_map/ppermute | solution.py:176
  78.0 4.5 %collective-permute-start.3 = (bf16[8,64,128]{2,1,0:T(8,128)(2,1)S(1)}, bf16[8,64,128]{2,1,0:T(8,128)(2,1)S(1)}, u32[]{:S(2)}, u32[]{:S(2)}) collective-permute-start(bf16[8,64,128]{2,1,0:T(8,128)(2,1)S(1)} %sum_other.2), channel_id=1, source_target_pairs={{0,4},{1,5},{2,6},{3,7},{4,0},{5,1},{6,2},{7,3},{8,12},{9,13},{10,... | collective-permute-start | bytes 393224 | tf_op jit(solution)/shard_map/ppermute | solution.py:181
  82.4 0.8 mid_level.6.refs_0_.refs_5_
  83.3 1.6 %collective-permute-done.4.refs_1_.refs_6_ = bf16[16,64,128]{2,1,0:T(8,128)(2,1)S(1)} collective-permute-done((bf16[16,64,128]{2,1,0:T(8,128)(2,1)S(1)}, bf16[16,64,128]{2,1,0:T(8,128)(2,1)S(1)}, u32[]{:S(2)}, u32[]{:S(2)}) %collective-permute-start.4) | collective-permute-done | bytes 262176 | tf_op jit(solution)/shard_map/ppermute | solution.py:176
  84.9 3.4 %collective-permute-done.5.refs_2_.refs_7_ = bf16[16,64,128]{2,1,0:T(8,128)(2,1)S(1)} collective-permute-done((bf16[16,64,128]{2,1,0:T(8,128)(2,1)S(1)}, bf16[16,64,128]{2,1,0:T(8,128)(2,1)S(1)}, u32[]{:S(2)}, u32[]{:S(2)}) %collective-permute-start.5) | collective-permute-done | bytes 262176 | tf_op jit(solution)/shard_map/ppermute | solution.py:176
  88.3 2.4 %collective-permute-done.6.refs_3_.refs_8_ = bf16[16,64,128]{2,1,0:T(8,128)(2,1)S(1)} collective-permute-done((bf16[16,64,128]{2,1,0:T(8,128)(2,1)S(1)}, bf16[16,64,128]{2,1,0:T(8,128)(2,1)S(1)}, u32[]{:S(2)}, u32[]{:S(2)}) %collective-permute-start.6) | collective-permute-done | bytes 262176 | tf_op jit(solution)/shard_map/ppermute | solution.py:176
  90.8 4.6 %collective-permute-start.7 = (bf16[8,64,128]{2,1,0:T(8,128)(2,1)S(1)}, bf16[8,64,128]{2,1,0:T(8,128)(2,1)S(1)}, u32[]{:S(2)}, u32[]{:S(2)}) collective-permute-start(bf16[8,64,128]{2,1,0:T(8,128)(2,1)S(1)} %sum_other.3), channel_id=1, source_target_pairs={{0,4},{1,5},{2,6},{3,7},{4,0},{5,1},{6,2},{7,3},{8,12},{9,13},{10,... | collective-permute-start | bytes 393224 | tf_op jit(solution)/shard_map/ppermute | solution.py:181
  95.4 7.7 %collective-permute-done.7.refs_9_ = bf16[8,64,128]{2,1,0:T(8,128)(2,1)S(1)} collective-permute-done((bf16[8,64,128]{2,1,0:T(8,128)(2,1)S(1)}, bf16[8,64,128]{2,1,0:T(8,128)(2,1)S(1)}, u32[]{:S(2)}, u32[]{:S(2)}) %collective-permute-start.7) | collective-permute-done | bytes 131104 | tf_op jit(solution)/shard_map/ppermute | solution.py:181
  103.1 2.2 %row_level.1 = bf16[8,128,128]{2,1,0:T(8,128)(2,1)} custom-call(s32[1]{0:T(128)} %bitcast.me_ref, s32[64]{0:T(128)S(1)} %copy-done.5, bf16[64,128,128]{2,1,0:T(8,128)(2,1)S(1)} %copy-done.3, bf16[16,64,128]{2,1,0:T(8,128)(2,1)S(1)} %mid_level.4.refs_0_, bf16[16,64,128]{2,1,0:T(8,128)(2,1)} %collective-permute-done.refs_1_, ...), custom_call_target="tpu_custom_call" | custom-call | flops 33554432 | bytes 1048576 | tf_op jit(solution)/shard_map/row_level/pallas_call | solution.py:161
  (15 shorter events, 0.9 us)
Async XLA Ops:
  6.9 40.9 %copy-start = (bf16[1,64,128,128]{3,2,1,0:T(8,128)(2,1)S(1)}, bf16[1,64,128,128]{3,2,1,0:T(8,128)(2,1)}, u32[]{:S(2)}) copy-start(bf16[1,64,128,128]{3,2,1,0:T(8,128)(2,1)} %param.12) | copy-start | bytes 6291460
  6.9 40.9 %copy-start.4 = (s32[1,64]{1,0:T(1,128)S(1)}, s32[1,64]{1,0:T(1,128)}, u32[]{:S(2)}) copy-start(s32[1,64]{1,0:T(1,128)} %param.13) | copy-start | bytes 772
  41.4 31.8 %all-to-all-start.1 = ((bf16[64,64,128]{2,1,0:T(8,128)(2,1)}), bf16[64,64,128]{2,1,0:T(8,128)(2,1)S(1)}, u32[]{:S(2)}, u32[]{:S(2)}) async-start(bf16[64,64,128]{2,1,0:T(8,128)(2,1)} %get-tuple-element.19), calls=%async_computation.1 | async-start | bytes 2097152 | tf_op jit(solution)/shard_map/all_to_all | solution.py:194
  47.7 1.2 %copy-start.1 = (bf16[64,64,128]{2,1,0:T(8,128)(2,1)S(1)}, bf16[64,64,128]{2,1,0:T(8,128)(2,1)}, u32[]{:S(2)}) copy-start(bf16[64,64,128]{2,1,0:T(8,128)(2,1)} %all_to_all.10.z_ref) | copy-start | bytes 3145732
  50.8 11.0 %collective-permute-start = (bf16[16,64,128]{2,1,0:T(8,128)(2,1)}, bf16[16,64,128]{2,1,0:T(8,128)(2,1)}, u32[]{:S(2)}, u32[]{:S(2)}) collective-permute-start(bf16[16,64,128]{2,1,0:T(8,128)(2,1)} %get-tuple-element.16), channel_id=1, source_target_pairs={{0,2},{1,3},{2,0},{3,1},{4,6},{5,7},{6,4},{7,5},{8,10},{9,11},{10,... | collective-permute-start | bytes 786440 | tf_op jit(solution)/shard_map/ppermute | solution.py:176
  52.2 12.3 %collective-permute-start.1 = (bf16[16,64,128]{2,1,0:T(8,128)(2,1)}, bf16[16,64,128]{2,1,0:T(8,128)(2,1)}, u32[]{:S(2)}, u32[]{:S(2)}) collective-permute-start(bf16[16,64,128]{2,1,0:T(8,128)(2,1)} %get-tuple-element.17), channel_id=1, source_target_pairs={{0,1},{1,2},{2,3},{3,0},{4,5},{5,6},{6,7},{7,4},{8,9},{9,10},{10,1... | collective-permute-start | bytes 786440 | tf_op jit(solution)/shard_map/ppermute | solution.py:176
  54.3 12.3 %collective-permute-start.2 = (bf16[16,64,128]{2,1,0:T(8,128)(2,1)}, bf16[16,64,128]{2,1,0:T(8,128)(2,1)}, u32[]{:S(2)}, u32[]{:S(2)}) collective-permute-start(bf16[16,64,128]{2,1,0:T(8,128)(2,1)} %get-tuple-element.18), channel_id=1, source_target_pairs={{0,3},{1,0},{2,1},{3,2},{4,7},{5,4},{6,5},{7,6},{8,11},{9,8},{10,9... | collective-permute-start | bytes 786440 | tf_op jit(solution)/shard_map/ppermute | solution.py:176
  54.3 1.2 %copy-start.2 = (bf16[64,64,128]{2,1,0:T(8,128)(2,1)S(1)}, bf16[64,64,128]{2,1,0:T(8,128)(2,1)}, u32[]{:S(2)}) copy-start(bf16[64,64,128]{2,1,0:T(8,128)(2,1)} %all_to_all.10.z_ref) | copy-start | bytes 3145732
  74.3 10.5 %collective-permute-start.4 = (bf16[16,64,128]{2,1,0:T(8,128)(2,1)S(1)}, bf16[16,64,128]{2,1,0:T(8,128)(2,1)S(1)}, u32[]{:S(2)}, u32[]{:S(2)}) collective-permute-start(bf16[16,64,128]{2,1,0:T(8,128)(2,1)S(1)} %get-tuple-element.22), channel_id=1, source_target_pairs={{0,2},{1,3},{2,0},{3,1},{4,6},{5,7},{6,4},{7,5},{8,10},{9,11},{10,... | collective-permute-start | bytes 786440 | tf_op jit(solution)/shard_map/ppermute | solution.py:176
  75.8 12.4 %collective-permute-start.5 = (bf16[16,64,128]{2,1,0:T(8,128)(2,1)S(1)}, bf16[16,64,128]{2,1,0:T(8,128)(2,1)S(1)}, u32[]{:S(2)}, u32[]{:S(2)}) collective-permute-start(bf16[16,64,128]{2,1,0:T(8,128)(2,1)S(1)} %get-tuple-element.23), channel_id=1, source_target_pairs={{0,1},{1,2},{2,3},{3,0},{4,5},{5,6},{6,7},{7,4},{8,9},{9,10},{10,1... | collective-permute-start | bytes 786440 | tf_op jit(solution)/shard_map/ppermute | solution.py:176
  78.0 25.2 %copy-start.3 = (bf16[64,128,128]{2,1,0:T(8,128)(2,1)S(1)}, bf16[64,128,128]{2,1,0:T(8,128)(2,1)}, u32[]{:S(2)}) copy-start(bf16[64,128,128]{2,1,0:T(8,128)(2,1)} %w_ref.3) | copy-start | bytes 6291460
  78.0 25.2 %copy-start.5 = (s32[64]{0:T(128)S(1)}, s32[64]{0:T(128)}, u32[]{:S(2)}) copy-start(s32[64]{0:T(128)} %rank_ref.3) | copy-start | bytes 772
  78.0 12.8 %collective-permute-start.6 = (bf16[16,64,128]{2,1,0:T(8,128)(2,1)S(1)}, bf16[16,64,128]{2,1,0:T(8,128)(2,1)S(1)}, u32[]{:S(2)}, u32[]{:S(2)}) collective-permute-start(bf16[16,64,128]{2,1,0:T(8,128)(2,1)S(1)} %get-tuple-element.24), channel_id=1, source_target_pairs={{0,3},{1,0},{2,1},{3,2},{4,7},{5,4},{6,5},{7,6},{8,11},{9,8},{10,9... | collective-permute-start | bytes 786440 | tf_op jit(solution)/shard_map/ppermute | solution.py:176
  78.0 17.5 %collective-permute-start.3 = (bf16[8,64,128]{2,1,0:T(8,128)(2,1)S(1)}, bf16[8,64,128]{2,1,0:T(8,128)(2,1)S(1)}, u32[]{:S(2)}, u32[]{:S(2)}) collective-permute-start(bf16[8,64,128]{2,1,0:T(8,128)(2,1)S(1)} %sum_other.2), channel_id=1, source_target_pairs={{0,4},{1,5},{2,6},{3,7},{4,0},{5,1},{6,2},{7,3},{8,12},{9,13},{10,... | collective-permute-start | bytes 393224 | tf_op jit(solution)/shard_map/ppermute | solution.py:181
  90.8 12.3 %collective-permute-start.7 = (bf16[8,64,128]{2,1,0:T(8,128)(2,1)S(1)}, bf16[8,64,128]{2,1,0:T(8,128)(2,1)S(1)}, u32[]{:S(2)}, u32[]{:S(2)}) collective-permute-start(bf16[8,64,128]{2,1,0:T(8,128)(2,1)S(1)} %sum_other.3), channel_id=1, source_target_pairs={{0,4},{1,5},{2,6},{3,7},{4,0},{5,1},{6,2},{7,3},{8,12},{9,13},{10,... | collective-permute-start | bytes 393224 | tf_op jit(solution)/shard_map/ppermute | solution.py:181

commit v3 on v2

v3 whole, which is shorter than its diff:
```python
import functools

import jax
import jax.numpy as jnp
from jax import lax
from jax.experimental import pallas as pl
from jax.experimental.pallas import tpu as pltpu
from jax.sharding import PartitionSpec as P

BW = 128
HALF = BW // 2
R = 128
PB = 64
STEP = 8
N_X = 4
N_Z = 2
OWN = 8
N_PLANE = 4
N_Y = 4
N_CORE = 2
Q = 2
PIECE = 16
CHUNKS = (80, 48)
BF16 = jnp.bfloat16
ANY = pl.BlockSpec(memory_space=pl.ANY)
SMEM = pl.BlockSpec(memory_space=pltpu.SMEM)
VMEM = pl.BlockSpec(memory_space=pltpu.VMEM)
SMALL = pltpu.CompilerParams(vmem_limit_bytes=12 * 2**20)


def masked_dot(blocks, factors, rank):
    product = jnp.dot(blocks, factors, preferred_element_type=jnp.float32)
    lane = lax.broadcasted_iota(jnp.int32, product.shape, 1)
    return jnp.where(lane < rank, product, 0.0)


def pair(even, odd):
    lane = lax.broadcasted_iota(jnp.int32, even.shape, 1)
    front = jnp.where(lane < HALF, even, pltpu.roll(odd, HALF, 1))
    back = jnp.where(lane < HALF, pltpu.roll(even, HALF, 1), odd)
    return front.astype(BF16), back.astype(BF16)


def col_kernel(at_ref, order_ref, rank_ref, z_ref, w_ref, *refs):
    straight_ref, out_refs = refs[0], refs[1 : 1 + N_CORE]
    z_buf, w_buf, first_buf, sems = refs[1 + N_CORE :]
    early, late = [], []
    for g in range(PB // STEP):
        part = pl.ds(g * STEP, STEP)
        early.append(pltpu.make_async_copy(z_ref.at[part], z_buf.at[part], sems.at[0, g]))
        early.append(pltpu.make_async_copy(w_ref.at[0, part], w_buf.at[0, part], sems.at[1, g]))
        late.append(pltpu.make_async_copy(w_ref.at[1, part], w_buf.at[1, part], sems.at[2, g]))
    for copy in early + late:
        copy.start()
    for g in range(PB // STEP):
        early[2 * g].wait()
        early[2 * g + 1].wait()
        blocks = range(g * STEP, (g + 1) * STEP)
        first = [masked_dot(z_buf[b], w_buf[0, b], rank_ref[0, b]) for b in blocks]
        for j in range(0, STEP, 2):
            front, back = pair(first[j], first[j + 1])
            first_buf[g * STEP + j] = front
            first_buf[g * STEP + j + 1] = back
    for copy in late:
        copy.wait()
    rows = CHUNKS[0]
    for e in range(N_CORE):
        for k in range(N_PLANE):
            for m in range(N_Y):
                for i in range(Q):
                    place = (at_ref[0] ^ flip(k, m, e)) * Q + i
                    b = order_ref[place]
                    middle = masked_dot(first_buf[b], w_buf[1, b], rank_ref[1, b]).astype(BF16)
                    straight_ref[place] = middle[:rows]
                    out_refs[e][(k * N_Y + m) * Q + i] = middle[rows:]


def flip(k, m, e):
    return (k * N_Y + m) * N_CORE + e


def col_levels(at, order, ranks, right_sides, factors):
    straight, stepped = CHUNKS
    return pl.pallas_call(
        col_kernel,
        out_shape=[jax.ShapeDtypeStruct((PB, straight, BW), BF16)]
        + [jax.ShapeDtypeStruct((PB // N_CORE, stepped, BW), BF16)] * N_CORE,
        in_specs=[SMEM, SMEM, SMEM, ANY, ANY],
        out_specs=[VMEM] * (1 + N_CORE),
        scratch_shapes=[
            pltpu.VMEM((PB, R, BW), BF16),
            pltpu.VMEM((2, PB, BW, BW), BF16),
            pltpu.VMEM((PB, R, BW), BF16),
            pltpu.SemaphoreType.DMA((3, PB // STEP)),
        ],
        cost_estimate=pl.CostEstimate(
            flops=4 * PB * R * BW * BW, bytes_accessed=8 * 2**20, transcendentals=0
        ),
        name="col_levels",
    )(at, order, ranks, right_sides, factors)


def regroup_kernel(moves, n_in, *refs):
    for source, start, target, place in moves:
        refs[n_in + target][place : place + Q] = refs[source][start : start + Q]


def regroup(rows, moves, n_out, pieces):
    return pl.pallas_call(
        functools.partial(regroup_kernel, moves, len(pieces)),
        out_shape=[jax.ShapeDtypeStruct((PIECE, rows, BW), BF16)] * n_out,
        in_specs=[VMEM] * len(pieces),
        out_specs=[VMEM] * n_out,
        compiler_params=SMALL,
        cost_estimate=pl.CostEstimate(
            flops=0, bytes_accessed=4 * n_out * PIECE * rows * BW, transcendentals=0
        ),
        name="regroup",
    )(*pieces)


def for_y():
    moves = []
    for m in range(1, N_Y):
        for e in range(N_CORE):
            for k in range(N_PLANE):
                moves.append((e, (k * N_Y + m) * Q, m - 1, (e * N_PLANE + k) * Q))
    return moves


def for_planes():
    moves = []
    for k in range(N_PLANE):
        for m in range(N_Y):
            for e in range(N_CORE):
                place = (m * N_CORE + e) * Q
                if m == 0:
                    moves.append((e, k * N_Y * Q, k, place))
                else:
                    moves.append((N_CORE + m - 1, (e * N_PLANE + k) * Q, k, place))
    return moves


def mid_kernel(offsets, at_ref, rank_ref, z_ref, w_ref, *out_refs):
    for d, out_ref in zip(offsets, out_refs):
        for h in range(N_Z):
            base = (h * N_X + lax.rem(at_ref[1] + d, N_X)) * STEP
            for j in range(STEP):
                inner = masked_dot(z_ref[base + j], w_ref[base + j], rank_ref[base + j])
                out_ref[h * STEP + j] = inner.astype(BF16)


def mid_level(rows, offsets, at, ranks, blocks, factors):
    n = len(offsets)
    count = n * N_Z * STEP
    return pl.pallas_call(
        functools.partial(mid_kernel, offsets),
        out_shape=[jax.ShapeDtypeStruct((N_Z * STEP, rows, BW), BF16)] * n,
        in_specs=[SMEM, SMEM, VMEM, VMEM],
        out_specs=[VMEM] * n,
        compiler_params=SMALL,
        cost_estimate=pl.CostEstimate(
            flops=2 * count * rows * BW * BW,
            bytes_accessed=count * (4 * rows + 2 * BW) * BW,
            transcendentals=0,
        ),
        name="mid_level",
    )(at, ranks, blocks, factors)


def stepped_kernel(at_ref, rank_ref, w_ref, *refs):
    pieces, out_refs, inner_buf = refs[:N_PLANE], refs[N_PLANE:-1], refs[-1]
    for k in range(N_PLANE):
        for m in range(N_Y):
            for e in range(N_CORE):
                for i in range(Q):
                    b = (at_ref[0] ^ flip(k, m, e)) * Q + i
                    block = pieces[k][(m * N_CORE + e) * Q + i]
                    inner_buf[b] = masked_dot(block, w_ref[b], rank_ref[b]).astype(BF16)
    for d, out_ref in enumerate(out_refs):
        for h in range(N_Z):
            base = (h * N_X + lax.rem(at_ref[1] + d, N_X)) * STEP
            out_ref[h * STEP : (h + 1) * STEP] = inner_buf[pl.ds(base, STEP)]


def mid_stepped(rows, at, ranks, factors, pieces):
    return pl.pallas_call(
        stepped_kernel,
        out_shape=[jax.ShapeDtypeStruct((N_Z * STEP, rows, BW), BF16)] * N_X,
        in_specs=[SMEM, SMEM, VMEM] + [VMEM] * N_PLANE,
        out_specs=[VMEM] * N_X,
        scratch_shapes=[pltpu.VMEM((PB, rows, BW), BF16)],
        compiler_params=SMALL,
        cost_estimate=pl.CostEstimate(
            flops=2 * PB * rows * BW * BW,
            bytes_accessed=PB * (4 * rows + 2 * BW) * BW,
            transcendentals=0,
        ),
        name="mid_stepped",
    )(at, ranks, factors, *pieces)


def total_of(refs, half):
    total = refs[0][half].astype(jnp.float32)
    for ref in refs[1:]:
        total = total + ref[half].astype(jnp.float32)
    return total


def sum_kernel(at_ref, *refs):
    half = pl.ds((1 - at_ref[2]) * STEP, STEP)
    refs[N_X][...] = total_of(refs[:N_X], half).astype(BF16)


def sum_other(rows, at, parts):
    return pl.pallas_call(
        sum_kernel,
        out_shape=jax.ShapeDtypeStruct((STEP, rows, BW), BF16),
        in_specs=[SMEM] + [VMEM] * N_X,
        out_specs=VMEM,
        compiler_params=SMALL,
        cost_estimate=pl.CostEstimate(
            flops=4 * STEP * rows * BW, bytes_accessed=10 * STEP * rows * BW, transcendentals=0
        ),
        name="sum_other",
    )(at, *parts)


def row_kernel(at_ref, rank_ref, w_ref, *refs):
    out_ref = refs[-1]
    base = at_ref[3] * OWN
    half = pl.ds(at_ref[2] * STEP, STEP)
    start = 0
    for n, rows in enumerate(CHUNKS):
        near = refs[n * (N_X + 1) : n * (N_X + 1) + N_X]
        far = refs[n * (N_X + 1) + N_X]
        total = total_of(near, half) + far[...].astype(jnp.float32)
        for j in range(0, OWN, 2):
            for i, block in enumerate(pair(total[j], total[j + 1])):
                product = masked_dot(block, w_ref[base + j + i], rank_ref[base + j + i])
                out_ref[j + i, start : start + rows] = product.astype(BF16)
        start += rows


def row_level(at, ranks, factors, parts):
    return pl.pallas_call(
        row_kernel,
        out_shape=jax.ShapeDtypeStruct((OWN, R, BW), BF16),
        in_specs=[SMEM, SMEM, VMEM] + [VMEM] * len(parts),
        out_specs=VMEM,
        compiler_params=SMALL,
        cost_estimate=pl.CostEstimate(
            flops=2 * OWN * R * BW * BW, bytes_accessed=2**20, transcendentals=0
        ),
        name="row_level",
    )(at, ranks, factors, *parts)


def around_x(value, d):
    pairs = [(z * N_X + x, z * N_X + (x + d) % N_X) for z in range(N_Z) for x in range(N_X)]
    return lax.ppermute(value, "col", pairs)


def across_z(value):
    half = N_X * N_Z // 2
    return lax.ppermute(value, "col", [(i, (i + half) % (2 * half)) for i in range(2 * half)])


def across_row(value, k, m, e):
    return lax.ppermute(
        value, "row", [(r, r ^ flip(k, m, e)) for r in range(N_PLANE * N_Y * N_CORE)]
    )


def shards(
    right_sides, col_factors, col_ranks, block_order, mid_factors, mid_ranks, row_factors, row_ranks
):
    me = lax.axis_index("col").astype(jnp.int32)
    row = lax.axis_index("row").astype(jnp.int32)
    at = jnp.stack([row, lax.rem(me, N_X), lax.div(me, N_X), me])
    ranks, factors = mid_ranks[0], mid_factors[0]
    straight_rows, stepped_rows = CHUNKS
    middle, same, other = col_levels(at, block_order[0], col_ranks, right_sides, col_factors)

    regrouped = lax.all_to_all(middle, "row", split_axis=0, concat_axis=0, tiled=True)

    cores = [same, across_row(other, 0, 0, 1)]
    pieces = regroup(stepped_rows, for_y(), N_Y - 1, cores)
    lines = [across_row(piece, 0, m + 1, 0) for m, piece in enumerate(pieces)]
    pieces = regroup(stepped_rows, for_planes(), N_PLANE, cores + lines)
    planes = [pieces[0]] + [across_row(pieces[k], k, 0, 0) for k in range(1, N_PLANE)]

    sent = mid_level(straight_rows, (2, 1, 3), at, ranks, regrouped, factors)
    kept = mid_level(straight_rows, (0,), at, ranks, regrouped, factors)
    near = list(kept) + [around_x(piece, d) for piece, d in zip(sent, (2, 1, 3))]
    parts = near + [across_z(sum_other(straight_rows, at, near))]

    inner = mid_stepped(stepped_rows, at, ranks, factors, planes)
    near = [inner[0]] + [around_x(inner[d], d) for d in (2, 1, 3)]
    parts += near + [across_z(sum_other(stepped_rows, at, near))]
    return row_level(at, row_ranks, row_factors, parts)


def solution(mesh):
    in_specs = (
        P(("col", "row"), None, None),
        P(None, ("col", "row"), None, None),
        P(None, ("col", "row")),
        P(("col", "row"), None),
        P("col", "row", None, None),
        P("col", "row"),
        P("row", None, None),
        P("row"),
    )
    out_specs = P(("row", "col"), None, None)
    return jax.shard_map(shards, mesh=mesh, in_specs=in_specs, out_specs=out_specs, check_vma=False)
```

time: 106 us -> 96.6 us (0.911)
  the two profiles are of different devices: /device:TPU:38 before, /device:TPU:8 now
where the time goes in v3:
time: 96.6 us; the launch traced here: 96.3 us
  waiting for transfers between devices  42.9 us (44%)
  starting transfers between devices  35.8 us (37%)
  Pallas kernels  13.8 us (14%)
  local copies, waits for them, and re-layouts  3.09 us (3%)
    ppermute x7, waiting for transfers between devices, across_row(): lax.ppermute(value, 'row', [(r, r ^ flip(k, m, e)) for r in range(N_PLANE...  28.4 us
    ppermute x6, starting transfers between devices, around_x(): return lax.ppermute(value, 'col', pairs)  9.88 us
    all_to_all x1, starting transfers between devices, shards(): lax.all_to_all(middle, 'row', split_axis=0, concat_axis=0, tiled=True)  9.28 us
    ppermute x2, starting transfers between devices, across_z(): lax.ppermute(value, 'col', [(i, (i + half) % (2 * half)) for i in range(2...  9.16 us
    ppermute x7, starting transfers between devices, across_row(): lax.ppermute(value, 'row', [(r, r ^ flip(k, m, e)) for r in range(N_PLANE...  7.48 us
    pallas_call x1, Pallas kernels, col_levels(): pl.pallas_call(col_kernel, out_shape=[jax.ShapeDtypeStruct((PB, straight,...  6.33 us
    ppermute x2, waiting for transfers between devices, across_z(): lax.ppermute(value, 'col', [(i, (i + half) % (2 * half)) for i in range(2...  6.14 us
    all_to_all x1, waiting for transfers between devices, shards(): lax.all_to_all(middle, 'row', split_axis=0, concat_axis=0, tiled=True)  5.84 us
  transfers between devices with their start and end apart: 16, of which 8 were waited for; matrix products, arithmetic and copies ran while one was open for 0% of the time, Pallas kernels for 6%

profile of v3, /device:TPU:8, one launch (start us, length us, event | category | flops | bytes accessed | tf_op | source)
XLA Modules:
  0.0 96.3 jit_solution(522351973356560368)
XLA Ops:
  0.6 6.3 %col_levels.1 = (bf16[64,80,128]{2,1,0:T(8,128)(2,1)}, bf16[32,48,128]{2,1,0:T(8,128)(2,1)}, bf16[32,48,128]{2,1,0:T(8,128)(2,1)}) custom-call(s32[4]{0:T(128)} %pad_add_fusion.at_ref, s32[64]{0:T(128)} %bitcast.13, s32[2,64]{1,0:T(2,128)} %rank_ref.2, bf16[64,128,128]{2,1,0:T(8,128)(2,1)} %z_ref.1, bf16[2,64,128,128]{3,2,1,0:T(8,128)(2,1)} %w_ref.2), custom_call_target="tpu_custom_call" | custom-call | flops 536870912 | bytes 8388608 | tf_op jit(solution)/shard_map/col_levels/pallas_call | solution.py:84
  7.0 9.3 %all-to-all-start = ((bf16[64,80,128]{2,1,0:T(8,128)(2,1)}), bf16[64,80,128]{2,1,0:T(8,128)(2,1)S(1)}, u32[]{:S(2)}, u32[]{:S(2)}) async-start(bf16[64,80,128]{2,1,0:T(8,128)(2,1)} %get-tuple-element.22), calls=%async_computation | async-start | bytes 2621440 | tf_op jit(solution)/shard_map/all_to_all | solution.py:285
  16.5 1.8 %collective-permute-done.4.refs_1_ = bf16[32,48,128]{2,1,0:T(8,128)(2,1)S(1)} collective-permute-done((bf16[32,48,128]{2,1,0:T(8,128)(2,1)}, bf16[32,48,128]{2,1,0:T(8,128)(2,1)S(1)}, u32[]{:S(2)}, u32[]{:S(2)}) %collective-permute-start.4) | collective-permute-done | bytes 393248 | tf_op jit(solution)/shard_map/ppermute | solution.py:270
  18.3 1.0 %copy-done.2 = bf16[32,48,128]{2,1,0:T(8,128)(2,1)S(1)} copy-done((bf16[32,48,128]{2,1,0:T(8,128)(2,1)S(1)}, bf16[32,48,128]{2,1,0:T(8,128)(2,1)}, u32[]{:S(2)}) %copy-start.2) | copy-done | bytes 393240
  19.6 2.7 %collective-permute-start.6 = (bf16[16,48,128]{2,1,0:T(8,128)(2,1)S(1)}, bf16[16,48,128]{2,1,0:T(8,128)(2,1)S(1)}, u32[]{:S(2)}, u32[]{:S(2)}) collective-permute-start(bf16[16,48,128]{2,1,0:T(8,128)(2,1)S(1)} %get-tuple-element.29), channel_id=1, source_target_pairs={{0,32},{8,40},{16,48},{24,56},{32,0},{40,8},{48,16},{56,24},{64,96... | collective-permute-start | bytes 589832 | tf_op jit(solution)/shard_map/ppermute | solution.py:270
  22.9 9.8 %collective-permute-done.5.refs_2_ = bf16[16,48,128]{2,1,0:T(8,128)(2,1)S(1)} collective-permute-done((bf16[16,48,128]{2,1,0:T(8,128)(2,1)S(1)}, bf16[16,48,128]{2,1,0:T(8,128)(2,1)S(1)}, u32[]{:S(2)}, u32[]{:S(2)}) %collective-permute-start.5) | collective-permute-done | bytes 196640 | tf_op jit(solution)/shard_map/ppermute | solution.py:270
  32.7 7.6 %collective-permute-done.6.refs_3_ = bf16[16,48,128]{2,1,0:T(8,128)(2,1)S(1)} collective-permute-done((bf16[16,48,128]{2,1,0:T(8,128)(2,1)S(1)}, bf16[16,48,128]{2,1,0:T(8,128)(2,1)S(1)}, u32[]{:S(2)}, u32[]{:S(2)}) %collective-permute-start.6) | collective-permute-done | bytes 196640 | tf_op jit(solution)/shard_map/ppermute | solution.py:270
  43.1 3.6 %collective-permute-start.10 = (bf16[16,48,128]{2,1,0:T(8,128)(2,1)}, bf16[16,48,128]{2,1,0:T(8,128)(2,1)}, u32[]{:S(2)}, u32[]{:S(2)}) collective-permute-start(bf16[16,48,128]{2,1,0:T(8,128)(2,1)} %get-tuple-element.34), channel_id=1, source_target_pairs={{0,192},{8,200},{16,208},{24,216},{32,224},{40,232},{48,240},{56,2... | collective-permute-start | bytes 589832 | tf_op jit(solution)/shard_map/ppermute | solution.py:270
  46.6 5.8 %all-to-all-done.z_ref = bf16[64,80,128]{2,1,0:T(8,128)(2,1)S(1)} async-done(((bf16[64,80,128]{2,1,0:T(8,128)(2,1)}), bf16[64,80,128]{2,1,0:T(8,128)(2,1)S(1)}, u32[]{:S(2)}, u32[]{:S(2)}) %all-to-all-start) | async-done | bytes 1310752 | tf_op jit(solution)/shard_map/all_to_all | solution.py:285
  52.5 1.2 %mid_level.3 = (bf16[16,80,128]{2,1,0:T(8,128)(2,1)S(1)}, bf16[16,80,128]{2,1,0:T(8,128)(2,1)S(1)}, bf16[16,80,128]{2,1,0:T(8,128)(2,1)S(1)}) custom-call(s32[4]{0:T(128)S(1)} %copy-done.5, s32[64]{0:T(128)S(1)} %bitcast.10, bf16[64,80,128]{2,1,0:T(8,128)(2,1)S(1)} %all-to-all-done.z_ref, bf16[64,128,128]{2,1,0:T(8,128)(2,1)S(1)} %bitcast.7), custom_call_target="tpu_custom_call" | custom-call | flops 125829120 | bytes 3538944 | tf_op jit(solution)/shard_map/mid_level/pallas_call | solution.py:156
  53.7 2.7 %collective-permute-start = (bf16[16,80,128]{2,1,0:T(8,128)(2,1)S(1)}, bf16[16,80,128]{2,1,0:T(8,128)(2,1)S(1)}, u32[]{:S(2)}, u32[]{:S(2)}) collective-permute-start(bf16[16,80,128]{2,1,0:T(8,128)(2,1)S(1)} %get-tuple-element.23), channel_id=1, source_target_pairs={{0,2},{1,3},{2,0},{3,1},{4,6},{5,7},{6,4},{7,5},{8,10},{9,11},{10,... | collective-permute-start | bytes 983048 | tf_op jit(solution)/shard_map/ppermute | solution.py:261
  56.6 1.1 %collective-permute-start.1 = (bf16[16,80,128]{2,1,0:T(8,128)(2,1)S(1)}, bf16[16,80,128]{2,1,0:T(8,128)(2,1)S(1)}, u32[]{:S(2)}, u32[]{:S(2)}) collective-permute-start(bf16[16,80,128]{2,1,0:T(8,128)(2,1)S(1)} %get-tuple-element.24), channel_id=1, source_target_pairs={{0,1},{1,2},{2,3},{3,0},{4,5},{5,6},{6,7},{7,4},{8,9},{9,10},{10,1... | collective-permute-start | bytes 983048 | tf_op jit(solution)/shard_map/ppermute | solution.py:261
  57.6 2.2 %collective-permute-start.2 = (bf16[16,80,128]{2,1,0:T(8,128)(2,1)S(1)}, bf16[16,80,128]{2,1,0:T(8,128)(2,1)S(1)}, u32[]{:S(2)}, u32[]{:S(2)}) collective-permute-start(bf16[16,80,128]{2,1,0:T(8,128)(2,1)S(1)} %get-tuple-element.25), channel_id=1, source_target_pairs={{0,3},{1,0},{2,1},{3,2},{4,7},{5,4},{6,5},{7,6},{8,11},{9,8},{10,9... | collective-permute-start | bytes 983048 | tf_op jit(solution)/shard_map/ppermute | solution.py:261
  59.9 2.9 %collective-permute-done.8.refs_1_ = bf16[16,48,128]{2,1,0:T(8,128)(2,1)S(1)} collective-permute-done((bf16[16,48,128]{2,1,0:T(8,128)(2,1)S(1)}, bf16[16,48,128]{2,1,0:T(8,128)(2,1)S(1)}, u32[]{:S(2)}, u32[]{:S(2)}) %collective-permute-start.8) | collective-permute-done | bytes 196640 | tf_op jit(solution)/shard_map/ppermute | solution.py:270
  62.8 6.4 %collective-permute-done.9.refs_2_ = bf16[16,48,128]{2,1,0:T(8,128)(2,1)S(1)} collective-permute-done((bf16[16,48,128]{2,1,0:T(8,128)(2,1)S(1)}, bf16[16,48,128]{2,1,0:T(8,128)(2,1)S(1)}, u32[]{:S(2)}, u32[]{:S(2)}) %collective-permute-start.9) | collective-permute-done | bytes 196640 | tf_op jit(solution)/shard_map/ppermute | solution.py:270
  69.1 1.7 %mid_stepped.1 = (bf16[16,48,128]{2,1,0:T(8,128)(2,1)S(1)}, bf16[16,48,128]{2,1,0:T(8,128)(2,1)S(1)}, bf16[16,48,128]{2,1,0:T(8,128)(2,1)S(1)}, bf16[16,48,128]{2,1,0:T(8,128)(2,1)S(1)}) custom-call(s32[4]{0:T(128)S(1)} %copy-done.5, s32[64]{0:T(128)S(1)} %bitcast.11, bf16[64,128,128]{2,1,0:T(8,128)(2,1)S(1)} %bitcast.8, bf16[16,48,128]{2,1,0:T(8,128)(2,1)S(1)} %copy-done.4, ...), custom_call_target="tpu_custom_call" | custom-call | flops 100663296 | bytes 3670016 | tf_op jit(solution)/shard_map/mid_stepped/pallas_call | solution.py:187
  71.5 1.5 %collective-permute-start.12 = (bf16[16,48,128]{2,1,0:T(8,128)(2,1)S(1)}, bf16[16,48,128]{2,1,0:T(8,128)(2,1)S(1)}, u32[]{:S(2)}, u32[]{:S(2)}) collective-permute-start(bf16[16,48,128]{2,1,0:T(8,128)(2,1)S(1)} %get-tuple-element.37), channel_id=1, source_target_pairs={{0,1},{1,2},{2,3},{3,0},{4,5},{5,6},{6,7},{7,4},{8,9},{9,10},{10,1... | collective-permute-start | bytes 589832 | tf_op jit(solution)/shard_map/ppermute | solution.py:261
  73.0 1.7 %collective-permute-start.13 = (bf16[16,48,128]{2,1,0:T(8,128)(2,1)S(1)}, bf16[16,48,128]{2,1,0:T(8,128)(2,1)S(1)}, u32[]{:S(2)}, u32[]{:S(2)}) collective-permute-start(bf16[16,48,128]{2,1,0:T(8,128)(2,1)S(1)} %get-tuple-element.38), channel_id=1, source_target_pairs={{0,3},{1,0},{2,1},{3,2},{4,7},{5,4},{6,5},{7,6},{8,11},{9,8},{10,9... | collective-permute-start | bytes 589832 | tf_op jit(solution)/shard_map/ppermute | solution.py:261
  74.7 0.9 mid_level.2.refs_0_
  76.3 4.6 %collective-permute-start.3 = (bf16[8,80,128]{2,1,0:T(8,128)(2,1)S(1)}, bf16[8,80,128]{2,1,0:T(8,128)(2,1)S(1)}, u32[]{:S(2)}, u32[]{:S(2)}) collective-permute-start(bf16[8,80,128]{2,1,0:T(8,128)(2,1)S(1)} %sum_other.2), channel_id=1, source_target_pairs={{0,4},{1,5},{2,6},{3,7},{4,0},{5,1},{6,2},{7,3},{8,12},{9,13},{10,... | collective-permute-start | bytes 491528 | tf_op jit(solution)/shard_map/ppermute | solution.py:266
  80.9 2.5 %collective-permute-done.12.refs_2_.refs_7_ = bf16[16,48,128]{2,1,0:T(8,128)(2,1)S(1)} collective-permute-done((bf16[16,48,128]{2,1,0:T(8,128)(2,1)S(1)}, bf16[16,48,128]{2,1,0:T(8,128)(2,1)S(1)}, u32[]{:S(2)}, u32[]{:S(2)}) %collective-permute-start.12) | collective-permute-done | bytes 196640 | tf_op jit(solution)/shard_map/ppermute | solution.py:261
  83.9 4.6 %collective-permute-start.14 = (bf16[8,48,128]{2,1,0:T(8,128)(2,1)S(1)}, bf16[8,48,128]{2,1,0:T(8,128)(2,1)S(1)}, u32[]{:S(2)}, u32[]{:S(2)}) collective-permute-start(bf16[8,48,128]{2,1,0:T(8,128)(2,1)S(1)} %sum_other.3), channel_id=1, source_target_pairs={{0,4},{1,5},{2,6},{3,7},{4,0},{5,1},{6,2},{7,3},{8,12},{9,13},{10,... | collective-permute-start | bytes 294920 | tf_op jit(solution)/shard_map/ppermute | solution.py:266
  88.5 6.1 %collective-permute-done.14.refs_9_ = bf16[8,48,128]{2,1,0:T(8,128)(2,1)S(1)} collective-permute-done((bf16[8,48,128]{2,1,0:T(8,128)(2,1)S(1)}, bf16[8,48,128]{2,1,0:T(8,128)(2,1)S(1)}, u32[]{:S(2)}, u32[]{:S(2)}) %collective-permute-start.14) | collective-permute-done | bytes 98336 | tf_op jit(solution)/shard_map/ppermute | solution.py:266
  94.7 1.6 %row_level.1 = bf16[8,128,128]{2,1,0:T(8,128)(2,1)} custom-call(s32[4]{0:T(128)S(1)} %copy-done.5, s32[64]{0:T(128)S(1)} %copy-done.7, bf16[64,128,128]{2,1,0:T(8,128)(2,1)S(1)} %copy-done.1, bf16[16,80,128]{2,1,0:T(8,128)(2,1)S(1)} %mid_level.2.refs_0_, bf16[16,80,128]{2,1,0:T(8,128)(2,1)S(1)} %collective-permute-done.refs_1_, ...), custom_call_target="tpu_custom_call" | custom-call | flops 33554432 | bytes 1048576 | tf_op jit(solution)/shard_map/row_level/pallas_call | solution.py:246
  (42 shorter events, 6.5 us)
Async XLA Ops:
  6.9 45.6 %copy-start = (bf16[1,64,128,128]{3,2,1,0:T(8,128)(2,1)S(1)}, bf16[1,64,128,128]{3,2,1,0:T(8,128)(2,1)}, u32[]{:S(2)}) copy-start(bf16[1,64,128,128]{3,2,1,0:T(8,128)(2,1)} %param.12) | copy-start | bytes 6291460
  6.9 45.6 %copy-start.5 = (s32[4]{0:T(128)S(1)}, s32[4]{0:T(128)}, u32[]{:S(2)}) copy-start(s32[4]{0:T(128)} %pad_add_fusion.at_ref) | copy-start | bytes 52
  6.9 45.6 %copy-start.6 = (s32[1,64]{1,0:T(1,128)S(1)}, s32[1,64]{1,0:T(1,128)}, u32[]{:S(2)}) copy-start(s32[1,64]{1,0:T(1,128)} %param.13) | copy-start | bytes 772
  7.0 45.5 %all-to-all-start = ((bf16[64,80,128]{2,1,0:T(8,128)(2,1)}), bf16[64,80,128]{2,1,0:T(8,128)(2,1)S(1)}, u32[]{:S(2)}, u32[]{:S(2)}) async-start(bf16[64,80,128]{2,1,0:T(8,128)(2,1)} %get-tuple-element.22), calls=%async_computation | async-start | bytes 2621440 | tf_op jit(solution)/shard_map/all_to_all | solution.py:285
  16.2 2.0 %collective-permute-start.4 = (bf16[32,48,128]{2,1,0:T(8,128)(2,1)}, bf16[32,48,128]{2,1,0:T(8,128)(2,1)S(1)}, u32[]{:S(2)}, u32[]{:S(2)}) collective-permute-start(bf16[32,48,128]{2,1,0:T(8,128)(2,1)} %get-tuple-element.27), channel_id=1, source_target_pairs={{0,8},{8,0},{16,24},{24,16},{32,40},{40,32},{48,56},{56,48},{64,72... | collective-permute-start | bytes 1179656 | tf_op jit(solution)/shard_map/ppermute | solution.py:270
  19.3 13.4 %collective-permute-start.5 = (bf16[16,48,128]{2,1,0:T(8,128)(2,1)S(1)}, bf16[16,48,128]{2,1,0:T(8,128)(2,1)S(1)}, u32[]{:S(2)}, u32[]{:S(2)}) collective-permute-start(bf16[16,48,128]{2,1,0:T(8,128)(2,1)S(1)} %get-tuple-element.28), channel_id=1, source_target_pairs={{0,16},{8,24},{16,0},{24,8},{32,48},{40,56},{48,32},{56,40},{64,80... | collective-permute-start | bytes 589832 | tf_op jit(solution)/shard_map/ppermute | solution.py:270
  19.6 20.7 %collective-permute-start.6 = (bf16[16,48,128]{2,1,0:T(8,128)(2,1)S(1)}, bf16[16,48,128]{2,1,0:T(8,128)(2,1)S(1)}, u32[]{:S(2)}, u32[]{:S(2)}) collective-permute-start(bf16[16,48,128]{2,1,0:T(8,128)(2,1)S(1)} %get-tuple-element.29), channel_id=1, source_target_pairs={{0,32},{8,40},{16,48},{24,56},{32,0},{40,8},{48,16},{56,24},{64,96... | collective-permute-start | bytes 589832 | tf_op jit(solution)/shard_map/ppermute | solution.py:270
  22.3 18.0 %collective-permute-start.7 = (bf16[16,48,128]{2,1,0:T(8,128)(2,1)S(1)}, bf16[16,48,128]{2,1,0:T(8,128)(2,1)S(1)}, u32[]{:S(2)}, u32[]{:S(2)}) collective-permute-start(bf16[16,48,128]{2,1,0:T(8,128)(2,1)S(1)} %get-tuple-element.30), channel_id=1, source_target_pairs={{0,48},{8,56},{16,32},{24,40},{32,16},{40,24},{48,0},{56,8},{64,11... | collective-permute-start | bytes 589832 | tf_op jit(solution)/shard_map/ppermute | solution.py:270
  43.1 14.6 %collective-permute-start.10 = (bf16[16,48,128]{2,1,0:T(8,128)(2,1)}, bf16[16,48,128]{2,1,0:T(8,128)(2,1)}, u32[]{:S(2)}, u32[]{:S(2)}) collective-permute-start(bf16[16,48,128]{2,1,0:T(8,128)(2,1)} %get-tuple-element.34), channel_id=1, source_target_pairs={{0,192},{8,200},{16,208},{24,216},{32,224},{40,232},{48,240},{56,2... | collective-permute-start | bytes 589832 | tf_op jit(solution)/shard_map/ppermute | solution.py:270
  52.5 4.0 %copy-start.11 = (bf16[16,48,128]{2,1,0:T(8,128)(2,1)S(1)}, bf16[16,48,128]{2,1,0:T(8,128)(2,1)}, u32[]{:S(2)}) copy-start(bf16[16,48,128]{2,1,0:T(8,128)(2,1)} %copy-done.10) | copy-start | bytes 589828
  52.5 4.0 %copy-start.9 = (bf16[16,48,128]{2,1,0:T(8,128)(2,1)S(1)}, bf16[16,48,128]{2,1,0:T(8,128)(2,1)}, u32[]{:S(2)}) copy-start(bf16[16,48,128]{2,1,0:T(8,128)(2,1)} %copy-done.8) | copy-start | bytes 589828
  52.5 16.7 %copy-start.4 = (bf16[16,48,128]{2,1,0:T(8,128)(2,1)S(1)}, bf16[16,48,128]{2,1,0:T(8,128)(2,1)}, u32[]{:S(2)}) copy-start(bf16[16,48,128]{2,1,0:T(8,128)(2,1)} %copy-done.3) | copy-start | bytes 589828
  53.7 19.2 %collective-permute-start = (bf16[16,80,128]{2,1,0:T(8,128)(2,1)S(1)}, bf16[16,80,128]{2,1,0:T(8,128)(2,1)S(1)}, u32[]{:S(2)}, u32[]{:S(2)}) collective-permute-start(bf16[16,80,128]{2,1,0:T(8,128)(2,1)S(1)} %get-tuple-element.23), channel_id=1, source_target_pairs={{0,2},{1,3},{2,0},{3,1},{4,6},{5,7},{6,4},{7,5},{8,10},{9,11},{10,... | collective-permute-start | bytes 983048 | tf_op jit(solution)/shard_map/ppermute | solution.py:261
  56.5 6.3 %collective-permute-start.8 = (bf16[16,48,128]{2,1,0:T(8,128)(2,1)S(1)}, bf16[16,48,128]{2,1,0:T(8,128)(2,1)S(1)}, u32[]{:S(2)}, u32[]{:S(2)}) collective-permute-start(bf16[16,48,128]{2,1,0:T(8,128)(2,1)S(1)} %copy-done.11), channel_id=1, source_target_pairs={{0,64},{8,72},{16,80},{24,88},{32,96},{40,104},{48,112},{56,120},{... | collective-permute-start | bytes 589832 | tf_op jit(solution)/shard_map/ppermute | solution.py:270
  56.5 12.6 %collective-permute-start.9 = (bf16[16,48,128]{2,1,0:T(8,128)(2,1)S(1)}, bf16[16,48,128]{2,1,0:T(8,128)(2,1)S(1)}, u32[]{:S(2)}, u32[]{:S(2)}) collective-permute-start(bf16[16,48,128]{2,1,0:T(8,128)(2,1)S(1)} %copy-done.9), channel_id=1, source_target_pairs={{0,128},{8,136},{16,144},{24,152},{32,160},{40,168},{48,176},{56,1... | collective-permute-start | bytes 589832 | tf_op jit(solution)/shard_map/ppermute | solution.py:270
  56.6 19.0 %collective-permute-start.1 = (bf16[16,80,128]{2,1,0:T(8,128)(2,1)S(1)}, bf16[16,80,128]{2,1,0:T(8,128)(2,1)S(1)}, u32[]{:S(2)}, u32[]{:S(2)}) collective-permute-start(bf16[16,80,128]{2,1,0:T(8,128)(2,1)S(1)} %get-tuple-element.24), channel_id=1, source_target_pairs={{0,1},{1,2},{2,3},{3,0},{4,5},{5,6},{6,7},{7,4},{8,9},{9,10},{10,1... | collective-permute-start | bytes 983048 | tf_op jit(solution)/shard_map/ppermute | solution.py:261
  57.6 18.0 %collective-permute-start.2 = (bf16[16,80,128]{2,1,0:T(8,128)(2,1)S(1)}, bf16[16,80,128]{2,1,0:T(8,128)(2,1)S(1)}, u32[]{:S(2)}, u32[]{:S(2)}) collective-permute-start(bf16[16,80,128]{2,1,0:T(8,128)(2,1)S(1)} %get-tuple-element.25), channel_id=1, source_target_pairs={{0,3},{1,0},{2,1},{3,2},{4,7},{5,4},{6,5},{7,6},{8,11},{9,8},{10,9... | collective-permute-start | bytes 983048 | tf_op jit(solution)/shard_map/ppermute | solution.py:261
  70.8 10.0 %collective-permute-start.11 = (bf16[16,48,128]{2,1,0:T(8,128)(2,1)S(1)}, bf16[16,48,128]{2,1,0:T(8,128)(2,1)S(1)}, u32[]{:S(2)}, u32[]{:S(2)}) collective-permute-start(bf16[16,48,128]{2,1,0:T(8,128)(2,1)S(1)} %get-tuple-element.36), channel_id=1, source_target_pairs={{0,2},{1,3},{2,0},{3,1},{4,6},{5,7},{6,4},{7,5},{8,10},{9,11},{10,... | collective-permute-start | bytes 589832 | tf_op jit(solution)/shard_map/ppermute | solution.py:261
  71.5 11.9 %collective-permute-start.12 = (bf16[16,48,128]{2,1,0:T(8,128)(2,1)S(1)}, bf16[16,48,128]{2,1,0:T(8,128)(2,1)S(1)}, u32[]{:S(2)}, u32[]{:S(2)}) collective-permute-start(bf16[16,48,128]{2,1,0:T(8,128)(2,1)S(1)} %get-tuple-element.37), channel_id=1, source_target_pairs={{0,1},{1,2},{2,3},{3,0},{4,5},{5,6},{6,7},{7,4},{8,9},{9,10},{10,1... | collective-permute-start | bytes 589832 | tf_op jit(solution)/shard_map/ppermute | solution.py:261
  73.0 10.4 %collective-permute-start.13 = (bf16[16,48,128]{2,1,0:T(8,128)(2,1)S(1)}, bf16[16,48,128]{2,1,0:T(8,128)(2,1)S(1)}, u32[]{:S(2)}, u32[]{:S(2)}) collective-permute-start(bf16[16,48,128]{2,1,0:T(8,128)(2,1)S(1)} %get-tuple-element.38), channel_id=1, source_target_pairs={{0,3},{1,0},{2,1},{3,2},{4,7},{5,4},{6,5},{7,6},{8,11},{9,8},{10,9... | collective-permute-start | bytes 589832 | tf_op jit(solution)/shard_map/ppermute | solution.py:261
  75.6 19.1 %copy-start.1 = (bf16[64,128,128]{2,1,0:T(8,128)(2,1)S(1)}, bf16[64,128,128]{2,1,0:T(8,128)(2,1)}, u32[]{:S(2)}) copy-start(bf16[64,128,128]{2,1,0:T(8,128)(2,1)} %w_ref.3) | copy-start | bytes 6291460
  75.6 19.1 %copy-start.7 = (s32[64]{0:T(128)S(1)}, s32[64]{0:T(128)}, u32[]{:S(2)}) copy-start(s32[64]{0:T(128)} %rank_ref.3) | copy-start | bytes 772
  76.3 18.4 %collective-permute-start.3 = (bf16[8,80,128]{2,1,0:T(8,128)(2,1)S(1)}, bf16[8,80,128]{2,1,0:T(8,128)(2,1)S(1)}, u32[]{:S(2)}, u32[]{:S(2)}) collective-permute-start(bf16[8,80,128]{2,1,0:T(8,128)(2,1)S(1)} %sum_other.2), channel_id=1, source_target_pairs={{0,4},{1,5},{2,6},{3,7},{4,0},{5,1},{6,2},{7,3},{8,12},{9,13},{10,... | collective-permute-start | bytes 491528 | tf_op jit(solution)/shard_map/ppermute | solution.py:266
  83.9 10.7 %collective-permute-start.14 = (bf16[8,48,128]{2,1,0:T(8,128)(2,1)S(1)}, bf16[8,48,128]{2,1,0:T(8,128)(2,1)S(1)}, u32[]{:S(2)}, u32[]{:S(2)}) collective-permute-start(bf16[8,48,128]{2,1,0:T(8,128)(2,1)S(1)} %sum_other.3), channel_id=1, source_target_pairs={{0,4},{1,5},{2,6},{3,7},{4,0},{5,1},{6,2},{7,3},{8,12},{9,13},{10,... | collective-permute-start | bytes 294920 | tf_op jit(solution)/shard_map/ppermute | solution.py:266
  (4 other events, 3.0 us)

commit v4 on v3

--- a/solution.py
+++ b/solution.py
@@ -41,7 +41,7 @@
     return front.astype(BF16), back.astype(BF16)
 
 
-def col_kernel(at_ref, order_ref, rank_ref, z_ref, w_ref, *refs):
+def col_kernel(row_ref, me_ref, order_ref, rank_ref, z_ref, w_ref, *refs):
     straight_ref, out_refs = refs[0], refs[1 : 1 + N_CORE]
     z_buf, w_buf, first_buf, sems = refs[1 + N_CORE :]
     early, late = [], []
@@ -68,7 +68,7 @@
         for k in range(N_PLANE):
             for m in range(N_Y):
                 for i in range(Q):
-                    place = (at_ref[0] ^ flip(k, m, e)) * Q + i
+                    place = (row_ref[0] ^ flip(k, m, e)) * Q + i
                     b = order_ref[place]
                     middle = masked_dot(first_buf[b], w_buf[1, b], rank_ref[1, b]).astype(BF16)
                     straight_ref[place] = middle[:rows]
@@ -79,13 +79,13 @@
     return (k * N_Y + m) * N_CORE + e
 
 
-def col_levels(at, order, ranks, right_sides, factors):
+def col_levels(row, me, order, ranks, right_sides, factors):
     straight, stepped = CHUNKS
     return pl.pallas_call(
         col_kernel,
         out_shape=[jax.ShapeDtypeStruct((PB, straight, BW), BF16)]
         + [jax.ShapeDtypeStruct((PB // N_CORE, stepped, BW), BF16)] * N_CORE,
-        in_specs=[SMEM, SMEM, SMEM, ANY, ANY],
+        in_specs=[SMEM, SMEM, SMEM, SMEM, ANY, ANY],
         out_specs=[VMEM] * (1 + N_CORE),
         scratch_shapes=[
             pltpu.VMEM((PB, R, BW), BF16),
@@ -97,7 +97,7 @@
             flops=4 * PB * R * BW * BW, bytes_accessed=8 * 2**20, transcendentals=0
         ),
         name="col_levels",
-    )(at, order, ranks, right_sides, factors)
+    )(row, me, order, ranks, right_sides, factors)
 
 
 def regroup_kernel(moves, n_in, *refs):
@@ -141,16 +141,16 @@
     return moves
 
 
-def mid_kernel(offsets, at_ref, rank_ref, z_ref, w_ref, *out_refs):
+def mid_kernel(offsets, me_ref, rank_ref, z_ref, w_ref, *out_refs):
     for d, out_ref in zip(offsets, out_refs):
         for h in range(N_Z):
-            base = (h * N_X + lax.rem(at_ref[1] + d, N_X)) * STEP
+            base = (h * N_X + lax.rem(me_ref[0] + d, N_X)) * STEP
             for j in range(STEP):
                 inner = masked_dot(z_ref[base + j], w_ref[base + j], rank_ref[base + j])
                 out_ref[h * STEP + j] = inner.astype(BF16)
 
 
-def mid_level(rows, offsets, at, ranks, blocks, factors):
+def mid_level(rows, offsets, me, ranks, blocks, factors):
     n = len(offsets)
     count = n * N_Z * STEP
     return pl.pallas_call(
@@ -165,29 +165,29 @@
             transcendentals=0,
         ),
         name="mid_level",
-    )(at, ranks, blocks, factors)
-
-
-def stepped_kernel(at_ref, rank_ref, w_ref, *refs):
+    )(me, ranks, blocks, factors)
+
+
+def stepped_kernel(row_ref, me_ref, rank_ref, w_ref, *refs):
     pieces, out_refs, inner_buf = refs[:N_PLANE], refs[N_PLANE:-1], refs[-1]
     for k in range(N_PLANE):
         for m in range(N_Y):
             for e in range(N_CORE):
                 for i in range(Q):
-                    b = (at_ref[0] ^ flip(k, m, e)) * Q + i
+                    b = (row_ref[0] ^ flip(k, m, e)) * Q + i
                     block = pieces[k][(m * N_CORE + e) * Q + i]
                     inner_buf[b] = masked_dot(block, w_ref[b], rank_ref[b]).astype(BF16)
     for d, out_ref in enumerate(out_refs):
         for h in range(N_Z):
-            base = (h * N_X + lax.rem(at_ref[1] + d, N_X)) * STEP
+            base = (h * N_X + lax.rem(me_ref[0] + d, N_X)) * STEP
             out_ref[h * STEP : (h + 1) * STEP] = inner_buf[pl.ds(base, STEP)]
 
 
-def mid_stepped(rows, at, ranks, factors, pieces):
+def mid_stepped(rows, row, me, ranks, factors, pieces):
     return pl.pallas_call(
         stepped_kernel,
         out_shape=[jax.ShapeDtypeStruct((N_Z * STEP, rows, BW), BF16)] * N_X,
-        in_specs=[SMEM, SMEM, VMEM] + [VMEM] * N_PLANE,
+        in_specs=[SMEM, SMEM, SMEM, VMEM] + [VMEM] * N_PLANE,
         out_specs=[VMEM] * N_X,
         scratch_shapes=[pltpu.VMEM((PB, rows, BW), BF16)],
         compiler_params=SMALL,
@@ -197,7 +197,7 @@
             transcendentals=0,
         ),
         name="mid_stepped",
-    )(at, ranks, factors, *pieces)
+    )(row, me, ranks, factors, *pieces)
 
 
 def total_of(refs, half):
@@ -207,12 +207,12 @@
     return total
 
 
-def sum_kernel(at_ref, *refs):
-    half = pl.ds((1 - at_ref[2]) * STEP, STEP)
+def sum_kernel(me_ref, *refs):
+    half = pl.ds((1 - lax.div(me_ref[0], N_X)) * STEP, STEP)
     refs[N_X][...] = total_of(refs[:N_X], half).astype(BF16)
 
 
-def sum_other(rows, at, parts):
+def sum_other(rows, me, parts):
     return pl.pallas_call(
         sum_kernel,
         out_shape=jax.ShapeDtypeStruct((STEP, rows, BW), BF16),
@@ -223,13 +223,13 @@
             flops=4 * STEP * rows * BW, bytes_accessed=10 * STEP * rows * BW, transcendentals=0
         ),
         name="sum_other",
-    )(at, *parts)
-
-
-def row_kernel(at_ref, rank_ref, w_ref, *refs):
+    )(me, *parts)
+
+
+def row_kernel(me_ref, rank_ref, w_ref, *refs):
     out_ref = refs[-1]
-    base = at_ref[3] * OWN
-    half = pl.ds(at_ref[2] * STEP, STEP)
+    base = me_ref[0] * OWN
+    half = pl.ds(lax.div(me_ref[0], N_X) * STEP, STEP)
     start = 0
     for n, rows in enumerate(CHUNKS):
         near = refs[n * (N_X + 1) : n * (N_X + 1) + N_X]
@@ -242,7 +242,7 @@
         start += rows
 
 
-def row_level(at, ranks, factors, parts):
+def row_level(me, ranks, factors, parts):
     return pl.pallas_call(
         row_kernel,
         out_shape=jax.ShapeDtypeStruct((OWN, R, BW), BF16),
@@ -253,7 +253,7 @@
             flops=2 * OWN * R * BW * BW, bytes_accessed=2**20, transcendentals=0
         ),
         name="row_level",
-    )(at, ranks, factors, *parts)
+    )(me, ranks, factors, *parts)
 
 
 def around_x(value, d):
@@ -275,12 +275,13 @@
 def shards(
     right_sides, col_factors, col_ranks, block_order, mid_factors, mid_ranks, row_factors, row_ranks
 ):
-    me = lax.axis_index("col").astype(jnp.int32)
-    row = lax.axis_index("row").astype(jnp.int32)
-    at = jnp.stack([row, lax.rem(me, N_X), lax.div(me, N_X), me])
+    me = lax.axis_index("col").astype(jnp.int32).reshape(1)
+    row = lax.axis_index("row").astype(jnp.int32).reshape(1)
     ranks, factors = mid_ranks[0], mid_factors[0]
     straight_rows, stepped_rows = CHUNKS
-    middle, same, other = col_levels(at, block_order[0], col_ranks, right_sides, col_factors)
+    middle, same, other = col_levels(
+        row, me, block_order[0], col_ranks, right_sides, col_factors
+    )
 
     regrouped = lax.all_to_all(middle, "row", split_axis=0, concat_axis=0, tiled=True)
 
@@ -290,15 +291,14 @@
     pieces = regroup(stepped_rows, for_planes(), N_PLANE, cores + lines)
     planes = [pieces[0]] + [across_row(pieces[k], k, 0, 0) for k in range(1, N_PLANE)]
 
-    sent = mid_level(straight_rows, (2, 1, 3), at, ranks, regrouped, factors)
-    kept = mid_level(straight_rows, (0,), at, ranks, regrouped, factors)
-    near = list(kept) + [around_x(piece, d) for piece, d in zip(sent, (2, 1, 3))]
-    parts = near + [across_z(sum_other(straight_rows, at, near))]
-
-    inner = mid_stepped(stepped_rows, at, ranks, factors, planes)
+    inner = mid_level(straight_rows, (0, 1, 2, 3), me, ranks, regrouped, factors)
     near = [inner[0]] + [around_x(inner[d], d) for d in (2, 1, 3)]
-    parts += near + [across_z(sum_other(stepped_rows, at, near))]
-    return row_level(at, row_ranks, row_factors, parts)
+    parts = near + [across_z(sum_other(straight_rows, me, near))]
+
+    inner = mid_stepped(stepped_rows, row, me, ranks, factors, planes)
+    near = [inner[0]] + [around_x(inner[d], d) for d in (2, 1, 3)]
+    parts += near + [across_z(sum_other(stepped_rows, me, near))]
+    return row_level(me, row_ranks, row_factors, parts)
 
 
 def solution(mesh):

time: 96.6 us -> 93.8 us (0.971)
  Pallas kernels: 13.8 us -> 12.1 us
    ppermute x2, waiting for transfers between devices: 6.14 us -> 4.21 us  [across_z(): lax.ppermute(value, 'col', [(i, (i + half) % (2 * half)) for i in range(2...]
    ppermute x6, waiting for transfers between devices: 2.5 us -> 3.99 us  [around_x(): return lax.ppermute(value, 'col', pairs)]
    pallas_call x2, Pallas kernels: 1.23 us -> 0.14 us  [sum_other(): pl.pallas_call(sum_kernel, out_shape=jax.ShapeDtypeStruct((STEP, rows, BW...]
    pallas_call x2 -> x1, Pallas kernels: 2.1 us -> 1.39 us  [mid_level(): pl.pallas_call(functools.partial(mid_kernel, offsets), out_shape=[jax.Sha...]
    unnamed x24 -> x22, local copies, waits for them, and re-layouts: 3.09 us -> 3.07 us
  transfers between devices with their start and end apart: 16 -> 16, of which waited for: 8 -> 9; matrix products, arithmetic and copies ran while one was open for 0% -> 0% of each run, Pallas kernels for 6% -> 4%
where the time goes in v4:
time: 93.8 us; the launch traced here: 93.6 us
  waiting for transfers between devices  42.4 us (45%)
  starting transfers between devices  35.9 us (38%)
  Pallas kernels  12.1 us (13%)
  local copies, waits for them, and re-layouts  3.07 us (3%)
    ppermute x7, waiting for transfers between devices, across_row(): lax.ppermute(value, 'row', [(r, r ^ flip(k, m, e)) for r in range(N_PLANE...  28.3 us
    ppermute x6, starting transfers between devices, around_x(): return lax.ppermute(value, 'col', pairs)  10 us
    all_to_all x1, starting transfers between devices, shards(): lax.all_to_all(middle, 'row', split_axis=0, concat_axis=0, tiled=True)  9.28 us
    ppermute x2, starting transfers between devices, across_z(): lax.ppermute(value, 'col', [(i, (i + half) % (2 * half)) for i in range(2...  9.16 us
    ppermute x7, starting transfers between devices, across_row(): lax.ppermute(value, 'row', [(r, r ^ flip(k, m, e)) for r in range(N_PLANE...  7.48 us
    pallas_call x1, Pallas kernels, col_levels(): pl.pallas_call(col_kernel, out_shape=[jax.ShapeDtypeStruct((PB, straight,...  6.31 us
    all_to_all x1, waiting for transfers between devices, shards(): lax.all_to_all(middle, 'row', split_axis=0, concat_axis=0, tiled=True)  5.85 us
    ppermute x2, waiting for transfers between devices, across_z(): lax.ppermute(value, 'col', [(i, (i + half) % (2 * half)) for i in range(2...  4.21 us
  transfers between devices with their start and end apart: 16, of which 9 were waited for; matrix products, arithmetic and copies ran while one was open for 0% of the time, Pallas kernels for 4%

profile of v4, /device:TPU:8, one launch (start us, length us, event | category | flops | bytes accessed | tf_op | source)
XLA Modules:
  0.0 93.6 jit_solution(13163654712709659796)
XLA Ops:
  0.0 6.3 %col_levels.1 = (bf16[64,80,128]{2,1,0:T(8,128)(2,1)}, bf16[32,48,128]{2,1,0:T(8,128)(2,1)}, bf16[32,48,128]{2,1,0:T(8,128)(2,1)}) custom-call(s32[1]{0:T(128)} %bitcast.2.row_ref, s32[1]{0:T(128)} %bitcast.me_ref, s32[64]{0:T(128)} %bitcast.9, s32[2,64]{1,0:T(2,128)} %rank_ref.2, bf16[64,128,128]{2,1,0:T(8,128)(2,1)} %z_ref.1, bf16[2,64,128,128]{3,2,1,0:T(8,128)(2,1)} %w_ref.2), custom_call_target="tpu_custom_call" | custom-call | flops 536870912 | bytes 8388608 | tf_op jit(solution)/shard_map/col_levels/pallas_call | solution.py:84
  6.3 9.3 %all-to-all-start = ((bf16[64,80,128]{2,1,0:T(8,128)(2,1)}), bf16[64,80,128]{2,1,0:T(8,128)(2,1)S(1)}, u32[]{:S(2)}, u32[]{:S(2)}) async-start(bf16[64,80,128]{2,1,0:T(8,128)(2,1)} %get-tuple-element.23), calls=%async_computation | async-start | bytes 2621440 | tf_op jit(solution)/shard_map/all_to_all | solution.py:286
  15.9 1.8 %collective-permute-done.4.refs_1_ = bf16[32,48,128]{2,1,0:T(8,128)(2,1)S(1)} collective-permute-done((bf16[32,48,128]{2,1,0:T(8,128)(2,1)}, bf16[32,48,128]{2,1,0:T(8,128)(2,1)S(1)}, u32[]{:S(2)}, u32[]{:S(2)}) %collective-permute-start.4) | collective-permute-done | bytes 393248 | tf_op jit(solution)/shard_map/ppermute | solution.py:270
  17.6 1.0 %copy-done.2 = bf16[32,48,128]{2,1,0:T(8,128)(2,1)S(1)} copy-done((bf16[32,48,128]{2,1,0:T(8,128)(2,1)S(1)}, bf16[32,48,128]{2,1,0:T(8,128)(2,1)}, u32[]{:S(2)}) %copy-start.2) | copy-done | bytes 393240
  19.0 2.7 %collective-permute-start.6 = (bf16[16,48,128]{2,1,0:T(8,128)(2,1)S(1)}, bf16[16,48,128]{2,1,0:T(8,128)(2,1)S(1)}, u32[]{:S(2)}, u32[]{:S(2)}) collective-permute-start(bf16[16,48,128]{2,1,0:T(8,128)(2,1)S(1)} %get-tuple-element.31), channel_id=1, source_target_pairs={{0,32},{8,40},{16,48},{24,56},{32,0},{40,8},{48,16},{56,24},{64,96... | collective-permute-start | bytes 589832 | tf_op jit(solution)/shard_map/ppermute | solution.py:270
  22.3 9.8 %collective-permute-done.5.refs_2_ = bf16[16,48,128]{2,1,0:T(8,128)(2,1)S(1)} collective-permute-done((bf16[16,48,128]{2,1,0:T(8,128)(2,1)S(1)}, bf16[16,48,128]{2,1,0:T(8,128)(2,1)S(1)}, u32[]{:S(2)}, u32[]{:S(2)}) %collective-permute-start.5) | collective-permute-done | bytes 196640 | tf_op jit(solution)/shard_map/ppermute | solution.py:270
  32.1 7.6 %collective-permute-done.6.refs_3_ = bf16[16,48,128]{2,1,0:T(8,128)(2,1)S(1)} collective-permute-done((bf16[16,48,128]{2,1,0:T(8,128)(2,1)S(1)}, bf16[16,48,128]{2,1,0:T(8,128)(2,1)S(1)}, u32[]{:S(2)}, u32[]{:S(2)}) %collective-permute-start.6) | collective-permute-done | bytes 196640 | tf_op jit(solution)/shard_map/ppermute | solution.py:270
  42.4 3.6 %collective-permute-start.10 = (bf16[16,48,128]{2,1,0:T(8,128)(2,1)}, bf16[16,48,128]{2,1,0:T(8,128)(2,1)}, u32[]{:S(2)}, u32[]{:S(2)}) collective-permute-start(bf16[16,48,128]{2,1,0:T(8,128)(2,1)} %get-tuple-element.36), channel_id=1, source_target_pairs={{0,192},{8,200},{16,208},{24,216},{32,224},{40,232},{48,240},{56,2... | collective-permute-start | bytes 589832 | tf_op jit(solution)/shard_map/ppermute | solution.py:270
  46.0 5.9 %all-to-all-done.z_ref = bf16[64,80,128]{2,1,0:T(8,128)(2,1)S(1)} async-done(((bf16[64,80,128]{2,1,0:T(8,128)(2,1)}), bf16[64,80,128]{2,1,0:T(8,128)(2,1)S(1)}, u32[]{:S(2)}, u32[]{:S(2)}) %all-to-all-start) | async-done | bytes 1310752 | tf_op jit(solution)/shard_map/all_to_all | solution.py:286
  51.9 1.4 %mid_level.1 = (bf16[16,80,128]{2,1,0:T(8,128)(2,1)S(1)}, bf16[16,80,128]{2,1,0:T(8,128)(2,1)S(1)}, bf16[16,80,128]{2,1,0:T(8,128)(2,1)S(1)}, bf16[16,80,128]{2,1,0:T(8,128)(2,1)S(1)}) custom-call(s32[1]{0:T(128)} %bitcast.me_ref, s32[64]{0:T(128)S(1)} %bitcast.7, bf16[64,80,128]{2,1,0:T(8,128)(2,1)S(1)} %all-to-all-done.z_ref, bf16[64,128,128]{2,1,0:T(8,128)(2,1)S(1)} %bitcast.5), custom_call_target="tpu_custom_call" | custom-call | flops 167772160 | bytes 4718592 | tf_op jit(solution)/shard_map/mid_level/pallas_call | solution.py:156
  53.3 2.9 %collective-permute-start = (bf16[16,80,128]{2,1,0:T(8,128)(2,1)S(1)}, bf16[16,80,128]{2,1,0:T(8,128)(2,1)S(1)}, u32[]{:S(2)}, u32[]{:S(2)}) collective-permute-start(bf16[16,80,128]{2,1,0:T(8,128)(2,1)S(1)} %get-tuple-element.25), channel_id=1, source_target_pairs={{0,2},{1,3},{2,0},{3,1},{4,6},{5,7},{6,4},{7,5},{8,10},{9,11},{10,... | collective-permute-start | bytes 983048 | tf_op jit(solution)/shard_map/ppermute | solution.py:261
  56.3 0.9 collective-permute-start.1
  57.2 2.4 %collective-permute-start.2 = (bf16[16,80,128]{2,1,0:T(8,128)(2,1)S(1)}, bf16[16,80,128]{2,1,0:T(8,128)(2,1)S(1)}, u32[]{:S(2)}, u32[]{:S(2)}) collective-permute-start(bf16[16,80,128]{2,1,0:T(8,128)(2,1)S(1)} %get-tuple-element.27), channel_id=1, source_target_pairs={{0,3},{1,0},{2,1},{3,2},{4,7},{5,4},{6,5},{7,6},{8,11},{9,8},{10,9... | collective-permute-start | bytes 983048 | tf_op jit(solution)/shard_map/ppermute | solution.py:261
  59.6 2.8 %collective-permute-done.8.refs_1_ = bf16[16,48,128]{2,1,0:T(8,128)(2,1)S(1)} collective-permute-done((bf16[16,48,128]{2,1,0:T(8,128)(2,1)S(1)}, bf16[16,48,128]{2,1,0:T(8,128)(2,1)S(1)}, u32[]{:S(2)}, u32[]{:S(2)}) %collective-permute-start.8) | collective-permute-done | bytes 196640 | tf_op jit(solution)/shard_map/ppermute | solution.py:270
  62.5 6.3 %collective-permute-done.9.refs_2_ = bf16[16,48,128]{2,1,0:T(8,128)(2,1)S(1)} collective-permute-done((bf16[16,48,128]{2,1,0:T(8,128)(2,1)S(1)}, bf16[16,48,128]{2,1,0:T(8,128)(2,1)S(1)}, u32[]{:S(2)}, u32[]{:S(2)}) %collective-permute-start.9) | collective-permute-done | bytes 196640 | tf_op jit(solution)/shard_map/ppermute | solution.py:270
  68.7 1.8 %mid_stepped.1 = (bf16[16,48,128]{2,1,0:T(8,128)(2,1)S(1)}, bf16[16,48,128]{2,1,0:T(8,128)(2,1)S(1)}, bf16[16,48,128]{2,1,0:T(8,128)(2,1)S(1)}, bf16[16,48,128]{2,1,0:T(8,128)(2,1)S(1)}) custom-call(s32[1]{0:T(128)} %bitcast.2.row_ref, s32[1]{0:T(128)} %bitcast.me_ref, s32[64]{0:T(128)S(1)} %bitcast.8, bf16[64,128,128]{2,1,0:T(8,128)(2,1)S(1)} %bitcast.6, ...), custom_call_target="tpu_custom_call" | custom-call | flops 100663296 | bytes 3670016 | tf_op jit(solution)/shard_map/mid_stepped/pallas_call | solution.py:187
  71.2 1.5 %collective-permute-start.12 = (bf16[16,48,128]{2,1,0:T(8,128)(2,1)S(1)}, bf16[16,48,128]{2,1,0:T(8,128)(2,1)S(1)}, u32[]{:S(2)}, u32[]{:S(2)}) collective-permute-start(bf16[16,48,128]{2,1,0:T(8,128)(2,1)S(1)} %get-tuple-element.39), channel_id=1, source_target_pairs={{0,1},{1,2},{2,3},{3,0},{4,5},{5,6},{6,7},{7,4},{8,9},{9,10},{10,1... | collective-permute-start | bytes 589832 | tf_op jit(solution)/shard_map/ppermute | solution.py:261
  72.6 1.7 %collective-permute-start.13 = (bf16[16,48,128]{2,1,0:T(8,128)(2,1)S(1)}, bf16[16,48,128]{2,1,0:T(8,128)(2,1)S(1)}, u32[]{:S(2)}, u32[]{:S(2)}) collective-permute-start(bf16[16,48,128]{2,1,0:T(8,128)(2,1)S(1)} %get-tuple-element.40), channel_id=1, source_target_pairs={{0,3},{1,0},{2,1},{3,2},{4,7},{5,4},{6,5},{7,6},{8,11},{9,8},{10,9... | collective-permute-start | bytes 589832 | tf_op jit(solution)/shard_map/ppermute | solution.py:261
  74.5 4.6 %collective-permute-start.3 = (bf16[8,80,128]{2,1,0:T(8,128)(2,1)S(1)}, bf16[8,80,128]{2,1,0:T(8,128)(2,1)S(1)}, u32[]{:S(2)}, u32[]{:S(2)}) collective-permute-start(bf16[8,80,128]{2,1,0:T(8,128)(2,1)S(1)} %sum_other.2), channel_id=1, source_target_pairs={{0,4},{1,5},{2,6},{3,7},{4,0},{5,1},{6,2},{7,3},{8,12},{9,13},{10,... | collective-permute-start | bytes 491528 | tf_op jit(solution)/shard_map/ppermute | solution.py:266
  79.1 0.9 collective-permute-done.11.refs_1_.refs_6_
  80.0 3.1 %collective-permute-done.12.refs_2_.refs_7_ = bf16[16,48,128]{2,1,0:T(8,128)(2,1)S(1)} collective-permute-done((bf16[16,48,128]{2,1,0:T(8,128)(2,1)S(1)}, bf16[16,48,128]{2,1,0:T(8,128)(2,1)S(1)}, u32[]{:S(2)}, u32[]{:S(2)}) %collective-permute-start.12) | collective-permute-done | bytes 196640 | tf_op jit(solution)/shard_map/ppermute | solution.py:261
  83.1 4.6 %collective-permute-start.14 = (bf16[8,48,128]{2,1,0:T(8,128)(2,1)S(1)}, bf16[8,48,128]{2,1,0:T(8,128)(2,1)S(1)}, u32[]{:S(2)}, u32[]{:S(2)}) collective-permute-start(bf16[8,48,128]{2,1,0:T(8,128)(2,1)S(1)} %sum_other.3), channel_id=1, source_target_pairs={{0,4},{1,5},{2,6},{3,7},{4,0},{5,1},{6,2},{7,3},{8,12},{9,13},{10,... | collective-permute-start | bytes 294920 | tf_op jit(solution)/shard_map/ppermute | solution.py:266
  87.7 4.2 %collective-permute-done.14.refs_9_ = bf16[8,48,128]{2,1,0:T(8,128)(2,1)S(1)} collective-permute-done((bf16[8,48,128]{2,1,0:T(8,128)(2,1)S(1)}, bf16[8,48,128]{2,1,0:T(8,128)(2,1)S(1)}, u32[]{:S(2)}, u32[]{:S(2)}) %collective-permute-start.14) | collective-permute-done | bytes 98336 | tf_op jit(solution)/shard_map/ppermute | solution.py:266
  91.9 1.7 %row_level.1 = bf16[8,128,128]{2,1,0:T(8,128)(2,1)} custom-call(s32[1]{0:T(128)} %bitcast.me_ref, s32[64]{0:T(128)S(1)} %copy-done.6, bf16[64,128,128]{2,1,0:T(8,128)(2,1)S(1)} %copy-done.1, bf16[16,80,128]{2,1,0:T(8,128)(2,1)S(1)} %get-tuple-element.24.refs_0_, bf16[16,80,128]{2,1,0:T(8,128)(2,1)S(1)} %collective-permute-done.refs_1_, ...), custom_call_target="tpu_custom_call" | custom-call | flops 33554432 | bytes 1048576 | tf_op jit(solution)/shard_map/row_level/pallas_call | solution.py:246
  (38 shorter events, 4.8 us)
Async XLA Ops:
  6.3 45.6 %copy-start = (bf16[1,64,128,128]{3,2,1,0:T(8,128)(2,1)S(1)}, bf16[1,64,128,128]{3,2,1,0:T(8,128)(2,1)}, u32[]{:S(2)}) copy-start(bf16[1,64,128,128]{3,2,1,0:T(8,128)(2,1)} %param.12) | copy-start | bytes 6291460
  6.3 45.6 %copy-start.5 = (s32[1,64]{1,0:T(1,128)S(1)}, s32[1,64]{1,0:T(1,128)}, u32[]{:S(2)}) copy-start(s32[1,64]{1,0:T(1,128)} %param.13) | copy-start | bytes 772
  6.3 45.5 %all-to-all-start = ((bf16[64,80,128]{2,1,0:T(8,128)(2,1)}), bf16[64,80,128]{2,1,0:T(8,128)(2,1)S(1)}, u32[]{:S(2)}, u32[]{:S(2)}) async-start(bf16[64,80,128]{2,1,0:T(8,128)(2,1)} %get-tuple-element.23), calls=%async_computation | async-start | bytes 2621440 | tf_op jit(solution)/shard_map/all_to_all | solution.py:286
  15.6 2.0 %collective-permute-start.4 = (bf16[32,48,128]{2,1,0:T(8,128)(2,1)}, bf16[32,48,128]{2,1,0:T(8,128)(2,1)S(1)}, u32[]{:S(2)}, u32[]{:S(2)}) collective-permute-start(bf16[32,48,128]{2,1,0:T(8,128)(2,1)} %get-tuple-element.29), channel_id=1, source_target_pairs={{0,8},{8,0},{16,24},{24,16},{32,40},{40,32},{48,56},{56,48},{64,72... | collective-permute-start | bytes 1179656 | tf_op jit(solution)/shard_map/ppermute | solution.py:270
  17.6 1.0 %copy-start.2 = (bf16[32,48,128]{2,1,0:T(8,128)(2,1)S(1)}, bf16[32,48,128]{2,1,0:T(8,128)(2,1)}, u32[]{:S(2)}) copy-start(bf16[32,48,128]{2,1,0:T(8,128)(2,1)} %get-tuple-element.28.refs_0_) | copy-start | bytes 1179652
  18.7 13.4 %collective-permute-start.5 = (bf16[16,48,128]{2,1,0:T(8,128)(2,1)S(1)}, bf16[16,48,128]{2,1,0:T(8,128)(2,1)S(1)}, u32[]{:S(2)}, u32[]{:S(2)}) collective-permute-start(bf16[16,48,128]{2,1,0:T(8,128)(2,1)S(1)} %get-tuple-element.30), channel_id=1, source_target_pairs={{0,16},{8,24},{16,0},{24,8},{32,48},{40,56},{48,32},{56,40},{64,80... | collective-permute-start | bytes 589832 | tf_op jit(solution)/shard_map/ppermute | solution.py:270
  19.0 20.7 %collective-permute-start.6 = (bf16[16,48,128]{2,1,0:T(8,128)(2,1)S(1)}, bf16[16,48,128]{2,1,0:T(8,128)(2,1)S(1)}, u32[]{:S(2)}, u32[]{:S(2)}) collective-permute-start(bf16[16,48,128]{2,1,0:T(8,128)(2,1)S(1)} %get-tuple-element.31), channel_id=1, source_target_pairs={{0,32},{8,40},{16,48},{24,56},{32,0},{40,8},{48,16},{56,24},{64,96... | collective-permute-start | bytes 589832 | tf_op jit(solution)/shard_map/ppermute | solution.py:270
  21.7 18.0 %collective-permute-start.7 = (bf16[16,48,128]{2,1,0:T(8,128)(2,1)S(1)}, bf16[16,48,128]{2,1,0:T(8,128)(2,1)S(1)}, u32[]{:S(2)}, u32[]{:S(2)}) collective-permute-start(bf16[16,48,128]{2,1,0:T(8,128)(2,1)S(1)} %get-tuple-element.32), channel_id=1, source_target_pairs={{0,48},{8,56},{16,32},{24,40},{32,16},{40,24},{48,0},{56,8},{64,11... | collective-permute-start | bytes 589832 | tf_op jit(solution)/shard_map/ppermute | solution.py:270
  42.4 14.7 %collective-permute-start.10 = (bf16[16,48,128]{2,1,0:T(8,128)(2,1)}, bf16[16,48,128]{2,1,0:T(8,128)(2,1)}, u32[]{:S(2)}, u32[]{:S(2)}) collective-permute-start(bf16[16,48,128]{2,1,0:T(8,128)(2,1)} %get-tuple-element.36), channel_id=1, source_target_pairs={{0,192},{8,200},{16,208},{24,216},{32,224},{40,232},{48,240},{56,2... | collective-permute-start | bytes 589832 | tf_op jit(solution)/shard_map/ppermute | solution.py:270
  51.9 4.3 %copy-start.10 = (bf16[16,48,128]{2,1,0:T(8,128)(2,1)S(1)}, bf16[16,48,128]{2,1,0:T(8,128)(2,1)}, u32[]{:S(2)}) copy-start(bf16[16,48,128]{2,1,0:T(8,128)(2,1)} %copy-done.9) | copy-start | bytes 589828
  51.9 4.3 %copy-start.8 = (bf16[16,48,128]{2,1,0:T(8,128)(2,1)S(1)}, bf16[16,48,128]{2,1,0:T(8,128)(2,1)}, u32[]{:S(2)}) copy-start(bf16[16,48,128]{2,1,0:T(8,128)(2,1)} %copy-done.7) | copy-start | bytes 589828
  51.9 16.9 %copy-start.4 = (bf16[16,48,128]{2,1,0:T(8,128)(2,1)S(1)}, bf16[16,48,128]{2,1,0:T(8,128)(2,1)}, u32[]{:S(2)}) copy-start(bf16[16,48,128]{2,1,0:T(8,128)(2,1)} %copy-done.3) | copy-start | bytes 589828
  53.3 19.4 %collective-permute-start = (bf16[16,80,128]{2,1,0:T(8,128)(2,1)S(1)}, bf16[16,80,128]{2,1,0:T(8,128)(2,1)S(1)}, u32[]{:S(2)}, u32[]{:S(2)}) collective-permute-start(bf16[16,80,128]{2,1,0:T(8,128)(2,1)S(1)} %get-tuple-element.25), channel_id=1, source_target_pairs={{0,2},{1,3},{2,0},{3,1},{4,6},{5,7},{6,4},{7,5},{8,10},{9,11},{10,... | collective-permute-start | bytes 983048 | tf_op jit(solution)/shard_map/ppermute | solution.py:261
  56.2 6.3 %collective-permute-start.8 = (bf16[16,48,128]{2,1,0:T(8,128)(2,1)S(1)}, bf16[16,48,128]{2,1,0:T(8,128)(2,1)S(1)}, u32[]{:S(2)}, u32[]{:S(2)}) collective-permute-start(bf16[16,48,128]{2,1,0:T(8,128)(2,1)S(1)} %copy-done.10), channel_id=1, source_target_pairs={{0,64},{8,72},{16,80},{24,88},{32,96},{40,104},{48,112},{56,120},{... | collective-permute-start | bytes 589832 | tf_op jit(solution)/shard_map/ppermute | solution.py:270
  56.2 12.5 %collective-permute-start.9 = (bf16[16,48,128]{2,1,0:T(8,128)(2,1)S(1)}, bf16[16,48,128]{2,1,0:T(8,128)(2,1)S(1)}, u32[]{:S(2)}, u32[]{:S(2)}) collective-permute-start(bf16[16,48,128]{2,1,0:T(8,128)(2,1)S(1)} %copy-done.8), channel_id=1, source_target_pairs={{0,128},{8,136},{16,144},{24,152},{32,160},{40,168},{48,176},{56,1... | collective-permute-start | bytes 589832 | tf_op jit(solution)/shard_map/ppermute | solution.py:270
  56.3 18.1 %collective-permute-start.1 = (bf16[16,80,128]{2,1,0:T(8,128)(2,1)S(1)}, bf16[16,80,128]{2,1,0:T(8,128)(2,1)S(1)}, u32[]{:S(2)}, u32[]{:S(2)}) collective-permute-start(bf16[16,80,128]{2,1,0:T(8,128)(2,1)S(1)} %get-tuple-element.26), channel_id=1, source_target_pairs={{0,1},{1,2},{2,3},{3,0},{4,5},{5,6},{6,7},{7,4},{8,9},{9,10},{10,1... | collective-permute-start | bytes 983048 | tf_op jit(solution)/shard_map/ppermute | solution.py:261
  57.2 17.2 %collective-permute-start.2 = (bf16[16,80,128]{2,1,0:T(8,128)(2,1)S(1)}, bf16[16,80,128]{2,1,0:T(8,128)(2,1)S(1)}, u32[]{:S(2)}, u32[]{:S(2)}) collective-permute-start(bf16[16,80,128]{2,1,0:T(8,128)(2,1)S(1)} %get-tuple-element.27), channel_id=1, source_target_pairs={{0,3},{1,0},{2,1},{3,2},{4,7},{5,4},{6,5},{7,6},{8,11},{9,8},{10,9... | collective-permute-start | bytes 983048 | tf_op jit(solution)/shard_map/ppermute | solution.py:261
  68.7 23.2 %copy-start.1 = (bf16[64,128,128]{2,1,0:T(8,128)(2,1)S(1)}, bf16[64,128,128]{2,1,0:T(8,128)(2,1)}, u32[]{:S(2)}) copy-start(bf16[64,128,128]{2,1,0:T(8,128)(2,1)} %w_ref.3) | copy-start | bytes 6291460
  68.7 23.2 %copy-start.6 = (s32[64]{0:T(128)S(1)}, s32[64]{0:T(128)}, u32[]{:S(2)}) copy-start(s32[64]{0:T(128)} %rank_ref.3) | copy-start | bytes 772
  70.6 9.4 %collective-permute-start.11 = (bf16[16,48,128]{2,1,0:T(8,128)(2,1)S(1)}, bf16[16,48,128]{2,1,0:T(8,128)(2,1)S(1)}, u32[]{:S(2)}, u32[]{:S(2)}) collective-permute-start(bf16[16,48,128]{2,1,0:T(8,128)(2,1)S(1)} %get-tuple-element.38), channel_id=1, source_target_pairs={{0,2},{1,3},{2,0},{3,1},{4,6},{5,7},{6,4},{7,5},{8,10},{9,11},{10,... | collective-permute-start | bytes 589832 | tf_op jit(solution)/shard_map/ppermute | solution.py:261
  71.2 11.9 %collective-permute-start.12 = (bf16[16,48,128]{2,1,0:T(8,128)(2,1)S(1)}, bf16[16,48,128]{2,1,0:T(8,128)(2,1)S(1)}, u32[]{:S(2)}, u32[]{:S(2)}) collective-permute-start(bf16[16,48,128]{2,1,0:T(8,128)(2,1)S(1)} %get-tuple-element.39), channel_id=1, source_target_pairs={{0,1},{1,2},{2,3},{3,0},{4,5},{5,6},{6,7},{7,4},{8,9},{9,10},{10,1... | collective-permute-start | bytes 589832 | tf_op jit(solution)/shard_map/ppermute | solution.py:261
  72.6 10.4 %collective-permute-start.13 = (bf16[16,48,128]{2,1,0:T(8,128)(2,1)S(1)}, bf16[16,48,128]{2,1,0:T(8,128)(2,1)S(1)}, u32[]{:S(2)}, u32[]{:S(2)}) collective-permute-start(bf16[16,48,128]{2,1,0:T(8,128)(2,1)S(1)} %get-tuple-element.40), channel_id=1, source_target_pairs={{0,3},{1,0},{2,1},{3,2},{4,7},{5,4},{6,5},{7,6},{8,11},{9,8},{10,9... | collective-permute-start | bytes 589832 | tf_op jit(solution)/shard_map/ppermute | solution.py:261
  74.5 17.4 %collective-permute-start.3 = (bf16[8,80,128]{2,1,0:T(8,128)(2,1)S(1)}, bf16[8,80,128]{2,1,0:T(8,128)(2,1)S(1)}, u32[]{:S(2)}, u32[]{:S(2)}) collective-permute-start(bf16[8,80,128]{2,1,0:T(8,128)(2,1)S(1)} %sum_other.2), channel_id=1, source_target_pairs={{0,4},{1,5},{2,6},{3,7},{4,0},{5,1},{6,2},{7,3},{8,12},{9,13},{10,... | collective-permute-start | bytes 491528 | tf_op jit(solution)/shard_map/ppermute | solution.py:266
  83.1 8.8 %collective-permute-start.14 = (bf16[8,48,128]{2,1,0:T(8,128)(2,1)S(1)}, bf16[8,48,128]{2,1,0:T(8,128)(2,1)S(1)}, u32[]{:S(2)}, u32[]{:S(2)}) collective-permute-start(bf16[8,48,128]{2,1,0:T(8,128)(2,1)S(1)} %sum_other.3), channel_id=1, source_target_pairs={{0,4},{1,5},{2,6},{3,7},{4,0},{5,1},{6,2},{7,3},{8,12},{9,13},{10,... | collective-permute-start | bytes 294920 | tf_op jit(solution)/shard_map/ppermute | solution.py:266
  (3 other events, 2.0 us)

commit v5 on v4

--- a/solution.py
+++ b/solution.py
@@ -18,8 +18,15 @@
 N_PLANE = 4
 N_Y = 4
 N_CORE = 2
+PLANE = N_Y * N_CORE
 Q = 2
 PIECE = 16
+EARLY = 3
+HINT_CORE = 100000000000
+HINT_Y = 0
+HINT_PLANES = 0
+HINT_MID = 100000000000
+HINT_STEPPED = 100000000000
 CHUNKS = (80, 48)
 BF16 = jnp.bfloat16
 ANY = pl.BlockSpec(memory_space=pl.ANY)
@@ -42,8 +49,9 @@
 
 
 def col_kernel(row_ref, me_ref, order_ref, rank_ref, z_ref, w_ref, *refs):
-    straight_ref, out_refs = refs[0], refs[1 : 1 + N_CORE]
-    z_buf, w_buf, first_buf, sems = refs[1 + N_CORE :]
+    out_refs, (z_buf, w_buf, first_buf, sems) = refs[: 2 + N_CORE], refs[2 + N_CORE : 6 + N_CORE]
+    straight_buf, early_buf, *bufs = refs[6 + N_CORE : -1]
+    out_sems = refs[-1]
     early, late = [], []
     for g in range(PB // STEP):
         part = pl.ds(g * STEP, STEP)
@@ -64,15 +72,41 @@
     for copy in late:
         copy.wait()
     rows = CHUNKS[0]
-    for e in range(N_CORE):
-        for k in range(N_PLANE):
-            for m in range(N_Y):
+    outs = []
+
+    def send(buf, place, out_ref, start, count):
+        copy = pltpu.make_async_copy(
+            buf.at[pl.ds(place, count)], out_ref.at[pl.ds(start, count)], out_sems.at[len(outs)]
+        )
+        copy.start()
+        outs.append(copy)
+
+    for k in reversed(range(N_PLANE)):
+        for m in range(N_Y):
+            for e in range(N_CORE):
                 for i in range(Q):
+                    n = (m * N_CORE + e) * Q + i
                     place = (row_ref[0] ^ flip(k, m, e)) * Q + i
                     b = order_ref[place]
                     middle = masked_dot(first_buf[b], w_buf[1, b], rank_ref[1, b]).astype(BF16)
-                    straight_ref[place] = middle[:rows]
-                    out_refs[e][(k * N_Y + m) * Q + i] = middle[rows:]
+                    straight_buf[k * PIECE + near_place(row_ref, m, e) + i] = middle[:rows]
+                    if k == EARLY:
+                        early_buf[n] = middle[rows:]
+                    else:
+                        bufs[e][(k * N_Y + m) * Q + i] = middle[rows:]
+        start = ((row_ref[0] // PLANE) ^ k) * PIECE
+        send(straight_buf, k * PIECE, out_refs[0], start, PIECE)
+        if k == EARLY:
+            send(early_buf, 0, out_refs[1], 0, PIECE)
+        else:
+            for e in range(N_CORE):
+                send(bufs[e], k * N_Y * Q, out_refs[2 + e], k * N_Y * Q, N_Y * Q)
+    for copy in outs:
+        copy.wait()
+
+
+def near_place(row_ref, m, e):
+    return ((row_ref[0] % PLANE) ^ (m * N_CORE + e)) * Q
 
 
 def flip(k, m, e):
@@ -84,14 +118,20 @@
     return pl.pallas_call(
         col_kernel,
         out_shape=[jax.ShapeDtypeStruct((PB, straight, BW), BF16)]
-        + [jax.ShapeDtypeStruct((PB // N_CORE, stepped, BW), BF16)] * N_CORE,
+        + [jax.ShapeDtypeStruct((PIECE, stepped, BW), BF16)]
+        + [jax.ShapeDtypeStruct((EARLY * N_Y * Q, stepped, BW), BF16)] * N_CORE,
         in_specs=[SMEM, SMEM, SMEM, SMEM, ANY, ANY],
-        out_specs=[VMEM] * (1 + N_CORE),
+        out_specs=[ANY] * (2 + N_CORE),
         scratch_shapes=[
             pltpu.VMEM((PB, R, BW), BF16),
             pltpu.VMEM((2, PB, BW, BW), BF16),
             pltpu.VMEM((PB, R, BW), BF16),
             pltpu.SemaphoreType.DMA((3, PB // STEP)),
+            pltpu.VMEM((PB, straight, BW), BF16),
+            pltpu.VMEM((PIECE, stepped, BW), BF16),
+            pltpu.VMEM((EARLY * N_Y * Q, stepped, BW), BF16),
+            pltpu.VMEM((EARLY * N_Y * Q, stepped, BW), BF16),
+            pltpu.SemaphoreType.DMA((2 + EARLY * (1 + N_CORE),)),
         ],
         cost_estimate=pl.CostEstimate(
             flops=4 * PB * R * BW * BW, bytes_accessed=8 * 2**20, transcendentals=0
@@ -105,18 +145,38 @@
         refs[n_in + target][place : place + Q] = refs[source][start : start + Q]
 
 
-def regroup(rows, moves, n_out, pieces):
+def regroup(rows, moves, n_out, size, pieces, hint=0):
     return pl.pallas_call(
         functools.partial(regroup_kernel, moves, len(pieces)),
-        out_shape=[jax.ShapeDtypeStruct((PIECE, rows, BW), BF16)] * n_out,
+        out_shape=[jax.ShapeDtypeStruct((size, rows, BW), BF16)] * n_out,
         in_specs=[VMEM] * len(pieces),
         out_specs=[VMEM] * n_out,
         compiler_params=SMALL,
         cost_estimate=pl.CostEstimate(
-            flops=0, bytes_accessed=4 * n_out * PIECE * rows * BW, transcendentals=0
+            flops=hint, bytes_accessed=4 * n_out * size * rows * BW, transcendentals=0
         ),
         name="regroup",
     )(*pieces)
+
+
+def held(k, m, e):
+    if e == 1:
+        return 2, (k * N_Y + m) * Q
+    if k == EARLY:
+        return 1, m * N_CORE * Q
+    return 0, (k * N_Y + m) * Q
+
+
+def for_core():
+    moves = []
+    for k in range(N_PLANE):
+        for m in range(N_Y):
+            place = (k * N_Y + m) * Q
+            if k == EARLY:
+                moves.append((1, (m * N_CORE + 1) * Q, 0, place))
+            else:
+                moves.append((0, place, 0, place))
+    return moves
 
 
 def for_y():
@@ -124,7 +184,7 @@
     for m in range(1, N_Y):
         for e in range(N_CORE):
             for k in range(N_PLANE):
-                moves.append((e, (k * N_Y + m) * Q, m - 1, (e * N_PLANE + k) * Q))
+                moves.append((*held(k, m, e), m - 1, (e * N_PLANE + k) * Q))
     return moves
 
 
@@ -135,13 +195,13 @@
             for e in range(N_CORE):
                 place = (m * N_CORE + e) * Q
                 if m == 0:
-                    moves.append((e, k * N_Y * Q, k, place))
+                    moves.append((*held(k, m, e), k, place))
                 else:
-                    moves.append((N_CORE + m - 1, (e * N_PLANE + k) * Q, k, place))
+                    moves.append((2 + m, (e * N_PLANE + k) * Q, k, place))
     return moves
 
 
-def mid_kernel(offsets, me_ref, rank_ref, z_ref, w_ref, *out_refs):
+def mid_kernel(offsets, me_ref, rank_ref, z_ref, w_ref, after_ref, *out_refs):
     for d, out_ref in zip(offsets, out_refs):
         for h in range(N_Z):
             base = (h * N_X + lax.rem(me_ref[0] + d, N_X)) * STEP
@@ -150,22 +210,22 @@
                 out_ref[h * STEP + j] = inner.astype(BF16)
 
 
-def mid_level(rows, offsets, me, ranks, blocks, factors):
+def mid_level(rows, offsets, me, ranks, blocks, factors, after):
     n = len(offsets)
     count = n * N_Z * STEP
     return pl.pallas_call(
         functools.partial(mid_kernel, offsets),
         out_shape=[jax.ShapeDtypeStruct((N_Z * STEP, rows, BW), BF16)] * n,
-        in_specs=[SMEM, SMEM, VMEM, VMEM],
+        in_specs=[SMEM, SMEM, VMEM, VMEM, ANY],
         out_specs=[VMEM] * n,
         compiler_params=SMALL,
         cost_estimate=pl.CostEstimate(
-            flops=2 * count * rows * BW * BW,
+            flops=2 * count * rows * BW * BW + HINT_MID,
             bytes_accessed=count * (4 * rows + 2 * BW) * BW,
             transcendentals=0,
         ),
         name="mid_level",
-    )(me, ranks, blocks, factors)
+    )(me, ranks, blocks, factors, after)
 
 
 def stepped_kernel(row_ref, me_ref, rank_ref, w_ref, *refs):
@@ -192,7 +252,7 @@
         scratch_shapes=[pltpu.VMEM((PB, rows, BW), BF16)],
         compiler_params=SMALL,
         cost_estimate=pl.CostEstimate(
-            flops=2 * PB * rows * BW * BW,
+            flops=2 * PB * rows * BW * BW + HINT_STEPPED,
             bytes_accessed=PB * (4 * rows + 2 * BW) * BW,
             transcendentals=0,
         ),
@@ -279,19 +339,24 @@
     row = lax.axis_index("row").astype(jnp.int32).reshape(1)
     ranks, factors = mid_ranks[0], mid_factors[0]
     straight_rows, stepped_rows = CHUNKS
-    middle, same, other = col_levels(
+    middle, early, same, other = col_levels(
         row, me, block_order[0], col_ranks, right_sides, col_factors
     )
 
+    early = across_row(early, EARLY, 0, 0)
     regrouped = lax.all_to_all(middle, "row", split_axis=0, concat_axis=0, tiled=True)
 
-    cores = [same, across_row(other, 0, 0, 1)]
-    pieces = regroup(stepped_rows, for_y(), N_Y - 1, cores)
-    lines = [across_row(piece, 0, m + 1, 0) for m, piece in enumerate(pieces)]
-    pieces = regroup(stepped_rows, for_planes(), N_PLANE, cores + lines)
-    planes = [pieces[0]] + [across_row(pieces[k], k, 0, 0) for k in range(1, N_PLANE)]
-
-    inner = mid_level(straight_rows, (0, 1, 2, 3), me, ranks, regrouped, factors)
+    (other,) = regroup(
+        stepped_rows, for_core(), 1, PB // N_CORE, [other, early], HINT_CORE
+    )
+    pieces = [same, early, across_row(other, 0, 0, 1)]
+    lines = regroup(stepped_rows, for_y(), N_Y - 1, PIECE, pieces, HINT_Y)
+    pieces += [across_row(line, 0, m + 1, 0) for m, line in enumerate(lines)]
+    planes = list(regroup(stepped_rows, for_planes(), N_PLANE, PIECE, pieces, HINT_PLANES))
+    for k in range(1, EARLY):
+        planes[k] = across_row(planes[k], k, 0, 0)
+
+    inner = mid_level(straight_rows, (0, 1, 2, 3), me, ranks, regrouped, factors, planes[0])
     near = [inner[0]] + [around_x(inner[d], d) for d in (2, 1, 3)]
     parts = near + [across_z(sum_other(straight_rows, me, near))]
 

time: 93.8 us -> 92.2 us (0.983)
  the two profiles are of different devices: /device:TPU:8 before, /device:TPU:96 now
where the time goes in v5:
time: 92.2 us; the launch traced here: 92 us
  starting transfers between devices  43.2 us (47%)
  waiting for transfers between devices  36.5 us (40%)
  Pallas kernels  10.6 us (11%)
  local copies, waits for them, and re-layouts  1.62 us (2%)
    ppermute x7, waiting for transfers between devices, across_row(): lax.ppermute(value, 'row', [(r, r ^ flip(k, m, e)) for r in range(N_PLANE...  22 us
    ppermute x6, starting transfers between devices, around_x(): return lax.ppermute(value, 'col', pairs)  12.6 us
    ppermute x2, starting transfers between devices, across_z(): lax.ppermute(value, 'col', [(i, (i + half) % (2 * half)) for i in range(2...  11.7 us
    ppermute x7, starting transfers between devices, across_row(): lax.ppermute(value, 'row', [(r, r ^ flip(k, m, e)) for r in range(N_PLANE...  11.3 us
    ppermute x2, waiting for transfers between devices, across_z(): lax.ppermute(value, 'col', [(i, (i + half) % (2 * half)) for i in range(2...  8.74 us
    all_to_all x1, starting transfers between devices, shards(): lax.all_to_all(middle, 'row', split_axis=0, concat_axis=0, tiled=True)  7.56 us
    pallas_call x1, Pallas kernels, col_levels(): pl.pallas_call(col_kernel, out_shape=[jax.ShapeDtypeStruct((PB, straight,...  6.04 us
    ppermute x6, waiting for transfers between devices, around_x(): return lax.ppermute(value, 'col', pairs)  5.82 us
  transfers between devices with their start and end apart: 16, of which 8 were waited for; matrix products, arithmetic and copies ran while one was open for 0% of the time, Pallas kernels for 3%

profile of v5, /device:TPU:96, one launch (start us, length us, event | category | flops | bytes accessed | tf_op | source)
XLA Modules:
  0.0 92.0 jit_solution(14957883236154747609)
XLA Ops:
  0.0 6.0 %col_levels.1 = (bf16[64,80,128]{2,1,0:T(8,128)(2,1)}, bf16[16,48,128]{2,1,0:T(8,128)(2,1)}, bf16[24,48,128]{2,1,0:T(8,128)(2,1)}, bf16[24,48,128]{2,1,0:T(8,128)(2,1)}) custom-call(s32[1]{0:T(128)} %bitcast.2.row_ref, s32[1]{0:T(128)} %bitcast.me_ref, s32[64]{0:T(128)} %bitcast.9, s32[2,64]{1,0:T(2,128)} %rank_ref.2, bf16[64,128,128]{2,1,0:T(8,128)(2,1)} %z_ref.1, ...), custom_call_target="tpu_custom_call" | custom-call | flops 536870912 | bytes 8388608 | tf_op jit(solution)/shard_map/col_levels/pallas_call | solution.py:118
  6.1 1.0 %collective-permute-start = (bf16[16,48,128]{2,1,0:T(8,128)(2,1)}, bf16[16,48,128]{2,1,0:T(8,128)(2,1)S(1)}, u32[]{:S(2)}, u32[]{:S(2)}) collective-permute-start(bf16[16,48,128]{2,1,0:T(8,128)(2,1)} %get-tuple-element.26), channel_id=1, source_target_pairs={{0,192},{8,200},{16,208},{24,216},{32,224},{40,232},{48,240},{56,2... | collective-permute-start | bytes 589832 | tf_op jit(solution)/shard_map/ppermute | solution.py:330
  7.1 7.6 %all-to-all-start = ((bf16[64,80,128]{2,1,0:T(8,128)(2,1)}), bf16[64,80,128]{2,1,0:T(8,128)(2,1)S(1)}, u32[]{:S(2)}, u32[]{:S(2)}) async-start(bf16[64,80,128]{2,1,0:T(8,128)(2,1)} %get-tuple-element.24), calls=%async_computation | async-start | bytes 2621440 | tf_op jit(solution)/shard_map/all_to_all | solution.py:347
  15.0 1.7 %collective-permute-done.1.refs_2_ = bf16[32,48,128]{2,1,0:T(8,128)(2,1)S(1)} collective-permute-done((bf16[32,48,128]{2,1,0:T(8,128)(2,1)S(1)}, bf16[32,48,128]{2,1,0:T(8,128)(2,1)S(1)}, u32[]{:S(2)}, u32[]{:S(2)}) %collective-permute-start.1) | collective-permute-done | bytes 393248 | tf_op jit(solution)/shard_map/ppermute | solution.py:330
  16.8 1.7 %collective-permute-start.2 = (bf16[16,48,128]{2,1,0:T(8,128)(2,1)S(1)}, bf16[16,48,128]{2,1,0:T(8,128)(2,1)S(1)}, u32[]{:S(2)}, u32[]{:S(2)}) collective-permute-start(bf16[16,48,128]{2,1,0:T(8,128)(2,1)S(1)} %get-tuple-element.28), channel_id=1, source_target_pairs={{0,16},{8,24},{16,0},{24,8},{32,48},{40,56},{48,32},{56,40},{64,80... | collective-permute-start | bytes 589832 | tf_op jit(solution)/shard_map/ppermute | solution.py:330
  18.5 2.9 %collective-permute-start.3 = (bf16[16,48,128]{2,1,0:T(8,128)(2,1)S(1)}, bf16[16,48,128]{2,1,0:T(8,128)(2,1)S(1)}, u32[]{:S(2)}, u32[]{:S(2)}) collective-permute-start(bf16[16,48,128]{2,1,0:T(8,128)(2,1)S(1)} %get-tuple-element.29), channel_id=1, source_target_pairs={{0,32},{8,40},{16,48},{24,56},{32,0},{40,8},{48,16},{56,24},{64,96... | collective-permute-start | bytes 589832 | tf_op jit(solution)/shard_map/ppermute | solution.py:330
  21.6 10.8 %collective-permute-done.2.refs_3_ = bf16[16,48,128]{2,1,0:T(8,128)(2,1)S(1)} collective-permute-done((bf16[16,48,128]{2,1,0:T(8,128)(2,1)S(1)}, bf16[16,48,128]{2,1,0:T(8,128)(2,1)S(1)}, u32[]{:S(2)}, u32[]{:S(2)}) %collective-permute-start.2) | collective-permute-done | bytes 196640 | tf_op jit(solution)/shard_map/ppermute | solution.py:330
  32.4 7.2 %collective-permute-done.3.refs_4_ = bf16[16,48,128]{2,1,0:T(8,128)(2,1)S(1)} collective-permute-done((bf16[16,48,128]{2,1,0:T(8,128)(2,1)S(1)}, bf16[16,48,128]{2,1,0:T(8,128)(2,1)S(1)}, u32[]{:S(2)}, u32[]{:S(2)}) %collective-permute-start.3) | collective-permute-done | bytes 196640 | tf_op jit(solution)/shard_map/ppermute | solution.py:330
  39.7 5.4 %collective-permute-start.9 = (bf16[16,48,128]{2,1,0:T(8,128)(2,1)S(1)}, bf16[16,48,128]{2,1,0:T(8,128)(2,1)S(1)}, u32[]{:S(2)}, u32[]{:S(2)}) collective-permute-start(bf16[16,48,128]{2,1,0:T(8,128)(2,1)S(1)} %get-tuple-element.36), channel_id=1, source_target_pairs={{0,64},{8,72},{16,80},{24,88},{32,96},{40,104},{48,112},{56,120},{... | collective-permute-start | bytes 589832 | tf_op jit(solution)/shard_map/ppermute | solution.py:330
  45.1 1.6 %copy-done.3 = bf16[1,64,128,128]{3,2,1,0:T(8,128)(2,1)S(1)} copy-done((bf16[1,64,128,128]{3,2,1,0:T(8,128)(2,1)S(1)}, bf16[1,64,128,128]{3,2,1,0:T(8,128)(2,1)}, u32[]{:S(2)}) %copy-start.3) | copy-done | bytes 2097176
  46.7 1.4 %mid_level.1 = (bf16[16,80,128]{2,1,0:T(8,128)(2,1)S(1)}, bf16[16,80,128]{2,1,0:T(8,128)(2,1)S(1)}, bf16[16,80,128]{2,1,0:T(8,128)(2,1)S(1)}, bf16[16,80,128]{2,1,0:T(8,128)(2,1)S(1)}) custom-call(s32[1]{0:T(128)} %bitcast.me_ref, s32[64]{0:T(128)S(1)} %bitcast.7, bf16[64,80,128]{2,1,0:T(8,128)(2,1)S(1)} %all-to-all-done.z_ref, ...), custom_call_target="tpu_custom_call" | custom-call | flops 100167770112 | bytes 4718592 | tf_op jit(solution)/shard_map/mid_level/pallas_call | solution.py:216
  48.1 3.1 %collective-permute-start.5 = (bf16[16,80,128]{2,1,0:T(8,128)(2,1)S(1)}, bf16[16,80,128]{2,1,0:T(8,128)(2,1)S(1)}, u32[]{:S(2)}, u32[]{:S(2)}) collective-permute-start(bf16[16,80,128]{2,1,0:T(8,128)(2,1)S(1)} %get-tuple-element.33), channel_id=1, source_target_pairs={{0,2},{1,3},{2,0},{3,1},{4,6},{5,7},{6,4},{7,5},{8,10},{9,11},{10,... | collective-permute-start | bytes 983048 | tf_op jit(solution)/shard_map/ppermute | solution.py:321
  51.8 2.6 %collective-permute-start.7 = (bf16[16,80,128]{2,1,0:T(8,128)(2,1)S(1)}, bf16[16,80,128]{2,1,0:T(8,128)(2,1)S(1)}, u32[]{:S(2)}, u32[]{:S(2)}) collective-permute-start(bf16[16,80,128]{2,1,0:T(8,128)(2,1)S(1)} %get-tuple-element.35), channel_id=1, source_target_pairs={{0,3},{1,0},{2,1},{3,2},{4,7},{5,4},{6,5},{7,6},{8,11},{9,8},{10,9... | collective-permute-start | bytes 983048 | tf_op jit(solution)/shard_map/ppermute | solution.py:321
  54.4 1.9 %collective-permute-done.10.refs_2_ = bf16[16,48,128]{2,1,0:T(8,128)(2,1)S(1)} collective-permute-done((bf16[16,48,128]{2,1,0:T(8,128)(2,1)S(1)}, bf16[16,48,128]{2,1,0:T(8,128)(2,1)S(1)}, u32[]{:S(2)}, u32[]{:S(2)}) %collective-permute-start.10) | collective-permute-done | bytes 196640 | tf_op jit(solution)/shard_map/ppermute | solution.py:330
  56.3 1.3 %mid_stepped.1 = (bf16[16,48,128]{2,1,0:T(8,128)(2,1)S(1)}, bf16[16,48,128]{2,1,0:T(8,128)(2,1)S(1)}, bf16[16,48,128]{2,1,0:T(8,128)(2,1)S(1)}, bf16[16,48,128]{2,1,0:T(8,128)(2,1)S(1)}) custom-call(s32[1]{0:T(128)} %bitcast.2.row_ref, s32[1]{0:T(128)} %bitcast.me_ref, s32[64]{0:T(128)S(1)} %bitcast.8, bf16[64,128,128]{2,1,0:T(8,128)(2,1)S(1)} %bitcast.6, ...), custom_call_target="tpu_custom_call" | custom-call | flops 100100661248 | bytes 3670016 | tf_op jit(solution)/shard_map/mid_stepped/pallas_call | solution.py:247
  57.6 3.1 %collective-permute-start.11 = (bf16[16,48,128]{2,1,0:T(8,128)(2,1)S(1)}, bf16[16,48,128]{2,1,0:T(8,128)(2,1)S(1)}, u32[]{:S(2)}, u32[]{:S(2)}) collective-permute-start(bf16[16,48,128]{2,1,0:T(8,128)(2,1)S(1)} %get-tuple-element.40), channel_id=1, source_target_pairs={{0,2},{1,3},{2,0},{3,1},{4,6},{5,7},{6,4},{7,5},{8,10},{9,11},{10,... | collective-permute-start | bytes 589832 | tf_op jit(solution)/shard_map/ppermute | solution.py:321
  60.7 0.6 collective-permute-start.12
  61.4 2.6 %collective-permute-start.13 = (bf16[16,48,128]{2,1,0:T(8,128)(2,1)S(1)}, bf16[16,48,128]{2,1,0:T(8,128)(2,1)S(1)}, u32[]{:S(2)}, u32[]{:S(2)}) collective-permute-start(bf16[16,48,128]{2,1,0:T(8,128)(2,1)S(1)} %get-tuple-element.42), channel_id=1, source_target_pairs={{0,3},{1,0},{2,1},{3,2},{4,7},{5,4},{6,5},{7,6},{8,11},{9,8},{10,9... | collective-permute-start | bytes 589832 | tf_op jit(solution)/shard_map/ppermute | solution.py:321
  64.0 3.5 %collective-permute-done.6.refs_2_ = bf16[16,80,128]{2,1,0:T(8,128)(2,1)S(1)} collective-permute-done((bf16[16,80,128]{2,1,0:T(8,128)(2,1)S(1)}, bf16[16,80,128]{2,1,0:T(8,128)(2,1)S(1)}, u32[]{:S(2)}, u32[]{:S(2)}) %collective-permute-start.6) | collective-permute-done | bytes 327712 | tf_op jit(solution)/shard_map/ppermute | solution.py:321
  67.5 5.8 %collective-permute-start.8 = (bf16[8,80,128]{2,1,0:T(8,128)(2,1)S(1)}, bf16[8,80,128]{2,1,0:T(8,128)(2,1)S(1)}, u32[]{:S(2)}, u32[]{:S(2)}) collective-permute-start(bf16[8,80,128]{2,1,0:T(8,128)(2,1)S(1)} %sum_other.2), channel_id=1, source_target_pairs={{0,4},{1,5},{2,6},{3,7},{4,0},{5,1},{6,2},{7,3},{8,12},{9,13},{10,... | collective-permute-start | bytes 491528 | tf_op jit(solution)/shard_map/ppermute | solution.py:326
  73.3 2.3 %collective-permute-done.12.refs_2_.refs_7_ = bf16[16,48,128]{2,1,0:T(8,128)(2,1)S(1)} collective-permute-done((bf16[16,48,128]{2,1,0:T(8,128)(2,1)S(1)}, bf16[16,48,128]{2,1,0:T(8,128)(2,1)S(1)}, u32[]{:S(2)}, u32[]{:S(2)}) %collective-permute-start.12) | collective-permute-done | bytes 196640 | tf_op jit(solution)/shard_map/ppermute | solution.py:321
  75.7 5.9 %collective-permute-start.14 = (bf16[8,48,128]{2,1,0:T(8,128)(2,1)S(1)}, bf16[8,48,128]{2,1,0:T(8,128)(2,1)S(1)}, u32[]{:S(2)}, u32[]{:S(2)}) collective-permute-start(bf16[8,48,128]{2,1,0:T(8,128)(2,1)S(1)} %sum_other.3), channel_id=1, source_target_pairs={{0,4},{1,5},{2,6},{3,7},{4,0},{5,1},{6,2},{7,3},{8,12},{9,13},{10,... | collective-permute-start | bytes 294920 | tf_op jit(solution)/shard_map/ppermute | solution.py:326
  81.6 8.7 %collective-permute-done.14.refs_9_ = bf16[8,48,128]{2,1,0:T(8,128)(2,1)S(1)} collective-permute-done((bf16[8,48,128]{2,1,0:T(8,128)(2,1)S(1)}, bf16[8,48,128]{2,1,0:T(8,128)(2,1)S(1)}, u32[]{:S(2)}, u32[]{:S(2)}) %collective-permute-start.14) | collective-permute-done | bytes 98336 | tf_op jit(solution)/shard_map/ppermute | solution.py:326
  90.4 1.7 %row_level.1 = bf16[8,128,128]{2,1,0:T(8,128)(2,1)} custom-call(s32[1]{0:T(128)} %bitcast.me_ref, s32[64]{0:T(128)S(1)} %copy-done.2, bf16[64,128,128]{2,1,0:T(8,128)(2,1)S(1)} %copy-done, bf16[16,80,128]{2,1,0:T(8,128)(2,1)S(1)} %get-tuple-element.32.refs_0_, bf16[16,80,128]{2,1,0:T(8,128)(2,1)S(1)} %collective-permute-done.5.refs_1_, ...), custom_call_target="tpu_custom_call" | custom-call | flops 33554432 | bytes 1048576 | tf_op jit(solution)/shard_map/row_level/pallas_call | solution.py:306
  (31 shorter events, 1.5 us)
Async XLA Ops:
  6.0 8.9 %copy-start.5 = (bf16[24,48,128]{2,1,0:T(8,128)(2,1)S(1)}, bf16[24,48,128]{2,1,0:T(8,128)(2,1)}, u32[]{:S(2)}) copy-start(bf16[24,48,128]{2,1,0:T(8,128)(2,1)} %get-tuple-element.27.refs_0_) | copy-start | bytes 884740
  6.1 8.8 %collective-permute-start = (bf16[16,48,128]{2,1,0:T(8,128)(2,1)}, bf16[16,48,128]{2,1,0:T(8,128)(2,1)S(1)}, u32[]{:S(2)}, u32[]{:S(2)}) collective-permute-start(bf16[16,48,128]{2,1,0:T(8,128)(2,1)} %get-tuple-element.26), channel_id=1, source_target_pairs={{0,192},{8,200},{16,208},{24,216},{32,224},{40,232},{48,240},{56,2... | collective-permute-start | bytes 589832 | tf_op jit(solution)/shard_map/ppermute | solution.py:330
  7.1 38.0 %all-to-all-start = ((bf16[64,80,128]{2,1,0:T(8,128)(2,1)}), bf16[64,80,128]{2,1,0:T(8,128)(2,1)S(1)}, u32[]{:S(2)}, u32[]{:S(2)}) async-start(bf16[64,80,128]{2,1,0:T(8,128)(2,1)} %get-tuple-element.24), calls=%async_computation | async-start | bytes 2621440 | tf_op jit(solution)/shard_map/all_to_all | solution.py:347
  14.9 1.9 %copy-start.1 = (bf16[24,48,128]{2,1,0:T(8,128)(2,1)S(1)}, bf16[24,48,128]{2,1,0:T(8,128)(2,1)}, u32[]{:S(2)}) copy-start(bf16[24,48,128]{2,1,0:T(8,128)(2,1)} %get-tuple-element.25.refs_0_) | copy-start | bytes 884740
  14.9 30.1 %copy-start.6 = (s32[1,64]{1,0:T(1,128)S(1)}, s32[1,64]{1,0:T(1,128)}, u32[]{:S(2)}) copy-start(s32[1,64]{1,0:T(1,128)} %param.13) | copy-start | bytes 772
  14.9 1.8 %collective-permute-start.1 = (bf16[32,48,128]{2,1,0:T(8,128)(2,1)S(1)}, bf16[32,48,128]{2,1,0:T(8,128)(2,1)S(1)}, u32[]{:S(2)}, u32[]{:S(2)}) collective-permute-start(bf16[32,48,128]{2,1,0:T(8,128)(2,1)S(1)} %regroup.3), channel_id=1, source_target_pairs={{0,8},{8,0},{16,24},{24,16},{32,40},{40,32},{48,56},{56,48},{64,72... | collective-permute-start | bytes 1179656 | tf_op jit(solution)/shard_map/ppermute | solution.py:330
  16.8 15.6 %collective-permute-start.2 = (bf16[16,48,128]{2,1,0:T(8,128)(2,1)S(1)}, bf16[16,48,128]{2,1,0:T(8,128)(2,1)S(1)}, u32[]{:S(2)}, u32[]{:S(2)}) collective-permute-start(bf16[16,48,128]{2,1,0:T(8,128)(2,1)S(1)} %get-tuple-element.28), channel_id=1, source_target_pairs={{0,16},{8,24},{16,0},{24,8},{32,48},{40,56},{48,32},{56,40},{64,80... | collective-permute-start | bytes 589832 | tf_op jit(solution)/shard_map/ppermute | solution.py:330
  18.5 21.2 %collective-permute-start.3 = (bf16[16,48,128]{2,1,0:T(8,128)(2,1)S(1)}, bf16[16,48,128]{2,1,0:T(8,128)(2,1)S(1)}, u32[]{:S(2)}, u32[]{:S(2)}) collective-permute-start(bf16[16,48,128]{2,1,0:T(8,128)(2,1)S(1)} %get-tuple-element.29), channel_id=1, source_target_pairs={{0,32},{8,40},{16,48},{24,56},{32,0},{40,8},{48,16},{56,24},{64,96... | collective-permute-start | bytes 589832 | tf_op jit(solution)/shard_map/ppermute | solution.py:330
  21.4 18.3 %collective-permute-start.4 = (bf16[16,48,128]{2,1,0:T(8,128)(2,1)S(1)}, bf16[16,48,128]{2,1,0:T(8,128)(2,1)S(1)}, u32[]{:S(2)}, u32[]{:S(2)}) collective-permute-start(bf16[16,48,128]{2,1,0:T(8,128)(2,1)S(1)} %get-tuple-element.30), channel_id=1, source_target_pairs={{0,48},{8,56},{16,32},{24,40},{32,16},{40,24},{48,0},{56,8},{64,11... | collective-permute-start | bytes 589832 | tf_op jit(solution)/shard_map/ppermute | solution.py:330
  39.7 14.7 %collective-permute-start.9 = (bf16[16,48,128]{2,1,0:T(8,128)(2,1)S(1)}, bf16[16,48,128]{2,1,0:T(8,128)(2,1)S(1)}, u32[]{:S(2)}, u32[]{:S(2)}) collective-permute-start(bf16[16,48,128]{2,1,0:T(8,128)(2,1)S(1)} %get-tuple-element.36), channel_id=1, source_target_pairs={{0,64},{8,72},{16,80},{24,88},{32,96},{40,104},{48,112},{56,120},{... | collective-permute-start | bytes 589832 | tf_op jit(solution)/shard_map/ppermute | solution.py:330
  45.1 11.3 %collective-permute-start.10 = (bf16[16,48,128]{2,1,0:T(8,128)(2,1)S(1)}, bf16[16,48,128]{2,1,0:T(8,128)(2,1)S(1)}, u32[]{:S(2)}, u32[]{:S(2)}) collective-permute-start(bf16[16,48,128]{2,1,0:T(8,128)(2,1)S(1)} %get-tuple-element.37), channel_id=1, source_target_pairs={{0,128},{8,136},{16,144},{24,152},{32,160},{40,168},{48,176},{56,1... | collective-permute-start | bytes 589832 | tf_op jit(solution)/shard_map/ppermute | solution.py:330
  45.1 1.6 %copy-start.3 = (bf16[1,64,128,128]{3,2,1,0:T(8,128)(2,1)S(1)}, bf16[1,64,128,128]{3,2,1,0:T(8,128)(2,1)}, u32[]{:S(2)}) copy-start(bf16[1,64,128,128]{3,2,1,0:T(8,128)(2,1)} %param.12) | copy-start | bytes 6291460
  46.7 9.7 %copy-start.4 = (bf16[1,64,128,128]{3,2,1,0:T(8,128)(2,1)S(1)}, bf16[1,64,128,128]{3,2,1,0:T(8,128)(2,1)}, u32[]{:S(2)}) copy-start(bf16[1,64,128,128]{3,2,1,0:T(8,128)(2,1)} %param.12) | copy-start | bytes 6291460
  48.1 13.3 %collective-permute-start.5 = (bf16[16,80,128]{2,1,0:T(8,128)(2,1)S(1)}, bf16[16,80,128]{2,1,0:T(8,128)(2,1)S(1)}, u32[]{:S(2)}, u32[]{:S(2)}) collective-permute-start(bf16[16,80,128]{2,1,0:T(8,128)(2,1)S(1)} %get-tuple-element.33), channel_id=1, source_target_pairs={{0,2},{1,3},{2,0},{3,1},{4,6},{5,7},{6,4},{7,5},{8,10},{9,11},{10,... | collective-permute-start | bytes 983048 | tf_op jit(solution)/shard_map/ppermute | solution.py:321
  51.1 16.3 %collective-permute-start.6 = (bf16[16,80,128]{2,1,0:T(8,128)(2,1)S(1)}, bf16[16,80,128]{2,1,0:T(8,128)(2,1)S(1)}, u32[]{:S(2)}, u32[]{:S(2)}) collective-permute-start(bf16[16,80,128]{2,1,0:T(8,128)(2,1)S(1)} %get-tuple-element.34), channel_id=1, source_target_pairs={{0,1},{1,2},{2,3},{3,0},{4,5},{5,6},{6,7},{7,4},{8,9},{9,10},{10,1... | collective-permute-start | bytes 983048 | tf_op jit(solution)/shard_map/ppermute | solution.py:321
  51.8 15.7 %collective-permute-start.7 = (bf16[16,80,128]{2,1,0:T(8,128)(2,1)S(1)}, bf16[16,80,128]{2,1,0:T(8,128)(2,1)S(1)}, u32[]{:S(2)}, u32[]{:S(2)}) collective-permute-start(bf16[16,80,128]{2,1,0:T(8,128)(2,1)S(1)} %get-tuple-element.35), channel_id=1, source_target_pairs={{0,3},{1,0},{2,1},{3,2},{4,7},{5,4},{6,5},{7,6},{8,11},{9,8},{10,9... | collective-permute-start | bytes 983048 | tf_op jit(solution)/shard_map/ppermute | solution.py:321
  57.6 32.7 %copy-start = (bf16[64,128,128]{2,1,0:T(8,128)(2,1)S(1)}, bf16[64,128,128]{2,1,0:T(8,128)(2,1)}, u32[]{:S(2)}) copy-start(bf16[64,128,128]{2,1,0:T(8,128)(2,1)} %w_ref.3) | copy-start | bytes 6291460
  57.6 32.7 %copy-start.2 = (s32[64]{0:T(128)S(1)}, s32[64]{0:T(128)}, u32[]{:S(2)}) copy-start(s32[64]{0:T(128)} %rank_ref.3) | copy-start | bytes 772
  57.6 15.7 %collective-permute-start.11 = (bf16[16,48,128]{2,1,0:T(8,128)(2,1)S(1)}, bf16[16,48,128]{2,1,0:T(8,128)(2,1)S(1)}, u32[]{:S(2)}, u32[]{:S(2)}) collective-permute-start(bf16[16,48,128]{2,1,0:T(8,128)(2,1)S(1)} %get-tuple-element.40), channel_id=1, source_target_pairs={{0,2},{1,3},{2,0},{3,1},{4,6},{5,7},{6,4},{7,5},{8,10},{9,11},{10,... | collective-permute-start | bytes 589832 | tf_op jit(solution)/shard_map/ppermute | solution.py:321
  60.7 15.0 %collective-permute-start.12 = (bf16[16,48,128]{2,1,0:T(8,128)(2,1)S(1)}, bf16[16,48,128]{2,1,0:T(8,128)(2,1)S(1)}, u32[]{:S(2)}, u32[]{:S(2)}) collective-permute-start(bf16[16,48,128]{2,1,0:T(8,128)(2,1)S(1)} %get-tuple-element.41), channel_id=1, source_target_pairs={{0,1},{1,2},{2,3},{3,0},{4,5},{5,6},{6,7},{7,4},{8,9},{9,10},{10,1... | collective-permute-start | bytes 589832 | tf_op jit(solution)/shard_map/ppermute | solution.py:321
  61.4 14.3 %collective-permute-start.13 = (bf16[16,48,128]{2,1,0:T(8,128)(2,1)S(1)}, bf16[16,48,128]{2,1,0:T(8,128)(2,1)S(1)}, u32[]{:S(2)}, u32[]{:S(2)}) collective-permute-start(bf16[16,48,128]{2,1,0:T(8,128)(2,1)S(1)} %get-tuple-element.42), channel_id=1, source_target_pairs={{0,3},{1,0},{2,1},{3,2},{4,7},{5,4},{6,5},{7,6},{8,11},{9,8},{10,9... | collective-permute-start | bytes 589832 | tf_op jit(solution)/shard_map/ppermute | solution.py:321
  67.5 22.8 %collective-permute-start.8 = (bf16[8,80,128]{2,1,0:T(8,128)(2,1)S(1)}, bf16[8,80,128]{2,1,0:T(8,128)(2,1)S(1)}, u32[]{:S(2)}, u32[]{:S(2)}) collective-permute-start(bf16[8,80,128]{2,1,0:T(8,128)(2,1)S(1)} %sum_other.2), channel_id=1, source_target_pairs={{0,4},{1,5},{2,6},{3,7},{4,0},{5,1},{6,2},{7,3},{8,12},{9,13},{10,... | collective-permute-start | bytes 491528 | tf_op jit(solution)/shard_map/ppermute | solution.py:326
  75.7 14.6 %collective-permute-start.14 = (bf16[8,48,128]{2,1,0:T(8,128)(2,1)S(1)}, bf16[8,48,128]{2,1,0:T(8,128)(2,1)S(1)}, u32[]{:S(2)}, u32[]{:S(2)}) collective-permute-start(bf16[8,48,128]{2,1,0:T(8,128)(2,1)S(1)} %sum_other.3), channel_id=1, source_target_pairs={{0,4},{1,5},{2,6},{3,7},{4,0},{5,1},{6,2},{7,3},{8,12},{9,13},{10,... | collective-permute-start | bytes 294920 | tf_op jit(solution)/shard_map/ppermute | solution.py:326

commit v6 on v5

--- a/solution.py
+++ b/solution.py
@@ -12,6 +12,7 @@
 R = 128
 PB = 64
 STEP = 8
+SIDE = STEP // 2
 N_X = 4
 N_Z = 2
 OWN = 8
@@ -26,6 +27,7 @@
 HINT_Y = 0
 HINT_PLANES = 0
 HINT_MID = 100000000000
+HINT_JOIN = 0
 HINT_STEPPED = 100000000000
 CHUNKS = (80, 48)
 BF16 = jnp.bfloat16
@@ -201,31 +203,65 @@
     return moves
 
 
-def mid_kernel(offsets, me_ref, rank_ref, z_ref, w_ref, after_ref, *out_refs):
-    for d, out_ref in zip(offsets, out_refs):
+def mid_kernel(me_ref, rank_ref, z_ref, w_ref, after_ref, *out_refs):
+    for d in (2, 1, 3, 0):
         for h in range(N_Z):
             base = (h * N_X + lax.rem(me_ref[0] + d, N_X)) * STEP
             for j in range(STEP):
                 inner = masked_dot(z_ref[base + j], w_ref[base + j], rank_ref[base + j])
-                out_ref[h * STEP + j] = inner.astype(BF16)
-
-
-def mid_level(rows, offsets, me, ranks, blocks, factors, after):
-    n = len(offsets)
-    count = n * N_Z * STEP
-    return pl.pallas_call(
-        functools.partial(mid_kernel, offsets),
-        out_shape=[jax.ShapeDtypeStruct((N_Z * STEP, rows, BW), BF16)] * n,
+                if d == 2:
+                    out_refs[2 + j // SIDE][h * SIDE + j % SIDE] = inner.astype(BF16)
+                else:
+                    out_refs[d if d < 2 else 4][h * STEP + j] = inner.astype(BF16)
+
+
+def mid_level(rows, me, ranks, blocks, factors, after):
+    whole = jax.ShapeDtypeStruct((N_Z * STEP, rows, BW), BF16)
+    side = jax.ShapeDtypeStruct((N_Z * SIDE, rows, BW), BF16)
+    return pl.pallas_call(
+        mid_kernel,
+        out_shape=[whole, whole, side, side, whole],
         in_specs=[SMEM, SMEM, VMEM, VMEM, ANY],
-        out_specs=[VMEM] * n,
-        compiler_params=SMALL,
-        cost_estimate=pl.CostEstimate(
-            flops=2 * count * rows * BW * BW + HINT_MID,
-            bytes_accessed=count * (4 * rows + 2 * BW) * BW,
+        out_specs=[VMEM] * 5,
+        compiler_params=SMALL,
+        cost_estimate=pl.CostEstimate(
+            flops=2 * PB * rows * BW * BW + HINT_MID,
+            bytes_accessed=PB * (4 * rows + 2 * BW) * BW,
             transcendentals=0,
         ),
         name="mid_level",
     )(me, ranks, blocks, factors, after)
+
+
+def join_kernel(right_ref, left_ref, from_left_ref, from_right_ref, right_out, left_out):
+    for h in range(N_Z):
+        a, b = h * STEP, h * STEP + SIDE
+        sides = slice(h * SIDE, (h + 1) * SIDE)
+        first, second = slice(a, a + SIDE), slice(b, b + SIDE)
+        right_out[first] = added(right_ref[first], from_left_ref[sides])
+        right_out[second] = right_ref[second]
+        left_out[first] = left_ref[first]
+        left_out[second] = added(left_ref[second], from_right_ref[sides])
+
+
+def added(a, b):
+    return (a.astype(jnp.float32) + b.astype(jnp.float32)).astype(BF16)
+
+
+def join_sides(rows, right, left, from_left, from_right):
+    return pl.pallas_call(
+        join_kernel,
+        out_shape=[jax.ShapeDtypeStruct((N_Z * STEP, rows, BW), BF16)] * 2,
+        in_specs=[VMEM] * 4,
+        out_specs=[VMEM] * 2,
+        compiler_params=SMALL,
+        cost_estimate=pl.CostEstimate(
+            flops=STEP * rows * BW + HINT_JOIN,
+            bytes_accessed=12 * N_Z * STEP * rows * BW,
+            transcendentals=0,
+        ),
+        name="join_sides",
+    )(right, left, from_left, from_right)
 
 
 def stepped_kernel(row_ref, me_ref, rank_ref, w_ref, *refs):
@@ -269,14 +305,14 @@
 
 def sum_kernel(me_ref, *refs):
     half = pl.ds((1 - lax.div(me_ref[0], N_X)) * STEP, STEP)
-    refs[N_X][...] = total_of(refs[:N_X], half).astype(BF16)
+    refs[-1][...] = total_of(refs[:-1], half).astype(BF16)
 
 
 def sum_other(rows, me, parts):
     return pl.pallas_call(
         sum_kernel,
         out_shape=jax.ShapeDtypeStruct((STEP, rows, BW), BF16),
-        in_specs=[SMEM] + [VMEM] * N_X,
+        in_specs=[SMEM] + [VMEM] * len(parts),
         out_specs=VMEM,
         compiler_params=SMALL,
         cost_estimate=pl.CostEstimate(
@@ -291,9 +327,10 @@
     base = me_ref[0] * OWN
     half = pl.ds(lax.div(me_ref[0], N_X) * STEP, STEP)
     start = 0
-    for n, rows in enumerate(CHUNKS):
-        near = refs[n * (N_X + 1) : n * (N_X + 1) + N_X]
-        far = refs[n * (N_X + 1) + N_X]
+    for rows, near, far in (
+        (CHUNKS[0], refs[:3], refs[3]),
+        (CHUNKS[1], refs[4 : 4 + N_X], refs[4 + N_X]),
+    ):
         total = total_of(near, half) + far[...].astype(jnp.float32)
         for j in range(0, OWN, 2):
             for i, block in enumerate(pair(total[j], total[j + 1])):
@@ -356,8 +393,12 @@
     for k in range(1, EARLY):
         planes[k] = across_row(planes[k], k, 0, 0)
 
-    inner = mid_level(straight_rows, (0, 1, 2, 3), me, ranks, regrouped, factors, planes[0])
-    near = [inner[0]] + [around_x(inner[d], d) for d in (2, 1, 3)]
+    own, right, first, second, left = mid_level(
+        straight_rows, me, ranks, regrouped, factors, planes[0]
+    )
+    from_left, from_right = around_x(first, 1), around_x(second, 3)
+    right, left = join_sides(straight_rows, right, left, from_left, from_right)
+    near = [own, around_x(right, 1), around_x(left, 3)]
     parts = near + [across_z(sum_other(straight_rows, me, near))]
 
     inner = mid_stepped(stepped_rows, row, me, ranks, factors, planes)

time: 92.2 us -> 92.1 us (level)
  the two profiles are of different devices: /device:TPU:96 before, /device:TPU:102 now
where the time goes in v6:
time: 92.1 us; the launch traced here: 91.9 us
  waiting for transfers between devices  44.1 us (48%)
  starting transfers between devices  35.3 us (38%)
  Pallas kernels  10.7 us (12%)
  local copies, waits for them, and re-layouts  1.62 us (2%)
    ppermute x7, waiting for transfers between devices, across_row(): lax.ppermute(value, 'row', [(r, r ^ flip(k, m, e)) for r in range(N_PLANE...  20 us
    ppermute x7, waiting for transfers between devices, around_x(): return lax.ppermute(value, 'col', pairs)  16.1 us
    ppermute x7, starting transfers between devices, across_row(): lax.ppermute(value, 'row', [(r, r ^ flip(k, m, e)) for r in range(N_PLANE...  10.3 us
    ppermute x2, starting transfers between devices, across_z(): lax.ppermute(value, 'col', [(i, (i + half) % (2 * half)) for i in range(2...  8.75 us
    all_to_all x1, starting transfers between devices, shards(): lax.all_to_all(middle, 'row', split_axis=0, concat_axis=0, tiled=True)  8.48 us
    ppermute x2, waiting for transfers between devices, across_z(): lax.ppermute(value, 'col', [(i, (i + half) % (2 * half)) for i in range(2...  7.98 us
    ppermute x7, starting transfers between devices, around_x(): return lax.ppermute(value, 'col', pairs)  7.7 us
    pallas_call x1, Pallas kernels, col_levels(): pl.pallas_call(col_kernel, out_shape=[jax.ShapeDtypeStruct((PB, straight,...  6.03 us
  transfers between devices with their start and end apart: 17, of which 9 were waited for; matrix products, arithmetic and copies ran while one was open for 0% of the time, Pallas kernels for 3%

profile of v6, /device:TPU:102, one launch (start us, length us, event | category | flops | bytes accessed | tf_op | source)
XLA Modules:
  0.0 91.9 jit_solution(17284951282199297677)
XLA Ops:
  0.0 6.0 %col_levels.1 = (bf16[64,80,128]{2,1,0:T(8,128)(2,1)}, bf16[16,48,128]{2,1,0:T(8,128)(2,1)}, bf16[24,48,128]{2,1,0:T(8,128)(2,1)}, bf16[24,48,128]{2,1,0:T(8,128)(2,1)}) custom-call(s32[1]{0:T(128)} %bitcast.2.row_ref, s32[1]{0:T(128)} %bitcast.me_ref, s32[64]{0:T(128)} %bitcast.9, s32[2,64]{1,0:T(2,128)} %rank_ref.2, bf16[64,128,128]{2,1,0:T(8,128)(2,1)} %z_ref.1, ...), custom_call_target="tpu_custom_call" | custom-call | flops 536870912 | bytes 8388608 | tf_op jit(solution)/shard_map/col_levels/pallas_call | solution.py:120
  6.2 8.5 %all-to-all-start = ((bf16[64,80,128]{2,1,0:T(8,128)(2,1)}), bf16[64,80,128]{2,1,0:T(8,128)(2,1)S(1)}, u32[]{:S(2)}, u32[]{:S(2)}) async-start(bf16[64,80,128]{2,1,0:T(8,128)(2,1)} %get-tuple-element.27), calls=%async_computation | async-start | bytes 2621440 | tf_op jit(solution)/shard_map/all_to_all | solution.py:384
  15.0 1.7 %collective-permute-done.1.refs_2_ = bf16[32,48,128]{2,1,0:T(8,128)(2,1)S(1)} collective-permute-done((bf16[32,48,128]{2,1,0:T(8,128)(2,1)S(1)}, bf16[32,48,128]{2,1,0:T(8,128)(2,1)S(1)}, u32[]{:S(2)}, u32[]{:S(2)}) %collective-permute-start.1) | collective-permute-done | bytes 393248 | tf_op jit(solution)/shard_map/ppermute | solution.py:367
  16.8 1.7 %collective-permute-start.2 = (bf16[16,48,128]{2,1,0:T(8,128)(2,1)S(1)}, bf16[16,48,128]{2,1,0:T(8,128)(2,1)S(1)}, u32[]{:S(2)}, u32[]{:S(2)}) collective-permute-start(bf16[16,48,128]{2,1,0:T(8,128)(2,1)S(1)} %get-tuple-element.31), channel_id=1, source_target_pairs={{0,16},{8,24},{16,0},{24,8},{32,48},{40,56},{48,32},{56,40},{64,80... | collective-permute-start | bytes 589832 | tf_op jit(solution)/shard_map/ppermute | solution.py:367
  18.5 2.9 %collective-permute-start.3 = (bf16[16,48,128]{2,1,0:T(8,128)(2,1)S(1)}, bf16[16,48,128]{2,1,0:T(8,128)(2,1)S(1)}, u32[]{:S(2)}, u32[]{:S(2)}) collective-permute-start(bf16[16,48,128]{2,1,0:T(8,128)(2,1)S(1)} %get-tuple-element.32), channel_id=1, source_target_pairs={{0,32},{8,40},{16,48},{24,56},{32,0},{40,8},{48,16},{56,24},{64,96... | collective-permute-start | bytes 589832 | tf_op jit(solution)/shard_map/ppermute | solution.py:367
  21.6 10.8 %collective-permute-done.2.refs_3_ = bf16[16,48,128]{2,1,0:T(8,128)(2,1)S(1)} collective-permute-done((bf16[16,48,128]{2,1,0:T(8,128)(2,1)S(1)}, bf16[16,48,128]{2,1,0:T(8,128)(2,1)S(1)}, u32[]{:S(2)}, u32[]{:S(2)}) %collective-permute-start.2) | collective-permute-done | bytes 196640 | tf_op jit(solution)/shard_map/ppermute | solution.py:367
  32.4 7.2 %collective-permute-done.3.refs_4_ = bf16[16,48,128]{2,1,0:T(8,128)(2,1)S(1)} collective-permute-done((bf16[16,48,128]{2,1,0:T(8,128)(2,1)S(1)}, bf16[16,48,128]{2,1,0:T(8,128)(2,1)S(1)}, u32[]{:S(2)}, u32[]{:S(2)}) %collective-permute-start.3) | collective-permute-done | bytes 196640 | tf_op jit(solution)/shard_map/ppermute | solution.py:367
  39.7 5.4 %collective-permute-start.10 = (bf16[16,48,128]{2,1,0:T(8,128)(2,1)S(1)}, bf16[16,48,128]{2,1,0:T(8,128)(2,1)S(1)}, u32[]{:S(2)}, u32[]{:S(2)}) collective-permute-start(bf16[16,48,128]{2,1,0:T(8,128)(2,1)S(1)} %get-tuple-element.42), channel_id=1, source_target_pairs={{0,64},{8,72},{16,80},{24,88},{32,96},{40,104},{48,112},{56,120},{... | collective-permute-start | bytes 589832 | tf_op jit(solution)/shard_map/ppermute | solution.py:367
  45.1 1.6 %copy-done.3 = bf16[1,64,128,128]{3,2,1,0:T(8,128)(2,1)S(1)} copy-done((bf16[1,64,128,128]{3,2,1,0:T(8,128)(2,1)S(1)}, bf16[1,64,128,128]{3,2,1,0:T(8,128)(2,1)}, u32[]{:S(2)}) %copy-start.3) | copy-done | bytes 2097176
  46.7 1.4 %mid_level.1 = (bf16[16,80,128]{2,1,0:T(8,128)(2,1)S(1)}, bf16[16,80,128]{2,1,0:T(8,128)(2,1)S(1)}, bf16[8,80,128]{2,1,0:T(8,128)(2,1)S(1)}, bf16[8,80,128]{2,1,0:T(8,128)(2,1)S(1)}, bf16[16,80,128]{2,1,0:T(8,128)(2,1)S(1)}) custom-call(s32[1]{0:T(128)} %bitcast.me_ref, s32[64]{0:T(128)S(1)} %bitcast.7, bf16[64,80,128]{2,1,0:T(8,128)(2,1)S(1)} %all-to-all-done.z_ref, ...), custom_call_target="tpu_custom_call" | custom-call | flops 100167770112 | bytes 4718592 | tf_op jit(solution)/shard_map/mid_level/pallas_call | solution.py:221
  48.1 0.6 collective-permute-start.5
  48.6 1.5 %collective-permute-start.6 = (bf16[8,80,128]{2,1,0:T(8,128)(2,1)S(1)}, bf16[8,80,128]{2,1,0:T(8,128)(2,1)S(1)}, u32[]{:S(2)}, u32[]{:S(2)}) collective-permute-start(bf16[8,80,128]{2,1,0:T(8,128)(2,1)S(1)} %get-tuple-element.39), channel_id=1, source_target_pairs={{0,3},{1,0},{2,1},{3,2},{4,7},{5,4},{6,5},{7,6},{8,11},{9,8},{10,9... | collective-permute-start | bytes 491528 | tf_op jit(solution)/shard_map/ppermute | solution.py:358
  50.2 4.8 %collective-permute-done.5.from_left_ref = bf16[8,80,128]{2,1,0:T(8,128)(2,1)S(1)} collective-permute-done((bf16[8,80,128]{2,1,0:T(8,128)(2,1)S(1)}, bf16[8,80,128]{2,1,0:T(8,128)(2,1)S(1)}, u32[]{:S(2)}, u32[]{:S(2)}) %collective-permute-start.5) | collective-permute-done | bytes 163872 | tf_op jit(solution)/shard_map/ppermute | solution.py:358
  55.0 1.9 %collective-permute-done.6.from_right_ref = bf16[8,80,128]{2,1,0:T(8,128)(2,1)S(1)} collective-permute-done((bf16[8,80,128]{2,1,0:T(8,128)(2,1)S(1)}, bf16[8,80,128]{2,1,0:T(8,128)(2,1)S(1)}, u32[]{:S(2)}, u32[]{:S(2)}) %collective-permute-start.6) | collective-permute-done | bytes 163872 | tf_op jit(solution)/shard_map/ppermute | solution.py:358
  57.3 1.8 %collective-permute-start.8 = (bf16[16,80,128]{2,1,0:T(8,128)(2,1)S(1)}, bf16[16,80,128]{2,1,0:T(8,128)(2,1)S(1)}, u32[]{:S(2)}, u32[]{:S(2)}) collective-permute-start(bf16[16,80,128]{2,1,0:T(8,128)(2,1)S(1)} %get-tuple-element.41), channel_id=1, source_target_pairs={{0,3},{1,0},{2,1},{3,2},{4,7},{5,4},{6,5},{7,6},{8,11},{9,8},{10,9... | collective-permute-start | bytes 983048 | tf_op jit(solution)/shard_map/ppermute | solution.py:358
  59.1 1.3 %mid_stepped.1 = (bf16[16,48,128]{2,1,0:T(8,128)(2,1)S(1)}, bf16[16,48,128]{2,1,0:T(8,128)(2,1)S(1)}, bf16[16,48,128]{2,1,0:T(8,128)(2,1)S(1)}, bf16[16,48,128]{2,1,0:T(8,128)(2,1)S(1)}) custom-call(s32[1]{0:T(128)} %bitcast.2.row_ref, s32[1]{0:T(128)} %bitcast.me_ref, s32[64]{0:T(128)S(1)} %bitcast.8, bf16[64,128,128]{2,1,0:T(8,128)(2,1)S(1)} %bitcast.6, ...), custom_call_target="tpu_custom_call" | custom-call | flops 100100661248 | bytes 3670016 | tf_op jit(solution)/shard_map/mid_stepped/pallas_call | solution.py:283
  60.4 1.5 %collective-permute-start.12 = (bf16[16,48,128]{2,1,0:T(8,128)(2,1)S(1)}, bf16[16,48,128]{2,1,0:T(8,128)(2,1)S(1)}, u32[]{:S(2)}, u32[]{:S(2)}) collective-permute-start(bf16[16,48,128]{2,1,0:T(8,128)(2,1)S(1)} %get-tuple-element.46), channel_id=1, source_target_pairs={{0,2},{1,3},{2,0},{3,1},{4,6},{5,7},{6,4},{7,5},{8,10},{9,11},{10,... | collective-permute-start | bytes 589832 | tf_op jit(solution)/shard_map/ppermute | solution.py:358
  61.9 1.8 %collective-permute-start.13 = (bf16[16,48,128]{2,1,0:T(8,128)(2,1)S(1)}, bf16[16,48,128]{2,1,0:T(8,128)(2,1)S(1)}, u32[]{:S(2)}, u32[]{:S(2)}) collective-permute-start(bf16[16,48,128]{2,1,0:T(8,128)(2,1)S(1)} %get-tuple-element.47), channel_id=1, source_target_pairs={{0,1},{1,2},{2,3},{3,0},{4,5},{5,6},{6,7},{7,4},{8,9},{9,10},{10,1... | collective-permute-start | bytes 589832 | tf_op jit(solution)/shard_map/ppermute | solution.py:358
  63.9 3.7 %collective-permute-done.7.refs_1_ = bf16[16,80,128]{2,1,0:T(8,128)(2,1)S(1)} collective-permute-done((bf16[16,80,128]{2,1,0:T(8,128)(2,1)S(1)}, bf16[16,80,128]{2,1,0:T(8,128)(2,1)S(1)}, u32[]{:S(2)}, u32[]{:S(2)}) %collective-permute-start.7) | collective-permute-done | bytes 327712 | tf_op jit(solution)/shard_map/ppermute | solution.py:358
  67.6 5.7 %collective-permute-done.8.refs_2_ = bf16[16,80,128]{2,1,0:T(8,128)(2,1)S(1)} collective-permute-done((bf16[16,80,128]{2,1,0:T(8,128)(2,1)S(1)}, bf16[16,80,128]{2,1,0:T(8,128)(2,1)S(1)}, u32[]{:S(2)}, u32[]{:S(2)}) %collective-permute-start.8) | collective-permute-done | bytes 327712 | tf_op jit(solution)/shard_map/ppermute | solution.py:358
  73.4 5.8 %collective-permute-start.9 = (bf16[8,80,128]{2,1,0:T(8,128)(2,1)S(1)}, bf16[8,80,128]{2,1,0:T(8,128)(2,1)S(1)}, u32[]{:S(2)}, u32[]{:S(2)}) collective-permute-start(bf16[8,80,128]{2,1,0:T(8,128)(2,1)S(1)} %sum_other.2), channel_id=1, source_target_pairs={{0,4},{1,5},{2,6},{3,7},{4,0},{5,1},{6,2},{7,3},{8,12},{9,13},{10,... | collective-permute-start | bytes 491528 | tf_op jit(solution)/shard_map/ppermute | solution.py:363
  79.3 2.9 %collective-permute-start.15 = (bf16[8,48,128]{2,1,0:T(8,128)(2,1)S(1)}, bf16[8,48,128]{2,1,0:T(8,128)(2,1)S(1)}, u32[]{:S(2)}, u32[]{:S(2)}) collective-permute-start(bf16[8,48,128]{2,1,0:T(8,128)(2,1)S(1)} %sum_other.3), channel_id=1, source_target_pairs={{0,4},{1,5},{2,6},{3,7},{4,0},{5,1},{6,2},{7,3},{8,12},{9,13},{10,... | collective-permute-start | bytes 294920 | tf_op jit(solution)/shard_map/ppermute | solution.py:363
  82.2 8.0 %collective-permute-done.15.refs_8_ = bf16[8,48,128]{2,1,0:T(8,128)(2,1)S(1)} collective-permute-done((bf16[8,48,128]{2,1,0:T(8,128)(2,1)S(1)}, bf16[8,48,128]{2,1,0:T(8,128)(2,1)S(1)}, u32[]{:S(2)}, u32[]{:S(2)}) %collective-permute-start.15) | collective-permute-done | bytes 98336 | tf_op jit(solution)/shard_map/ppermute | solution.py:363
  90.2 1.6 %row_level.1 = bf16[8,128,128]{2,1,0:T(8,128)(2,1)} custom-call(s32[1]{0:T(128)} %bitcast.me_ref, s32[64]{0:T(128)S(1)} %copy-done.2, bf16[64,128,128]{2,1,0:T(8,128)(2,1)S(1)} %copy-done, bf16[16,80,128]{2,1,0:T(8,128)(2,1)S(1)} %get-tuple-element.35.refs_0_, bf16[16,80,128]{2,1,0:T(8,128)(2,1)S(1)} %collective-permute-done.7.refs_1_, ...), custom_call_target="tpu_custom_call" | custom-call | flops 33554432 | bytes 1048576 | tf_op jit(solution)/shard_map/row_level/pallas_call | solution.py:343
  (34 shorter events, 1.6 us)
Async XLA Ops:
  6.0 8.9 %copy-start.5 = (bf16[24,48,128]{2,1,0:T(8,128)(2,1)S(1)}, bf16[24,48,128]{2,1,0:T(8,128)(2,1)}, u32[]{:S(2)}) copy-start(bf16[24,48,128]{2,1,0:T(8,128)(2,1)} %get-tuple-element.30.refs_0_) | copy-start | bytes 884740
  6.1 8.8 %collective-permute-start = (bf16[16,48,128]{2,1,0:T(8,128)(2,1)}, bf16[16,48,128]{2,1,0:T(8,128)(2,1)S(1)}, u32[]{:S(2)}, u32[]{:S(2)}) collective-permute-start(bf16[16,48,128]{2,1,0:T(8,128)(2,1)} %get-tuple-element.29), channel_id=1, source_target_pairs={{0,192},{8,200},{16,208},{24,216},{32,224},{40,232},{48,240},{56,2... | collective-permute-start | bytes 589832 | tf_op jit(solution)/shard_map/ppermute | solution.py:367
  6.2 38.9 %all-to-all-start = ((bf16[64,80,128]{2,1,0:T(8,128)(2,1)}), bf16[64,80,128]{2,1,0:T(8,128)(2,1)S(1)}, u32[]{:S(2)}, u32[]{:S(2)}) async-start(bf16[64,80,128]{2,1,0:T(8,128)(2,1)} %get-tuple-element.27), calls=%async_computation | async-start | bytes 2621440 | tf_op jit(solution)/shard_map/all_to_all | solution.py:384
  14.9 1.9 %copy-start.1 = (bf16[24,48,128]{2,1,0:T(8,128)(2,1)S(1)}, bf16[24,48,128]{2,1,0:T(8,128)(2,1)}, u32[]{:S(2)}) copy-start(bf16[24,48,128]{2,1,0:T(8,128)(2,1)} %get-tuple-element.28.refs_0_) | copy-start | bytes 884740
  14.9 30.1 %copy-start.6 = (s32[1,64]{1,0:T(1,128)S(1)}, s32[1,64]{1,0:T(1,128)}, u32[]{:S(2)}) copy-start(s32[1,64]{1,0:T(1,128)} %param.13) | copy-start | bytes 772
  14.9 1.8 %collective-permute-start.1 = (bf16[32,48,128]{2,1,0:T(8,128)(2,1)S(1)}, bf16[32,48,128]{2,1,0:T(8,128)(2,1)S(1)}, u32[]{:S(2)}, u32[]{:S(2)}) collective-permute-start(bf16[32,48,128]{2,1,0:T(8,128)(2,1)S(1)} %regroup.3), channel_id=1, source_target_pairs={{0,8},{8,0},{16,24},{24,16},{32,40},{40,32},{48,56},{56,48},{64,72... | collective-permute-start | bytes 1179656 | tf_op jit(solution)/shard_map/ppermute | solution.py:367
  16.8 15.6 %collective-permute-start.2 = (bf16[16,48,128]{2,1,0:T(8,128)(2,1)S(1)}, bf16[16,48,128]{2,1,0:T(8,128)(2,1)S(1)}, u32[]{:S(2)}, u32[]{:S(2)}) collective-permute-start(bf16[16,48,128]{2,1,0:T(8,128)(2,1)S(1)} %get-tuple-element.31), channel_id=1, source_target_pairs={{0,16},{8,24},{16,0},{24,8},{32,48},{40,56},{48,32},{56,40},{64,80... | collective-permute-start | bytes 589832 | tf_op jit(solution)/shard_map/ppermute | solution.py:367
  18.5 21.2 %collective-permute-start.3 = (bf16[16,48,128]{2,1,0:T(8,128)(2,1)S(1)}, bf16[16,48,128]{2,1,0:T(8,128)(2,1)S(1)}, u32[]{:S(2)}, u32[]{:S(2)}) collective-permute-start(bf16[16,48,128]{2,1,0:T(8,128)(2,1)S(1)} %get-tuple-element.32), channel_id=1, source_target_pairs={{0,32},{8,40},{16,48},{24,56},{32,0},{40,8},{48,16},{56,24},{64,96... | collective-permute-start | bytes 589832 | tf_op jit(solution)/shard_map/ppermute | solution.py:367
  21.4 18.3 %collective-permute-start.4 = (bf16[16,48,128]{2,1,0:T(8,128)(2,1)S(1)}, bf16[16,48,128]{2,1,0:T(8,128)(2,1)S(1)}, u32[]{:S(2)}, u32[]{:S(2)}) collective-permute-start(bf16[16,48,128]{2,1,0:T(8,128)(2,1)S(1)} %get-tuple-element.33), channel_id=1, source_target_pairs={{0,48},{8,56},{16,32},{24,40},{32,16},{40,24},{48,0},{56,8},{64,11... | collective-permute-start | bytes 589832 | tf_op jit(solution)/shard_map/ppermute | solution.py:367
  39.7 19.4 %collective-permute-start.10 = (bf16[16,48,128]{2,1,0:T(8,128)(2,1)S(1)}, bf16[16,48,128]{2,1,0:T(8,128)(2,1)S(1)}, u32[]{:S(2)}, u32[]{:S(2)}) collective-permute-start(bf16[16,48,128]{2,1,0:T(8,128)(2,1)S(1)} %get-tuple-element.42), channel_id=1, source_target_pairs={{0,64},{8,72},{16,80},{24,88},{32,96},{40,104},{48,112},{56,120},{... | collective-permute-start | bytes 589832 | tf_op jit(solution)/shard_map/ppermute | solution.py:367
  45.1 14.0 %collective-permute-start.11 = (bf16[16,48,128]{2,1,0:T(8,128)(2,1)S(1)}, bf16[16,48,128]{2,1,0:T(8,128)(2,1)S(1)}, u32[]{:S(2)}, u32[]{:S(2)}) collective-permute-start(bf16[16,48,128]{2,1,0:T(8,128)(2,1)S(1)} %get-tuple-element.43), channel_id=1, source_target_pairs={{0,128},{8,136},{16,144},{24,152},{32,160},{40,168},{48,176},{56,1... | collective-permute-start | bytes 589832 | tf_op jit(solution)/shard_map/ppermute | solution.py:367
  45.1 1.6 %copy-start.3 = (bf16[1,64,128,128]{3,2,1,0:T(8,128)(2,1)S(1)}, bf16[1,64,128,128]{3,2,1,0:T(8,128)(2,1)}, u32[]{:S(2)}) copy-start(bf16[1,64,128,128]{3,2,1,0:T(8,128)(2,1)} %param.12) | copy-start | bytes 6291460
  46.7 12.4 %copy-start.4 = (bf16[1,64,128,128]{3,2,1,0:T(8,128)(2,1)S(1)}, bf16[1,64,128,128]{3,2,1,0:T(8,128)(2,1)}, u32[]{:S(2)}) copy-start(bf16[1,64,128,128]{3,2,1,0:T(8,128)(2,1)} %param.12) | copy-start | bytes 6291460
  48.1 6.9 %collective-permute-start.5 = (bf16[8,80,128]{2,1,0:T(8,128)(2,1)S(1)}, bf16[8,80,128]{2,1,0:T(8,128)(2,1)S(1)}, u32[]{:S(2)}, u32[]{:S(2)}) collective-permute-start(bf16[8,80,128]{2,1,0:T(8,128)(2,1)S(1)} %get-tuple-element.38), channel_id=1, source_target_pairs={{0,1},{1,2},{2,3},{3,0},{4,5},{5,6},{6,7},{7,4},{8,9},{9,10},{10,1... | collective-permute-start | bytes 491528 | tf_op jit(solution)/shard_map/ppermute | solution.py:358
  48.6 8.3 %collective-permute-start.6 = (bf16[8,80,128]{2,1,0:T(8,128)(2,1)S(1)}, bf16[8,80,128]{2,1,0:T(8,128)(2,1)S(1)}, u32[]{:S(2)}, u32[]{:S(2)}) collective-permute-start(bf16[8,80,128]{2,1,0:T(8,128)(2,1)S(1)} %get-tuple-element.39), channel_id=1, source_target_pairs={{0,3},{1,0},{2,1},{3,2},{4,7},{5,4},{6,5},{7,6},{8,11},{9,8},{10,9... | collective-permute-start | bytes 491528 | tf_op jit(solution)/shard_map/ppermute | solution.py:358
  57.0 10.6 %collective-permute-start.7 = (bf16[16,80,128]{2,1,0:T(8,128)(2,1)S(1)}, bf16[16,80,128]{2,1,0:T(8,128)(2,1)S(1)}, u32[]{:S(2)}, u32[]{:S(2)}) collective-permute-start(bf16[16,80,128]{2,1,0:T(8,128)(2,1)S(1)} %get-tuple-element.40), channel_id=1, source_target_pairs={{0,1},{1,2},{2,3},{3,0},{4,5},{5,6},{6,7},{7,4},{8,9},{9,10},{10,1... | collective-permute-start | bytes 983048 | tf_op jit(solution)/shard_map/ppermute | solution.py:358
  57.3 16.0 %collective-permute-start.8 = (bf16[16,80,128]{2,1,0:T(8,128)(2,1)S(1)}, bf16[16,80,128]{2,1,0:T(8,128)(2,1)S(1)}, u32[]{:S(2)}, u32[]{:S(2)}) collective-permute-start(bf16[16,80,128]{2,1,0:T(8,128)(2,1)S(1)} %get-tuple-element.41), channel_id=1, source_target_pairs={{0,3},{1,0},{2,1},{3,2},{4,7},{5,4},{6,5},{7,6},{8,11},{9,8},{10,9... | collective-permute-start | bytes 983048 | tf_op jit(solution)/shard_map/ppermute | solution.py:358
  59.1 31.1 %copy-start = (bf16[64,128,128]{2,1,0:T(8,128)(2,1)S(1)}, bf16[64,128,128]{2,1,0:T(8,128)(2,1)}, u32[]{:S(2)}) copy-start(bf16[64,128,128]{2,1,0:T(8,128)(2,1)} %w_ref.3) | copy-start | bytes 6291460
  59.1 31.1 %copy-start.2 = (s32[64]{0:T(128)S(1)}, s32[64]{0:T(128)}, u32[]{:S(2)}) copy-start(s32[64]{0:T(128)} %rank_ref.3) | copy-start | bytes 772
  60.4 18.8 %collective-permute-start.12 = (bf16[16,48,128]{2,1,0:T(8,128)(2,1)S(1)}, bf16[16,48,128]{2,1,0:T(8,128)(2,1)S(1)}, u32[]{:S(2)}, u32[]{:S(2)}) collective-permute-start(bf16[16,48,128]{2,1,0:T(8,128)(2,1)S(1)} %get-tuple-element.46), channel_id=1, source_target_pairs={{0,2},{1,3},{2,0},{3,1},{4,6},{5,7},{6,4},{7,5},{8,10},{9,11},{10,... | collective-permute-start | bytes 589832 | tf_op jit(solution)/shard_map/ppermute | solution.py:358
  61.9 17.3 %collective-permute-start.13 = (bf16[16,48,128]{2,1,0:T(8,128)(2,1)S(1)}, bf16[16,48,128]{2,1,0:T(8,128)(2,1)S(1)}, u32[]{:S(2)}, u32[]{:S(2)}) collective-permute-start(bf16[16,48,128]{2,1,0:T(8,128)(2,1)S(1)} %get-tuple-element.47), channel_id=1, source_target_pairs={{0,1},{1,2},{2,3},{3,0},{4,5},{5,6},{6,7},{7,4},{8,9},{9,10},{10,1... | collective-permute-start | bytes 589832 | tf_op jit(solution)/shard_map/ppermute | solution.py:358
  63.7 15.5 %collective-permute-start.14 = (bf16[16,48,128]{2,1,0:T(8,128)(2,1)S(1)}, bf16[16,48,128]{2,1,0:T(8,128)(2,1)S(1)}, u32[]{:S(2)}, u32[]{:S(2)}) collective-permute-start(bf16[16,48,128]{2,1,0:T(8,128)(2,1)S(1)} %get-tuple-element.48), channel_id=1, source_target_pairs={{0,3},{1,0},{2,1},{3,2},{4,7},{5,4},{6,5},{7,6},{8,11},{9,8},{10,9... | collective-permute-start | bytes 589832 | tf_op jit(solution)/shard_map/ppermute | solution.py:358
  73.4 16.8 %collective-permute-start.9 = (bf16[8,80,128]{2,1,0:T(8,128)(2,1)S(1)}, bf16[8,80,128]{2,1,0:T(8,128)(2,1)S(1)}, u32[]{:S(2)}, u32[]{:S(2)}) collective-permute-start(bf16[8,80,128]{2,1,0:T(8,128)(2,1)S(1)} %sum_other.2), channel_id=1, source_target_pairs={{0,4},{1,5},{2,6},{3,7},{4,0},{5,1},{6,2},{7,3},{8,12},{9,13},{10,... | collective-permute-start | bytes 491528 | tf_op jit(solution)/shard_map/ppermute | solution.py:363
  79.3 10.9 %collective-permute-start.15 = (bf16[8,48,128]{2,1,0:T(8,128)(2,1)S(1)}, bf16[8,48,128]{2,1,0:T(8,128)(2,1)S(1)}, u32[]{:S(2)}, u32[]{:S(2)}) collective-permute-start(bf16[8,48,128]{2,1,0:T(8,128)(2,1)S(1)} %sum_other.3), channel_id=1, source_target_pairs={{0,4},{1,5},{2,6},{3,7},{4,0},{5,1},{6,2},{7,3},{8,12},{9,13},{10,... | collective-permute-start | bytes 294920 | tf_op jit(solution)/shard_map/ppermute | solution.py:363

commit v7 on v6

--- a/solution.py
+++ b/solution.py
@@ -147,18 +147,18 @@
         refs[n_in + target][place : place + Q] = refs[source][start : start + Q]
 
 
-def regroup(rows, moves, n_out, size, pieces, hint=0):
-    return pl.pallas_call(
-        functools.partial(regroup_kernel, moves, len(pieces)),
+def regroup(rows, moves, n_out, size, pieces, hint=0, after=()):
+    return pl.pallas_call(
+        functools.partial(regroup_kernel, moves, len(pieces) + len(after)),
         out_shape=[jax.ShapeDtypeStruct((size, rows, BW), BF16)] * n_out,
-        in_specs=[VMEM] * len(pieces),
+        in_specs=[VMEM] * len(pieces) + [ANY] * len(after),
         out_specs=[VMEM] * n_out,
         compiler_params=SMALL,
         cost_estimate=pl.CostEstimate(
             flops=hint, bytes_accessed=4 * n_out * size * rows * BW, transcendentals=0
         ),
         name="regroup",
-    )(*pieces)
+    )(*pieces, *after)
 
 
 def held(k, m, e):
@@ -203,33 +203,65 @@
     return moves
 
 
-def mid_kernel(me_ref, rank_ref, z_ref, w_ref, after_ref, *out_refs):
-    for d in (2, 1, 3, 0):
+def pick_kernel(me_ref, w_ref, far_ref, near_ref):
+    for n, d in enumerate((2, 1, 3, 0)):
+        for h in range(N_Z):
+            base = (h * N_X + lax.rem(me_ref[0] + d, N_X)) * STEP
+            out_ref, slot = (far_ref, h) if n == 0 else (near_ref, (n - 1) * N_Z + h)
+            out_ref[slot * STEP : (slot + 1) * STEP] = w_ref[pl.ds(base, STEP)]
+
+
+def pick_factors(me, factors):
+    count = N_Z * STEP
+    return pl.pallas_call(
+        pick_kernel,
+        out_shape=[
+            jax.ShapeDtypeStruct((count, BW, BW), BF16),
+            jax.ShapeDtypeStruct((PB - count, BW, BW), BF16),
+        ],
+        in_specs=[SMEM, VMEM],
+        out_specs=[VMEM] * 2,
+        compiler_params=SMALL,
+        cost_estimate=pl.CostEstimate(
+            flops=0, bytes_accessed=4 * PB * BW * BW, transcendentals=0
+        ),
+        name="pick_factors",
+    )(me, factors)
+
+
+def far_kernel(me_ref, rank_ref, z_ref, w_ref, after_ref, first_ref, second_ref):
+    for h in range(N_Z):
+        base = (h * N_X + lax.rem(me_ref[0] + 2, N_X)) * STEP
+        for j in range(STEP):
+            inner = masked_dot(z_ref[base + j], w_ref[h * STEP + j], rank_ref[base + j])
+            out_ref = first_ref if j < SIDE else second_ref
+            out_ref[h * SIDE + j % SIDE] = inner.astype(BF16)
+
+
+def near_kernel(me_ref, rank_ref, z_ref, w_ref, after_ref, *out_refs):
+    for n, d in enumerate((1, 3, 0)):
         for h in range(N_Z):
             base = (h * N_X + lax.rem(me_ref[0] + d, N_X)) * STEP
             for j in range(STEP):
-                inner = masked_dot(z_ref[base + j], w_ref[base + j], rank_ref[base + j])
-                if d == 2:
-                    out_refs[2 + j // SIDE][h * SIDE + j % SIDE] = inner.astype(BF16)
-                else:
-                    out_refs[d if d < 2 else 4][h * STEP + j] = inner.astype(BF16)
-
-
-def mid_level(rows, me, ranks, blocks, factors, after):
-    whole = jax.ShapeDtypeStruct((N_Z * STEP, rows, BW), BF16)
-    side = jax.ShapeDtypeStruct((N_Z * SIDE, rows, BW), BF16)
-    return pl.pallas_call(
-        mid_kernel,
-        out_shape=[whole, whole, side, side, whole],
+                factors = w_ref[(n * N_Z + h) * STEP + j]
+                inner = masked_dot(z_ref[base + j], factors, rank_ref[base + j])
+                out_refs[n][h * STEP + j] = inner.astype(BF16)
+
+
+def mid_part(kernel, name, rows, sizes, me, ranks, blocks, factors, after):
+    count = factors.shape[0]
+    return pl.pallas_call(
+        kernel,
+        out_shape=[jax.ShapeDtypeStruct((size, rows, BW), BF16) for size in sizes],
         in_specs=[SMEM, SMEM, VMEM, VMEM, ANY],
-        out_specs=[VMEM] * 5,
-        compiler_params=SMALL,
-        cost_estimate=pl.CostEstimate(
-            flops=2 * PB * rows * BW * BW + HINT_MID,
-            bytes_accessed=PB * (4 * rows + 2 * BW) * BW,
+        out_specs=[VMEM] * len(sizes),
+        compiler_params=SMALL,
+        cost_estimate=pl.CostEstimate(
+            flops=2 * count * rows * BW * BW + HINT_MID,
+            bytes_accessed=count * (4 * rows + 2 * BW) * BW,
             transcendentals=0,
         ),
-        name="mid_level",
+        name=name,
     )(me, ranks, blocks, factors, after)
 
 
@@ -389,12 +421,22 @@
     pieces = [same, early, across_row(other, 0, 0, 1)]
     lines = regroup(stepped_rows, for_y(), N_Y - 1, PIECE, pieces, HINT_Y)
     pieces += [across_row(line, 0, m + 1, 0) for m, line in enumerate(lines)]
-    planes = list(regroup(stepped_rows, for_planes(), N_PLANE, PIECE, pieces, HINT_PLANES))
+    far_factors, near_factors = pick_factors(me, factors)
+    planes = list(
+        regroup(
+            stepped_rows, for_planes(), N_PLANE, PIECE, pieces, HINT_PLANES, [far_factors]
+        )
+    )
     for k in range(1, EARLY):
         planes[k] = across_row(planes[k], k, 0, 0)
 
-    own, right, first, second, left = mid_level(
-        straight_rows, me, ranks, regrouped, factors, planes[0]
+    first, second = mid_part(
+        far_kernel, "mid_far", straight_rows, [STEP, STEP], me, ranks, regrouped, far_factors,
+        planes[0],
+    )
+    right, left, own = mid_part(
+        near_kernel, "mid_near", straight_rows, [N_Z * STEP] * 3, me, ranks, regrouped,
+        near_factors, first,
     )
     from_left, from_right = around_x(first, 1), around_x(second, 3)
     right, left = join_sides(straight_rows, right, left, from_left, from_right)

time: 92.1 us -> 90.6 us (0.984)
  the two profiles are of different devices: /device:TPU:102 before, /device:TPU:38 now
where the time goes in v7:
time: 90.6 us; the launch traced here: 90.3 us
  starting transfers between devices  39.2 us (43%)
  waiting for transfers between devices  37 us (41%)
  Pallas kernels  12.8 us (14%)
  local copies, waits for them, and re-layouts  1.21 us (1%)
    ppermute x7, waiting for transfers between devices, across_row(): lax.ppermute(value, 'row', [(r, r ^ flip(k, m, e)) for r in range(N_PLANE...  20.3 us
    ppermute x7, starting transfers between devices, across_row(): lax.ppermute(value, 'row', [(r, r ^ flip(k, m, e)) for r in range(N_PLANE...  13 us
    ppermute x2, starting transfers between devices, across_z(): lax.ppermute(value, 'col', [(i, (i + half) % (2 * half)) for i in range(2...  11.2 us
    ppermute x7, waiting for transfers between devices, around_x(): return lax.ppermute(value, 'col', pairs)  10.4 us
    ppermute x7, starting transfers between devices, around_x(): return lax.ppermute(value, 'col', pairs)  7.52 us
    all_to_all x1, starting transfers between devices, shards(): lax.all_to_all(middle, 'row', split_axis=0, concat_axis=0, tiled=True)  7.45 us
    ppermute x2, waiting for transfers between devices, across_z(): lax.ppermute(value, 'col', [(i, (i + half) % (2 * half)) for i in range(2...  6.38 us
    pallas_call x1, Pallas kernels, col_levels(): pl.pallas_call(col_kernel, out_shape=[jax.ShapeDtypeStruct((PB, straight,...  6.02 us
  transfers between devices with their start and end apart: 17, of which 10 were waited for; matrix products, arithmetic and copies ran while one was open for 0% of the time, Pallas kernels for 6%

profile of v7, /device:TPU:38, one launch (start us, length us, event | category | flops | bytes accessed | tf_op | source)
XLA Modules:
  0.0 90.3 jit_solution(16630249821643045601)
XLA Ops:
  0.0 6.0 %col_levels.1 = (bf16[64,80,128]{2,1,0:T(8,128)(2,1)}, bf16[16,48,128]{2,1,0:T(8,128)(2,1)}, bf16[24,48,128]{2,1,0:T(8,128)(2,1)}, bf16[24,48,128]{2,1,0:T(8,128)(2,1)}) custom-call(s32[1]{0:T(128)} %bitcast.2.row_ref, s32[1]{0:T(128)} %bitcast.me_ref, s32[64]{0:T(128)} %bitcast.10, s32[2,64]{1,0:T(2,128)} %rank_ref.2, bf16[64,128,128]{2,1,0:T(8,128)(2,1)} %z_ref.1, ...), custom_call_target="tpu_custom_call" | custom-call | flops 536870912 | bytes 8388608 | tf_op jit(solution)/shard_map/col_levels/pallas_call | solution.py:120
  6.0 2.0 %collective-permute-start = (bf16[16,48,128]{2,1,0:T(8,128)(2,1)}, bf16[16,48,128]{2,1,0:T(8,128)(2,1)S(1)}, u32[]{:S(2)}, u32[]{:S(2)}) collective-permute-start(bf16[16,48,128]{2,1,0:T(8,128)(2,1)} %get-tuple-element.33), channel_id=1, source_target_pairs={{0,192},{8,200},{16,208},{24,216},{32,224},{40,232},{48,240},{56,2... | collective-permute-start | bytes 589832 | tf_op jit(solution)/shard_map/ppermute | solution.py:399
  8.0 7.4 %all-to-all-start = ((bf16[64,80,128]{2,1,0:T(8,128)(2,1)}), bf16[64,80,128]{2,1,0:T(8,128)(2,1)S(1)}, u32[]{:S(2)}, u32[]{:S(2)}) async-start(bf16[64,80,128]{2,1,0:T(8,128)(2,1)} %get-tuple-element.29), calls=%async_computation | async-start | bytes 2621440 | tf_op jit(solution)/shard_map/all_to_all | solution.py:416
  15.5 2.8 %collective-permute-done.refs_1_ = bf16[16,48,128]{2,1,0:T(8,128)(2,1)S(1)} collective-permute-done((bf16[16,48,128]{2,1,0:T(8,128)(2,1)}, bf16[16,48,128]{2,1,0:T(8,128)(2,1)S(1)}, u32[]{:S(2)}, u32[]{:S(2)}) %collective-permute-start) | collective-permute-done | bytes 196640 | tf_op jit(solution)/shard_map/ppermute | solution.py:399
  18.4 1.7 %collective-permute-done.1.refs_2_ = bf16[32,48,128]{2,1,0:T(8,128)(2,1)S(1)} collective-permute-done((bf16[32,48,128]{2,1,0:T(8,128)(2,1)S(1)}, bf16[32,48,128]{2,1,0:T(8,128)(2,1)S(1)}, u32[]{:S(2)}, u32[]{:S(2)}) %collective-permute-start.1) | collective-permute-done | bytes 393248 | tf_op jit(solution)/shard_map/ppermute | solution.py:399
  20.2 1.4 %collective-permute-start.2 = (bf16[16,48,128]{2,1,0:T(8,128)(2,1)S(1)}, bf16[16,48,128]{2,1,0:T(8,128)(2,1)S(1)}, u32[]{:S(2)}, u32[]{:S(2)}) collective-permute-start(bf16[16,48,128]{2,1,0:T(8,128)(2,1)S(1)} %get-tuple-element.35), channel_id=1, source_target_pairs={{0,16},{8,24},{16,0},{24,8},{32,48},{40,56},{48,32},{56,40},{64,80... | collective-permute-start | bytes 589832 | tf_op jit(solution)/shard_map/ppermute | solution.py:399
  21.6 4.7 %collective-permute-start.3 = (bf16[16,48,128]{2,1,0:T(8,128)(2,1)S(1)}, bf16[16,48,128]{2,1,0:T(8,128)(2,1)S(1)}, u32[]{:S(2)}, u32[]{:S(2)}) collective-permute-start(bf16[16,48,128]{2,1,0:T(8,128)(2,1)S(1)} %get-tuple-element.36), channel_id=1, source_target_pairs={{0,32},{8,40},{16,48},{24,56},{32,0},{40,8},{48,16},{56,24},{64,96... | collective-permute-start | bytes 589832 | tf_op jit(solution)/shard_map/ppermute | solution.py:399
  27.6 4.0 %collective-permute-done.2.refs_3_ = bf16[16,48,128]{2,1,0:T(8,128)(2,1)S(1)} collective-permute-done((bf16[16,48,128]{2,1,0:T(8,128)(2,1)S(1)}, bf16[16,48,128]{2,1,0:T(8,128)(2,1)S(1)}, u32[]{:S(2)}, u32[]{:S(2)}) %collective-permute-start.2) | collective-permute-done | bytes 196640 | tf_op jit(solution)/shard_map/ppermute | solution.py:399
  31.6 10.8 %collective-permute-done.3.refs_4_ = bf16[16,48,128]{2,1,0:T(8,128)(2,1)S(1)} collective-permute-done((bf16[16,48,128]{2,1,0:T(8,128)(2,1)S(1)}, bf16[16,48,128]{2,1,0:T(8,128)(2,1)S(1)}, u32[]{:S(2)}, u32[]{:S(2)}) %collective-permute-start.3) | collective-permute-done | bytes 196640 | tf_op jit(solution)/shard_map/ppermute | solution.py:399
  44.2 4.8 %collective-permute-start.11 = (bf16[16,48,128]{2,1,0:T(8,128)(2,1)}, bf16[16,48,128]{2,1,0:T(8,128)(2,1)}, u32[]{:S(2)}, u32[]{:S(2)}) collective-permute-start(bf16[16,48,128]{2,1,0:T(8,128)(2,1)} %get-tuple-element.47), channel_id=1, source_target_pairs={{0,128},{8,136},{16,144},{24,152},{32,160},{40,168},{48,176},{56,1... | collective-permute-start | bytes 589832 | tf_op jit(solution)/shard_map/ppermute | solution.py:399
  50.4 1.5 %collective-permute-start.6 = (bf16[8,80,128]{2,1,0:T(8,128)(2,1)S(1)}, bf16[8,80,128]{2,1,0:T(8,128)(2,1)S(1)}, u32[]{:S(2)}, u32[]{:S(2)}) collective-permute-start(bf16[8,80,128]{2,1,0:T(8,128)(2,1)S(1)} %get-tuple-element.43), channel_id=1, source_target_pairs={{0,3},{1,0},{2,1},{3,2},{4,7},{5,4},{6,5},{7,6},{8,11},{9,8},{10,9... | collective-permute-start | bytes 491528 | tf_op jit(solution)/shard_map/ppermute | solution.py:390
  51.9 1.2 %mid_near.1 = (bf16[16,80,128]{2,1,0:T(8,128)(2,1)S(1)}, bf16[16,80,128]{2,1,0:T(8,128)(2,1)S(1)}, bf16[16,80,128]{2,1,0:T(8,128)(2,1)S(1)}) custom-call(s32[1]{0:T(128)} %bitcast.me_ref, s32[64]{0:T(128)S(1)} %bitcast.8, bf16[64,80,128]{2,1,0:T(8,128)(2,1)S(1)} %all-to-all-done.z_ref, bf16[48,128,128]{2,1,0:T(8,128)(2,1)S(1)} %copy-done.6, ...), custom_call_target="tpu_custom_call" | custom-call | flops 100125827072 | bytes 3538944 | tf_op jit(solution)/shard_map/mid_near/pallas_call | solution.py:253
  53.1 2.1 %collective-permute-done.5.from_left_ref = bf16[8,80,128]{2,1,0:T(8,128)(2,1)S(1)} collective-permute-done((bf16[8,80,128]{2,1,0:T(8,128)(2,1)S(1)}, bf16[8,80,128]{2,1,0:T(8,128)(2,1)S(1)}, u32[]{:S(2)}, u32[]{:S(2)}) %collective-permute-start.5) | collective-permute-done | bytes 163872 | tf_op jit(solution)/shard_map/ppermute | solution.py:390
  55.2 1.7 %collective-permute-done.6.from_right_ref = bf16[8,80,128]{2,1,0:T(8,128)(2,1)S(1)} collective-permute-done((bf16[8,80,128]{2,1,0:T(8,128)(2,1)S(1)}, bf16[8,80,128]{2,1,0:T(8,128)(2,1)S(1)}, u32[]{:S(2)}, u32[]{:S(2)}) %collective-permute-start.6) | collective-permute-done | bytes 163872 | tf_op jit(solution)/shard_map/ppermute | solution.py:390
  57.3 1.8 %collective-permute-start.8 = (bf16[16,80,128]{2,1,0:T(8,128)(2,1)S(1)}, bf16[16,80,128]{2,1,0:T(8,128)(2,1)S(1)}, u32[]{:S(2)}, u32[]{:S(2)}) collective-permute-start(bf16[16,80,128]{2,1,0:T(8,128)(2,1)S(1)} %get-tuple-element.45), channel_id=1, source_target_pairs={{0,3},{1,0},{2,1},{3,2},{4,7},{5,4},{6,5},{7,6},{8,11},{9,8},{10,9... | collective-permute-start | bytes 983048 | tf_op jit(solution)/shard_map/ppermute | solution.py:390
  59.1 1.9 %mid_stepped.1 = (bf16[16,48,128]{2,1,0:T(8,128)(2,1)S(1)}, bf16[16,48,128]{2,1,0:T(8,128)(2,1)S(1)}, bf16[16,48,128]{2,1,0:T(8,128)(2,1)S(1)}, bf16[16,48,128]{2,1,0:T(8,128)(2,1)S(1)}) custom-call(s32[1]{0:T(128)} %bitcast.2.row_ref, s32[1]{0:T(128)} %bitcast.me_ref, s32[64]{0:T(128)S(1)} %bitcast.9, bf16[64,128,128]{2,1,0:T(8,128)(2,1)S(1)} %bitcast.6, ...), custom_call_target="tpu_custom_call" | custom-call | flops 100100661248 | bytes 3670016 | tf_op jit(solution)/shard_map/mid_stepped/pallas_call | solution.py:315
  61.1 1.3 %collective-permute-start.12 = (bf16[16,48,128]{2,1,0:T(8,128)(2,1)S(1)}, bf16[16,48,128]{2,1,0:T(8,128)(2,1)S(1)}, u32[]{:S(2)}, u32[]{:S(2)}) collective-permute-start(bf16[16,48,128]{2,1,0:T(8,128)(2,1)S(1)} %get-tuple-element.50), channel_id=1, source_target_pairs={{0,2},{1,3},{2,0},{3,1},{4,6},{5,7},{6,4},{7,5},{8,10},{9,11},{10,... | collective-permute-start | bytes 589832 | tf_op jit(solution)/shard_map/ppermute | solution.py:390
  62.4 1.8 %collective-permute-start.13 = (bf16[16,48,128]{2,1,0:T(8,128)(2,1)S(1)}, bf16[16,48,128]{2,1,0:T(8,128)(2,1)S(1)}, u32[]{:S(2)}, u32[]{:S(2)}) collective-permute-start(bf16[16,48,128]{2,1,0:T(8,128)(2,1)S(1)} %get-tuple-element.51), channel_id=1, source_target_pairs={{0,1},{1,2},{2,3},{3,0},{4,5},{5,6},{6,7},{7,4},{8,9},{9,10},{10,1... | collective-permute-start | bytes 589832 | tf_op jit(solution)/shard_map/ppermute | solution.py:390
  64.4 2.9 %collective-permute-done.7.refs_1_ = bf16[16,80,128]{2,1,0:T(8,128)(2,1)S(1)} collective-permute-done((bf16[16,80,128]{2,1,0:T(8,128)(2,1)S(1)}, bf16[16,80,128]{2,1,0:T(8,128)(2,1)S(1)}, u32[]{:S(2)}, u32[]{:S(2)}) %collective-permute-start.7) | collective-permute-done | bytes 327712 | tf_op jit(solution)/shard_map/ppermute | solution.py:390
  67.3 3.6 %collective-permute-done.8.refs_2_ = bf16[16,80,128]{2,1,0:T(8,128)(2,1)S(1)} collective-permute-done((bf16[16,80,128]{2,1,0:T(8,128)(2,1)S(1)}, bf16[16,80,128]{2,1,0:T(8,128)(2,1)S(1)}, u32[]{:S(2)}, u32[]{:S(2)}) %collective-permute-start.8) | collective-permute-done | bytes 327712 | tf_op jit(solution)/shard_map/ppermute | solution.py:390
  71.0 7.9 %collective-permute-start.9 = (bf16[8,80,128]{2,1,0:T(8,128)(2,1)S(1)}, bf16[8,80,128]{2,1,0:T(8,128)(2,1)S(1)}, u32[]{:S(2)}, u32[]{:S(2)}) collective-permute-start(bf16[8,80,128]{2,1,0:T(8,128)(2,1)S(1)} %sum_other.2), channel_id=1, source_target_pairs={{0,4},{1,5},{2,6},{3,7},{4,0},{5,1},{6,2},{7,3},{8,12},{9,13},{10,... | collective-permute-start | bytes 491528 | tf_op jit(solution)/shard_map/ppermute | solution.py:395
  79.0 3.3 %collective-permute-start.15 = (bf16[8,48,128]{2,1,0:T(8,128)(2,1)S(1)}, bf16[8,48,128]{2,1,0:T(8,128)(2,1)S(1)}, u32[]{:S(2)}, u32[]{:S(2)}) collective-permute-start(bf16[8,48,128]{2,1,0:T(8,128)(2,1)S(1)} %sum_other.3), channel_id=1, source_target_pairs={{0,4},{1,5},{2,6},{3,7},{4,0},{5,1},{6,2},{7,3},{8,12},{9,13},{10,... | collective-permute-start | bytes 294920 | tf_op jit(solution)/shard_map/ppermute | solution.py:395
  82.3 6.4 %collective-permute-done.15.refs_8_ = bf16[8,48,128]{2,1,0:T(8,128)(2,1)S(1)} collective-permute-done((bf16[8,48,128]{2,1,0:T(8,128)(2,1)S(1)}, bf16[8,48,128]{2,1,0:T(8,128)(2,1)S(1)}, u32[]{:S(2)}, u32[]{:S(2)}) %collective-permute-start.15) | collective-permute-done | bytes 98336 | tf_op jit(solution)/shard_map/ppermute | solution.py:395
  88.7 1.6 %row_level.1 = bf16[8,128,128]{2,1,0:T(8,128)(2,1)} custom-call(s32[1]{0:T(128)} %bitcast.me_ref, s32[64]{0:T(128)S(1)} %copy-done.4, bf16[64,128,128]{2,1,0:T(8,128)(2,1)S(1)} %copy-done, bf16[16,80,128]{2,1,0:T(8,128)(2,1)S(1)} %get-tuple-element.40.refs_0_, bf16[16,80,128]{2,1,0:T(8,128)(2,1)S(1)} %collective-permute-done.7.refs_1_, ...), custom_call_target="tpu_custom_call" | custom-call | flops 33554432 | bytes 1048576 | tf_op jit(solution)/shard_map/row_level/pallas_call | solution.py:375
  (40 shorter events, 5.5 us)
Async XLA Ops:
  6.0 12.3 %copy-start.7 = (bf16[24,48,128]{2,1,0:T(8,128)(2,1)S(1)}, bf16[24,48,128]{2,1,0:T(8,128)(2,1)}, u32[]{:S(2)}) copy-start(bf16[24,48,128]{2,1,0:T(8,128)(2,1)} %get-tuple-element.34.refs_0_) | copy-start | bytes 884740
  6.0 12.2 %collective-permute-start = (bf16[16,48,128]{2,1,0:T(8,128)(2,1)}, bf16[16,48,128]{2,1,0:T(8,128)(2,1)S(1)}, u32[]{:S(2)}, u32[]{:S(2)}) collective-permute-start(bf16[16,48,128]{2,1,0:T(8,128)(2,1)} %get-tuple-element.33), channel_id=1, source_target_pairs={{0,192},{8,200},{16,208},{24,216},{32,224},{40,232},{48,240},{56,2... | collective-permute-start | bytes 589832 | tf_op jit(solution)/shard_map/ppermute | solution.py:399
  8.0 40.9 %all-to-all-start = ((bf16[64,80,128]{2,1,0:T(8,128)(2,1)}), bf16[64,80,128]{2,1,0:T(8,128)(2,1)S(1)}, u32[]{:S(2)}, u32[]{:S(2)}) async-start(bf16[64,80,128]{2,1,0:T(8,128)(2,1)} %get-tuple-element.29), calls=%async_computation | async-start | bytes 2621440 | tf_op jit(solution)/shard_map/all_to_all | solution.py:416
  18.3 8.0 %copy-start.1 = (bf16[1,64,128,128]{3,2,1,0:T(8,128)(2,1)S(1)}, bf16[1,64,128,128]{3,2,1,0:T(8,128)(2,1)}, u32[]{:S(2)}) copy-start(bf16[1,64,128,128]{3,2,1,0:T(8,128)(2,1)} %param.12) | copy-start | bytes 6291460
  18.3 1.8 %collective-permute-start.1 = (bf16[32,48,128]{2,1,0:T(8,128)(2,1)S(1)}, bf16[32,48,128]{2,1,0:T(8,128)(2,1)S(1)}, u32[]{:S(2)}, u32[]{:S(2)}) collective-permute-start(bf16[32,48,128]{2,1,0:T(8,128)(2,1)S(1)} %regroup.3), channel_id=1, source_target_pairs={{0,8},{8,0},{16,24},{24,16},{32,40},{40,32},{48,56},{56,48},{64,72... | collective-permute-start | bytes 1179656 | tf_op jit(solution)/shard_map/ppermute | solution.py:399
  20.2 28.8 %copy-start.8 = (s32[1,64]{1,0:T(1,128)S(1)}, s32[1,64]{1,0:T(1,128)}, u32[]{:S(2)}) copy-start(s32[1,64]{1,0:T(1,128)} %param.13) | copy-start | bytes 772
  20.2 11.4 %collective-permute-start.2 = (bf16[16,48,128]{2,1,0:T(8,128)(2,1)S(1)}, bf16[16,48,128]{2,1,0:T(8,128)(2,1)S(1)}, u32[]{:S(2)}, u32[]{:S(2)}) collective-permute-start(bf16[16,48,128]{2,1,0:T(8,128)(2,1)S(1)} %get-tuple-element.35), channel_id=1, source_target_pairs={{0,16},{8,24},{16,0},{24,8},{32,48},{40,56},{48,32},{56,40},{64,80... | collective-permute-start | bytes 589832 | tf_op jit(solution)/shard_map/ppermute | solution.py:399
  21.6 20.8 %collective-permute-start.3 = (bf16[16,48,128]{2,1,0:T(8,128)(2,1)S(1)}, bf16[16,48,128]{2,1,0:T(8,128)(2,1)S(1)}, u32[]{:S(2)}, u32[]{:S(2)}) collective-permute-start(bf16[16,48,128]{2,1,0:T(8,128)(2,1)S(1)} %get-tuple-element.36), channel_id=1, source_target_pairs={{0,32},{8,40},{16,48},{24,56},{32,0},{40,8},{48,16},{56,24},{64,96... | collective-permute-start | bytes 589832 | tf_op jit(solution)/shard_map/ppermute | solution.py:399
  26.3 17.1 %collective-permute-start.4 = (bf16[16,48,128]{2,1,0:T(8,128)(2,1)S(1)}, bf16[16,48,128]{2,1,0:T(8,128)(2,1)S(1)}, u32[]{:S(2)}, u32[]{:S(2)}) collective-permute-start(bf16[16,48,128]{2,1,0:T(8,128)(2,1)S(1)} %get-tuple-element.37), channel_id=1, source_target_pairs={{0,48},{8,56},{16,32},{24,40},{32,16},{40,24},{48,0},{56,8},{64,11... | collective-permute-start | bytes 589832 | tf_op jit(solution)/shard_map/ppermute | solution.py:399
  44.2 14.9 %collective-permute-start.10 = (bf16[16,48,128]{2,1,0:T(8,128)(2,1)}, bf16[16,48,128]{2,1,0:T(8,128)(2,1)}, u32[]{:S(2)}, u32[]{:S(2)}) collective-permute-start(bf16[16,48,128]{2,1,0:T(8,128)(2,1)} %get-tuple-element.46), channel_id=1, source_target_pairs={{0,64},{8,72},{16,80},{24,88},{32,96},{40,104},{48,112},{56,120},{... | collective-permute-start | bytes 589832 | tf_op jit(solution)/shard_map/ppermute | solution.py:399
  44.2 14.9 %collective-permute-start.11 = (bf16[16,48,128]{2,1,0:T(8,128)(2,1)}, bf16[16,48,128]{2,1,0:T(8,128)(2,1)}, u32[]{:S(2)}, u32[]{:S(2)}) collective-permute-start(bf16[16,48,128]{2,1,0:T(8,128)(2,1)} %get-tuple-element.47), channel_id=1, source_target_pairs={{0,128},{8,136},{16,144},{24,152},{32,160},{40,168},{48,176},{56,1... | collective-permute-start | bytes 589832 | tf_op jit(solution)/shard_map/ppermute | solution.py:399
  49.0 3.0 %copy-start.6 = (bf16[48,128,128]{2,1,0:T(8,128)(2,1)S(1)}, bf16[48,128,128]{2,1,0:T(8,128)(2,1)}, u32[]{:S(2)}) copy-start(bf16[48,128,128]{2,1,0:T(8,128)(2,1)} %copy-done.5) | copy-start | bytes 4718596
  49.8 5.4 %collective-permute-start.5 = (bf16[8,80,128]{2,1,0:T(8,128)(2,1)S(1)}, bf16[8,80,128]{2,1,0:T(8,128)(2,1)S(1)}, u32[]{:S(2)}, u32[]{:S(2)}) collective-permute-start(bf16[8,80,128]{2,1,0:T(8,128)(2,1)S(1)} %get-tuple-element.39.after_ref), channel_id=1, source_target_pairs={{0,1},{1,2},{2,3},{3,0},{4,5},{5,6},{6,7},{7,4},{8,9},{9,10},{10,1... | collective-permute-start | bytes 491528 | tf_op jit(solution)/shard_map/ppermute | solution.py:390
  50.4 6.5 %collective-permute-start.6 = (bf16[8,80,128]{2,1,0:T(8,128)(2,1)S(1)}, bf16[8,80,128]{2,1,0:T(8,128)(2,1)S(1)}, u32[]{:S(2)}, u32[]{:S(2)}) collective-permute-start(bf16[8,80,128]{2,1,0:T(8,128)(2,1)S(1)} %get-tuple-element.43), channel_id=1, source_target_pairs={{0,3},{1,0},{2,1},{3,2},{4,7},{5,4},{6,5},{7,6},{8,11},{9,8},{10,9... | collective-permute-start | bytes 491528 | tf_op jit(solution)/shard_map/ppermute | solution.py:390
  51.9 7.2 %copy-start.2 = (bf16[1,64,128,128]{3,2,1,0:T(8,128)(2,1)S(1)}, bf16[1,64,128,128]{3,2,1,0:T(8,128)(2,1)}, u32[]{:S(2)}) copy-start(bf16[1,64,128,128]{3,2,1,0:T(8,128)(2,1)} %param.12) | copy-start | bytes 6291460
  57.0 10.3 %collective-permute-start.7 = (bf16[16,80,128]{2,1,0:T(8,128)(2,1)S(1)}, bf16[16,80,128]{2,1,0:T(8,128)(2,1)S(1)}, u32[]{:S(2)}, u32[]{:S(2)}) collective-permute-start(bf16[16,80,128]{2,1,0:T(8,128)(2,1)S(1)} %get-tuple-element.44), channel_id=1, source_target_pairs={{0,1},{1,2},{2,3},{3,0},{4,5},{5,6},{6,7},{7,4},{8,9},{9,10},{10,1... | collective-permute-start | bytes 983048 | tf_op jit(solution)/shard_map/ppermute | solution.py:390
  57.3 13.6 %collective-permute-start.8 = (bf16[16,80,128]{2,1,0:T(8,128)(2,1)S(1)}, bf16[16,80,128]{2,1,0:T(8,128)(2,1)S(1)}, u32[]{:S(2)}, u32[]{:S(2)}) collective-permute-start(bf16[16,80,128]{2,1,0:T(8,128)(2,1)S(1)} %get-tuple-element.45), channel_id=1, source_target_pairs={{0,3},{1,0},{2,1},{3,2},{4,7},{5,4},{6,5},{7,6},{8,11},{9,8},{10,9... | collective-permute-start | bytes 983048 | tf_op jit(solution)/shard_map/ppermute | solution.py:390
  59.1 29.6 %copy-start = (bf16[64,128,128]{2,1,0:T(8,128)(2,1)S(1)}, bf16[64,128,128]{2,1,0:T(8,128)(2,1)}, u32[]{:S(2)}) copy-start(bf16[64,128,128]{2,1,0:T(8,128)(2,1)} %w_ref.3) | copy-start | bytes 6291460
  59.1 29.6 %copy-start.4 = (s32[64]{0:T(128)S(1)}, s32[64]{0:T(128)}, u32[]{:S(2)}) copy-start(s32[64]{0:T(128)} %rank_ref.3) | copy-start | bytes 772
  61.1 17.9 %collective-permute-start.12 = (bf16[16,48,128]{2,1,0:T(8,128)(2,1)S(1)}, bf16[16,48,128]{2,1,0:T(8,128)(2,1)S(1)}, u32[]{:S(2)}, u32[]{:S(2)}) collective-permute-start(bf16[16,48,128]{2,1,0:T(8,128)(2,1)S(1)} %get-tuple-element.50), channel_id=1, source_target_pairs={{0,2},{1,3},{2,0},{3,1},{4,6},{5,7},{6,4},{7,5},{8,10},{9,11},{10,... | collective-permute-start | bytes 589832 | tf_op jit(solution)/shard_map/ppermute | solution.py:390
  62.4 16.6 %collective-permute-start.13 = (bf16[16,48,128]{2,1,0:T(8,128)(2,1)S(1)}, bf16[16,48,128]{2,1,0:T(8,128)(2,1)S(1)}, u32[]{:S(2)}, u32[]{:S(2)}) collective-permute-start(bf16[16,48,128]{2,1,0:T(8,128)(2,1)S(1)} %get-tuple-element.51), channel_id=1, source_target_pairs={{0,1},{1,2},{2,3},{3,0},{4,5},{5,6},{6,7},{7,4},{8,9},{9,10},{10,1... | collective-permute-start | bytes 589832 | tf_op jit(solution)/shard_map/ppermute | solution.py:390
  64.2 14.8 %collective-permute-start.14 = (bf16[16,48,128]{2,1,0:T(8,128)(2,1)S(1)}, bf16[16,48,128]{2,1,0:T(8,128)(2,1)S(1)}, u32[]{:S(2)}, u32[]{:S(2)}) collective-permute-start(bf16[16,48,128]{2,1,0:T(8,128)(2,1)S(1)} %get-tuple-element.52), channel_id=1, source_target_pairs={{0,3},{1,0},{2,1},{3,2},{4,7},{5,4},{6,5},{7,6},{8,11},{9,8},{10,9... | collective-permute-start | bytes 589832 | tf_op jit(solution)/shard_map/ppermute | solution.py:390
  71.0 17.7 %collective-permute-start.9 = (bf16[8,80,128]{2,1,0:T(8,128)(2,1)S(1)}, bf16[8,80,128]{2,1,0:T(8,128)(2,1)S(1)}, u32[]{:S(2)}, u32[]{:S(2)}) collective-permute-start(bf16[8,80,128]{2,1,0:T(8,128)(2,1)S(1)} %sum_other.2), channel_id=1, source_target_pairs={{0,4},{1,5},{2,6},{3,7},{4,0},{5,1},{6,2},{7,3},{8,12},{9,13},{10,... | collective-permute-start | bytes 491528 | tf_op jit(solution)/shard_map/ppermute | solution.py:395
  79.0 9.7 %collective-permute-start.15 = (bf16[8,48,128]{2,1,0:T(8,128)(2,1)S(1)}, bf16[8,48,128]{2,1,0:T(8,128)(2,1)S(1)}, u32[]{:S(2)}, u32[]{:S(2)}) collective-permute-start(bf16[8,48,128]{2,1,0:T(8,128)(2,1)S(1)} %sum_other.3), channel_id=1, source_target_pairs={{0,4},{1,5},{2,6},{3,7},{4,0},{5,1},{6,2},{7,3},{8,12},{9,13},{10,... | collective-permute-start | bytes 294920 | tf_op jit(solution)/shard_map/ppermute | solution.py:395
  (2 other events, 3.0 us)

commit v8 on v7

--- a/solution.py
+++ b/solution.py
@@ -296,26 +296,29 @@
     )(right, left, from_left, from_right)
 
 
-def stepped_kernel(row_ref, me_ref, rank_ref, w_ref, *refs):
-    pieces, out_refs, inner_buf = refs[:N_PLANE], refs[N_PLANE:-1], refs[-1]
+def stepped_kernel(row_ref, me_ref, rank_ref, far_ref, near_ref, *refs):
+    pieces, out_refs, block_buf = refs[:N_PLANE], refs[N_PLANE:-1], refs[-1]
     for k in range(N_PLANE):
         for m in range(N_Y):
             for e in range(N_CORE):
-                for i in range(Q):
-                    b = (row_ref[0] ^ flip(k, m, e)) * Q + i
-                    block = pieces[k][(m * N_CORE + e) * Q + i]
-                    inner_buf[b] = masked_dot(block, w_ref[b], rank_ref[b]).astype(BF16)
-    for d, out_ref in enumerate(out_refs):
+                b = (row_ref[0] ^ flip(k, m, e)) * Q
+                at = (m * N_CORE + e) * Q
+                block_buf[pl.ds(b, Q)] = pieces[k][at : at + Q]
+    for n, d in enumerate((2, 1, 3, 0)):
         for h in range(N_Z):
             base = (h * N_X + lax.rem(me_ref[0] + d, N_X)) * STEP
-            out_ref[h * STEP : (h + 1) * STEP] = inner_buf[pl.ds(base, STEP)]
-
-
-def mid_stepped(rows, row, me, ranks, factors, pieces):
+            w_ref, slot = (far_ref, h) if n == 0 else (near_ref, (n - 1) * N_Z + h)
+            for j in range(STEP):
+                factors = w_ref[slot * STEP + j]
+                inner = masked_dot(block_buf[base + j], factors, rank_ref[base + j])
+                out_refs[d][h * STEP + j] = inner.astype(BF16)
+
+
+def mid_stepped(rows, row, me, ranks, far_factors, near_factors, pieces):
     return pl.pallas_call(
         stepped_kernel,
         out_shape=[jax.ShapeDtypeStruct((N_Z * STEP, rows, BW), BF16)] * N_X,
-        in_specs=[SMEM, SMEM, SMEM, VMEM] + [VMEM] * N_PLANE,
+        in_specs=[SMEM, SMEM, SMEM, VMEM, VMEM] + [VMEM] * N_PLANE,
         out_specs=[VMEM] * N_X,
         scratch_shapes=[pltpu.VMEM((PB, rows, BW), BF16)],
         compiler_params=SMALL,
@@ -325,7 +328,7 @@
             transcendentals=0,
         ),
         name="mid_stepped",
-    )(row, me, ranks, factors, *pieces)
+    )(row, me, ranks, far_factors, near_factors, *pieces)
 
 
 def total_of(refs, half):
@@ -355,20 +358,25 @@
 
 
 def row_kernel(me_ref, rank_ref, w_ref, *refs):
-    out_ref = refs[-1]
+    out_ref, out_buf, sems = refs[-3:]
     base = me_ref[0] * OWN
     half = pl.ds(lax.div(me_ref[0], N_X) * STEP, STEP)
-    start = 0
-    for rows, near, far in (
-        (CHUNKS[0], refs[:3], refs[3]),
-        (CHUNKS[1], refs[4 : 4 + N_X], refs[4 + N_X]),
-    ):
-        total = total_of(near, half) + far[...].astype(jnp.float32)
-        for j in range(0, OWN, 2):
+    totals = []
+    for near, far in ((refs[:3], refs[3]), (refs[4 : 4 + N_X], refs[4 + N_X])):
+        totals.append(total_of(near, half) + far[...].astype(jnp.float32))
+    copies = []
+    for j in range(0, OWN, 2):
+        start = 0
+        for total, rows in zip(totals, CHUNKS):
             for i, block in enumerate(pair(total[j], total[j + 1])):
                 product = masked_dot(block, w_ref[base + j + i], rank_ref[base + j + i])
-                out_ref[j + i, start : start + rows] = product.astype(BF16)
-        start += rows
+                out_buf[j + i, start : start + rows] = product.astype(BF16)
+            start += rows
+        two = pl.ds(j, 2)
+        copies.append(pltpu.make_async_copy(out_buf.at[two], out_ref.at[two], sems.at[j // 2]))
+        copies[-1].start()
+    for copy in copies:
+        copy.wait()
 
 
 def row_level(me, ranks, factors, parts):
@@ -376,7 +384,11 @@
         row_kernel,
         out_shape=jax.ShapeDtypeStruct((OWN, R, BW), BF16),
         in_specs=[SMEM, SMEM, VMEM] + [VMEM] * len(parts),
-        out_specs=VMEM,
+        out_specs=ANY,
+        scratch_shapes=[
+            pltpu.VMEM((OWN, R, BW), BF16),
+            pltpu.SemaphoreType.DMA((OWN // 2,)),
+        ],
         compiler_params=SMALL,
         cost_estimate=pl.CostEstimate(
             flops=2 * OWN * R * BW * BW, bytes_accessed=2**20, transcendentals=0
@@ -443,7 +455,9 @@
     near = [own, around_x(right, 1), around_x(left, 3)]
     parts = near + [across_z(sum_other(straight_rows, me, near))]
 
-    inner = mid_stepped(stepped_rows, row, me, ranks, factors, planes)
+    inner = mid_stepped(
+        stepped_rows, row, me, ranks, far_factors, near_factors, planes
+    )
     near = [inner[0]] + [around_x(inner[d], d) for d in (2, 1, 3)]
     parts += near + [across_z(sum_other(stepped_rows, me, near))]
     return row_level(me, row_ranks, row_factors, parts)

time: 90.6 us -> 90.7 us (level)
    ppermute x7, waiting for transfers between devices: 10.4 us -> 9.29 us  [around_x(): return lax.ppermute(value, 'col', pairs)]
where the time goes in v8:
time: 90.7 us; the launch traced here: 90.5 us
  starting transfers between devices  40.1 us (44%)
  waiting for transfers between devices  36.1 us (40%)
  Pallas kernels  12.8 us (14%)
  local copies, waits for them, and re-layouts  1.21 us (1%)
    ppermute x7, waiting for transfers between devices, across_row(): lax.ppermute(value, 'row', [(r, r ^ flip(k, m, e)) for r in range(N_PLANE...  20.3 us
    ppermute x7, starting transfers between devices, across_row(): lax.ppermute(value, 'row', [(r, r ^ flip(k, m, e)) for r in range(N_PLANE...  13 us
    ppermute x2, starting transfers between devices, across_z(): lax.ppermute(value, 'col', [(i, (i + half) % (2 * half)) for i in range(2...  11.9 us
    ppermute x7, waiting for transfers between devices, around_x(): return lax.ppermute(value, 'col', pairs)  9.29 us
    ppermute x7, starting transfers between devices, around_x(): return lax.ppermute(value, 'col', pairs)  7.69 us
    all_to_all x1, starting transfers between devices, shards(): lax.all_to_all(middle, 'row', split_axis=0, concat_axis=0, tiled=True)  7.45 us
    ppermute x2, waiting for transfers between devices, across_z(): lax.ppermute(value, 'col', [(i, (i + half) % (2 * half)) for i in range(2...  6.59 us
    pallas_call x1, Pallas kernels, col_levels(): pl.pallas_call(col_kernel, out_shape=[jax.ShapeDtypeStruct((PB, straight,...  6.02 us
  transfers between devices with their start and end apart: 17, of which 10 were waited for; matrix products, arithmetic and copies ran while one was open for 0% of the time, Pallas kernels for 6%

profile of v8, /device:TPU:38, one launch (start us, length us, event | category | flops | bytes accessed | tf_op | source)
XLA Modules:
  0.0 90.5 jit_solution(15617049405663711746)
XLA Ops:
  0.0 6.0 %col_levels.1 = (bf16[64,80,128]{2,1,0:T(8,128)(2,1)}, bf16[16,48,128]{2,1,0:T(8,128)(2,1)}, bf16[24,48,128]{2,1,0:T(8,128)(2,1)}, bf16[24,48,128]{2,1,0:T(8,128)(2,1)}) custom-call(s32[1]{0:T(128)} %bitcast.2.row_ref, s32[1]{0:T(128)} %bitcast.me_ref, s32[64]{0:T(128)} %bitcast.9, s32[2,64]{1,0:T(2,128)} %rank_ref.2, bf16[64,128,128]{2,1,0:T(8,128)(2,1)} %z_ref.1, ...), custom_call_target="tpu_custom_call" | custom-call | flops 536870912 | bytes 8388608 | tf_op jit(solution)/shard_map/col_levels/pallas_call | solution.py:120
  6.0 2.0 %collective-permute-start = (bf16[16,48,128]{2,1,0:T(8,128)(2,1)}, bf16[16,48,128]{2,1,0:T(8,128)(2,1)S(1)}, u32[]{:S(2)}, u32[]{:S(2)}) collective-permute-start(bf16[16,48,128]{2,1,0:T(8,128)(2,1)} %get-tuple-element.33), channel_id=1, source_target_pairs={{0,192},{8,200},{16,208},{24,216},{32,224},{40,232},{48,240},{56,2... | collective-permute-start | bytes 589832 | tf_op jit(solution)/shard_map/ppermute | solution.py:411
  8.0 7.4 %all-to-all-start = ((bf16[64,80,128]{2,1,0:T(8,128)(2,1)}), bf16[64,80,128]{2,1,0:T(8,128)(2,1)S(1)}, u32[]{:S(2)}, u32[]{:S(2)}) async-start(bf16[64,80,128]{2,1,0:T(8,128)(2,1)} %get-tuple-element.29), calls=%async_computation | async-start | bytes 2621440 | tf_op jit(solution)/shard_map/all_to_all | solution.py:428
  15.5 2.8 %collective-permute-done.refs_1_ = bf16[16,48,128]{2,1,0:T(8,128)(2,1)S(1)} collective-permute-done((bf16[16,48,128]{2,1,0:T(8,128)(2,1)}, bf16[16,48,128]{2,1,0:T(8,128)(2,1)S(1)}, u32[]{:S(2)}, u32[]{:S(2)}) %collective-permute-start) | collective-permute-done | bytes 196640 | tf_op jit(solution)/shard_map/ppermute | solution.py:411
  18.4 1.7 %collective-permute-done.1.refs_2_ = bf16[32,48,128]{2,1,0:T(8,128)(2,1)S(1)} collective-permute-done((bf16[32,48,128]{2,1,0:T(8,128)(2,1)S(1)}, bf16[32,48,128]{2,1,0:T(8,128)(2,1)S(1)}, u32[]{:S(2)}, u32[]{:S(2)}) %collective-permute-start.1) | collective-permute-done | bytes 393248 | tf_op jit(solution)/shard_map/ppermute | solution.py:411
  20.2 1.4 %collective-permute-start.2 = (bf16[16,48,128]{2,1,0:T(8,128)(2,1)S(1)}, bf16[16,48,128]{2,1,0:T(8,128)(2,1)S(1)}, u32[]{:S(2)}, u32[]{:S(2)}) collective-permute-start(bf16[16,48,128]{2,1,0:T(8,128)(2,1)S(1)} %get-tuple-element.35), channel_id=1, source_target_pairs={{0,16},{8,24},{16,0},{24,8},{32,48},{40,56},{48,32},{56,40},{64,80... | collective-permute-start | bytes 589832 | tf_op jit(solution)/shard_map/ppermute | solution.py:411
  21.6 4.7 %collective-permute-start.3 = (bf16[16,48,128]{2,1,0:T(8,128)(2,1)S(1)}, bf16[16,48,128]{2,1,0:T(8,128)(2,1)S(1)}, u32[]{:S(2)}, u32[]{:S(2)}) collective-permute-start(bf16[16,48,128]{2,1,0:T(8,128)(2,1)S(1)} %get-tuple-element.36), channel_id=1, source_target_pairs={{0,32},{8,40},{16,48},{24,56},{32,0},{40,8},{48,16},{56,24},{64,96... | collective-permute-start | bytes 589832 | tf_op jit(solution)/shard_map/ppermute | solution.py:411
  27.6 4.0 %collective-permute-done.2.refs_3_ = bf16[16,48,128]{2,1,0:T(8,128)(2,1)S(1)} collective-permute-done((bf16[16,48,128]{2,1,0:T(8,128)(2,1)S(1)}, bf16[16,48,128]{2,1,0:T(8,128)(2,1)S(1)}, u32[]{:S(2)}, u32[]{:S(2)}) %collective-permute-start.2) | collective-permute-done | bytes 196640 | tf_op jit(solution)/shard_map/ppermute | solution.py:411
  31.6 10.8 %collective-permute-done.3.refs_4_ = bf16[16,48,128]{2,1,0:T(8,128)(2,1)S(1)} collective-permute-done((bf16[16,48,128]{2,1,0:T(8,128)(2,1)S(1)}, bf16[16,48,128]{2,1,0:T(8,128)(2,1)S(1)}, u32[]{:S(2)}, u32[]{:S(2)}) %collective-permute-start.3) | collective-permute-done | bytes 196640 | tf_op jit(solution)/shard_map/ppermute | solution.py:411
  44.2 4.8 %collective-permute-start.11 = (bf16[16,48,128]{2,1,0:T(8,128)(2,1)}, bf16[16,48,128]{2,1,0:T(8,128)(2,1)}, u32[]{:S(2)}, u32[]{:S(2)}) collective-permute-start(bf16[16,48,128]{2,1,0:T(8,128)(2,1)} %get-tuple-element.47), channel_id=1, source_target_pairs={{0,128},{8,136},{16,144},{24,152},{32,160},{40,168},{48,176},{56,1... | collective-permute-start | bytes 589832 | tf_op jit(solution)/shard_map/ppermute | solution.py:411
  50.4 1.5 %collective-permute-start.6 = (bf16[8,80,128]{2,1,0:T(8,128)(2,1)S(1)}, bf16[8,80,128]{2,1,0:T(8,128)(2,1)S(1)}, u32[]{:S(2)}, u32[]{:S(2)}) collective-permute-start(bf16[8,80,128]{2,1,0:T(8,128)(2,1)S(1)} %get-tuple-element.43), channel_id=1, source_target_pairs={{0,3},{1,0},{2,1},{3,2},{4,7},{5,4},{6,5},{7,6},{8,11},{9,8},{10,9... | collective-permute-start | bytes 491528 | tf_op jit(solution)/shard_map/ppermute | solution.py:402
  51.9 1.2 %mid_near.1 = (bf16[16,80,128]{2,1,0:T(8,128)(2,1)S(1)}, bf16[16,80,128]{2,1,0:T(8,128)(2,1)S(1)}, bf16[16,80,128]{2,1,0:T(8,128)(2,1)S(1)}) custom-call(s32[1]{0:T(128)} %bitcast.me_ref, s32[64]{0:T(128)S(1)} %bitcast.7, bf16[64,80,128]{2,1,0:T(8,128)(2,1)S(1)} %all-to-all-done.z_ref, bf16[48,128,128]{2,1,0:T(8,128)(2,1)S(1)} %copy-done.5, ...), custom_call_target="tpu_custom_call" | custom-call | flops 100125827072 | bytes 3538944 | tf_op jit(solution)/shard_map/mid_near/pallas_call | solution.py:253
  53.1 2.1 %collective-permute-done.5.from_left_ref = bf16[8,80,128]{2,1,0:T(8,128)(2,1)S(1)} collective-permute-done((bf16[8,80,128]{2,1,0:T(8,128)(2,1)S(1)}, bf16[8,80,128]{2,1,0:T(8,128)(2,1)S(1)}, u32[]{:S(2)}, u32[]{:S(2)}) %collective-permute-start.5) | collective-permute-done | bytes 163872 | tf_op jit(solution)/shard_map/ppermute | solution.py:402
  55.2 1.7 %collective-permute-done.6.from_right_ref = bf16[8,80,128]{2,1,0:T(8,128)(2,1)S(1)} collective-permute-done((bf16[8,80,128]{2,1,0:T(8,128)(2,1)S(1)}, bf16[8,80,128]{2,1,0:T(8,128)(2,1)S(1)}, u32[]{:S(2)}, u32[]{:S(2)}) %collective-permute-start.6) | collective-permute-done | bytes 163872 | tf_op jit(solution)/shard_map/ppermute | solution.py:402
  57.3 1.8 %collective-permute-start.8 = (bf16[16,80,128]{2,1,0:T(8,128)(2,1)S(1)}, bf16[16,80,128]{2,1,0:T(8,128)(2,1)S(1)}, u32[]{:S(2)}, u32[]{:S(2)}) collective-permute-start(bf16[16,80,128]{2,1,0:T(8,128)(2,1)S(1)} %get-tuple-element.45), channel_id=1, source_target_pairs={{0,3},{1,0},{2,1},{3,2},{4,7},{5,4},{6,5},{7,6},{8,11},{9,8},{10,9... | collective-permute-start | bytes 983048 | tf_op jit(solution)/shard_map/ppermute | solution.py:402
  59.1 1.9 %mid_stepped.1 = (bf16[16,48,128]{2,1,0:T(8,128)(2,1)S(1)}, bf16[16,48,128]{2,1,0:T(8,128)(2,1)S(1)}, bf16[16,48,128]{2,1,0:T(8,128)(2,1)S(1)}, bf16[16,48,128]{2,1,0:T(8,128)(2,1)S(1)}) custom-call(s32[1]{0:T(128)} %bitcast.2.row_ref, s32[1]{0:T(128)} %bitcast.me_ref, s32[64]{0:T(128)S(1)} %bitcast.8, ...), custom_call_target="tpu_custom_call" | custom-call | flops 100100661248 | bytes 3670016 | tf_op jit(solution)/shard_map/mid_stepped/pallas_call | solution.py:318
  61.0 1.5 %collective-permute-start.12 = (bf16[16,48,128]{2,1,0:T(8,128)(2,1)S(1)}, bf16[16,48,128]{2,1,0:T(8,128)(2,1)S(1)}, u32[]{:S(2)}, u32[]{:S(2)}) collective-permute-start(bf16[16,48,128]{2,1,0:T(8,128)(2,1)S(1)} %get-tuple-element.50), channel_id=1, source_target_pairs={{0,2},{1,3},{2,0},{3,1},{4,6},{5,7},{6,4},{7,5},{8,10},{9,11},{10,... | collective-permute-start | bytes 589832 | tf_op jit(solution)/shard_map/ppermute | solution.py:402
  62.5 1.8 %collective-permute-start.13 = (bf16[16,48,128]{2,1,0:T(8,128)(2,1)S(1)}, bf16[16,48,128]{2,1,0:T(8,128)(2,1)S(1)}, u32[]{:S(2)}, u32[]{:S(2)}) collective-permute-start(bf16[16,48,128]{2,1,0:T(8,128)(2,1)S(1)} %get-tuple-element.51), channel_id=1, source_target_pairs={{0,1},{1,2},{2,3},{3,0},{4,5},{5,6},{6,7},{7,4},{8,9},{9,10},{10,1... | collective-permute-start | bytes 589832 | tf_op jit(solution)/shard_map/ppermute | solution.py:402
  64.5 2.8 %collective-permute-done.7.refs_1_ = bf16[16,80,128]{2,1,0:T(8,128)(2,1)S(1)} collective-permute-done((bf16[16,80,128]{2,1,0:T(8,128)(2,1)S(1)}, bf16[16,80,128]{2,1,0:T(8,128)(2,1)S(1)}, u32[]{:S(2)}, u32[]{:S(2)}) %collective-permute-start.7) | collective-permute-done | bytes 327712 | tf_op jit(solution)/shard_map/ppermute | solution.py:402
  67.3 2.7 %collective-permute-done.8.refs_2_ = bf16[16,80,128]{2,1,0:T(8,128)(2,1)S(1)} collective-permute-done((bf16[16,80,128]{2,1,0:T(8,128)(2,1)S(1)}, bf16[16,80,128]{2,1,0:T(8,128)(2,1)S(1)}, u32[]{:S(2)}, u32[]{:S(2)}) %collective-permute-start.8) | collective-permute-done | bytes 327712 | tf_op jit(solution)/shard_map/ppermute | solution.py:402
  70.1 8.9 %collective-permute-start.9 = (bf16[8,80,128]{2,1,0:T(8,128)(2,1)S(1)}, bf16[8,80,128]{2,1,0:T(8,128)(2,1)S(1)}, u32[]{:S(2)}, u32[]{:S(2)}) collective-permute-start(bf16[8,80,128]{2,1,0:T(8,128)(2,1)S(1)} %sum_other.2), channel_id=1, source_target_pairs={{0,4},{1,5},{2,6},{3,7},{4,0},{5,1},{6,2},{7,3},{8,12},{9,13},{10,... | collective-permute-start | bytes 491528 | tf_op jit(solution)/shard_map/ppermute | solution.py:407
  79.0 3.1 %collective-permute-start.15 = (bf16[8,48,128]{2,1,0:T(8,128)(2,1)S(1)}, bf16[8,48,128]{2,1,0:T(8,128)(2,1)S(1)}, u32[]{:S(2)}, u32[]{:S(2)}) collective-permute-start(bf16[8,48,128]{2,1,0:T(8,128)(2,1)S(1)} %sum_other.3), channel_id=1, source_target_pairs={{0,4},{1,5},{2,6},{3,7},{4,0},{5,1},{6,2},{7,3},{8,12},{9,13},{10,... | collective-permute-start | bytes 294920 | tf_op jit(solution)/shard_map/ppermute | solution.py:407
  82.1 6.6 %collective-permute-done.15.refs_8_ = bf16[8,48,128]{2,1,0:T(8,128)(2,1)S(1)} collective-permute-done((bf16[8,48,128]{2,1,0:T(8,128)(2,1)S(1)}, bf16[8,48,128]{2,1,0:T(8,128)(2,1)S(1)}, u32[]{:S(2)}, u32[]{:S(2)}) %collective-permute-start.15) | collective-permute-done | bytes 98336 | tf_op jit(solution)/shard_map/ppermute | solution.py:407
  88.7 1.6 %row_level.1 = bf16[8,128,128]{2,1,0:T(8,128)(2,1)} custom-call(s32[1]{0:T(128)} %bitcast.me_ref, s32[64]{0:T(128)S(1)} %copy-done.3, bf16[64,128,128]{2,1,0:T(8,128)(2,1)S(1)} %copy-done, bf16[16,80,128]{2,1,0:T(8,128)(2,1)S(1)} %get-tuple-element.40.refs_0_, bf16[16,80,128]{2,1,0:T(8,128)(2,1)S(1)} %collective-permute-done.7.refs_1_, ...), custom_call_target="tpu_custom_call" | custom-call | flops 33554432 | bytes 1048576 | tf_op jit(solution)/shard_map/row_level/pallas_call | solution.py:383
  (38 shorter events, 5.5 us)
Async XLA Ops:
  6.0 12.3 %copy-start.6 = (bf16[24,48,128]{2,1,0:T(8,128)(2,1)S(1)}, bf16[24,48,128]{2,1,0:T(8,128)(2,1)}, u32[]{:S(2)}) copy-start(bf16[24,48,128]{2,1,0:T(8,128)(2,1)} %get-tuple-element.34.refs_0_) | copy-start | bytes 884740
  6.0 12.2 %collective-permute-start = (bf16[16,48,128]{2,1,0:T(8,128)(2,1)}, bf16[16,48,128]{2,1,0:T(8,128)(2,1)S(1)}, u32[]{:S(2)}, u32[]{:S(2)}) collective-permute-start(bf16[16,48,128]{2,1,0:T(8,128)(2,1)} %get-tuple-element.33), channel_id=1, source_target_pairs={{0,192},{8,200},{16,208},{24,216},{32,224},{40,232},{48,240},{56,2... | collective-permute-start | bytes 589832 | tf_op jit(solution)/shard_map/ppermute | solution.py:411
  8.0 40.9 %all-to-all-start = ((bf16[64,80,128]{2,1,0:T(8,128)(2,1)}), bf16[64,80,128]{2,1,0:T(8,128)(2,1)S(1)}, u32[]{:S(2)}, u32[]{:S(2)}) async-start(bf16[64,80,128]{2,1,0:T(8,128)(2,1)} %get-tuple-element.29), calls=%async_computation | async-start | bytes 2621440 | tf_op jit(solution)/shard_map/all_to_all | solution.py:428
  18.3 1.8 %copy-start.2 = (bf16[24,48,128]{2,1,0:T(8,128)(2,1)S(1)}, bf16[24,48,128]{2,1,0:T(8,128)(2,1)}, u32[]{:S(2)}) copy-start(bf16[24,48,128]{2,1,0:T(8,128)(2,1)} %get-tuple-element.32.refs_0_) | copy-start | bytes 884740
  18.3 8.0 %copy-start.1 = (bf16[1,64,128,128]{3,2,1,0:T(8,128)(2,1)S(1)}, bf16[1,64,128,128]{3,2,1,0:T(8,128)(2,1)}, u32[]{:S(2)}) copy-start(bf16[1,64,128,128]{3,2,1,0:T(8,128)(2,1)} %param.12) | copy-start | bytes 6291460
  18.3 1.8 %collective-permute-start.1 = (bf16[32,48,128]{2,1,0:T(8,128)(2,1)S(1)}, bf16[32,48,128]{2,1,0:T(8,128)(2,1)S(1)}, u32[]{:S(2)}, u32[]{:S(2)}) collective-permute-start(bf16[32,48,128]{2,1,0:T(8,128)(2,1)S(1)} %regroup.3), channel_id=1, source_target_pairs={{0,8},{8,0},{16,24},{24,16},{32,40},{40,32},{48,56},{56,48},{64,72... | collective-permute-start | bytes 1179656 | tf_op jit(solution)/shard_map/ppermute | solution.py:411
  20.2 28.8 %copy-start.7 = (s32[1,64]{1,0:T(1,128)S(1)}, s32[1,64]{1,0:T(1,128)}, u32[]{:S(2)}) copy-start(s32[1,64]{1,0:T(1,128)} %param.13) | copy-start | bytes 772
  20.2 11.4 %collective-permute-start.2 = (bf16[16,48,128]{2,1,0:T(8,128)(2,1)S(1)}, bf16[16,48,128]{2,1,0:T(8,128)(2,1)S(1)}, u32[]{:S(2)}, u32[]{:S(2)}) collective-permute-start(bf16[16,48,128]{2,1,0:T(8,128)(2,1)S(1)} %get-tuple-element.35), channel_id=1, source_target_pairs={{0,16},{8,24},{16,0},{24,8},{32,48},{40,56},{48,32},{56,40},{64,80... | collective-permute-start | bytes 589832 | tf_op jit(solution)/shard_map/ppermute | solution.py:411
  21.6 20.8 %collective-permute-start.3 = (bf16[16,48,128]{2,1,0:T(8,128)(2,1)S(1)}, bf16[16,48,128]{2,1,0:T(8,128)(2,1)S(1)}, u32[]{:S(2)}, u32[]{:S(2)}) collective-permute-start(bf16[16,48,128]{2,1,0:T(8,128)(2,1)S(1)} %get-tuple-element.36), channel_id=1, source_target_pairs={{0,32},{8,40},{16,48},{24,56},{32,0},{40,8},{48,16},{56,24},{64,96... | collective-permute-start | bytes 589832 | tf_op jit(solution)/shard_map/ppermute | solution.py:411
  26.3 17.1 %collective-permute-start.4 = (bf16[16,48,128]{2,1,0:T(8,128)(2,1)S(1)}, bf16[16,48,128]{2,1,0:T(8,128)(2,1)S(1)}, u32[]{:S(2)}, u32[]{:S(2)}) collective-permute-start(bf16[16,48,128]{2,1,0:T(8,128)(2,1)S(1)} %get-tuple-element.37), channel_id=1, source_target_pairs={{0,48},{8,56},{16,32},{24,40},{32,16},{40,24},{48,0},{56,8},{64,11... | collective-permute-start | bytes 589832 | tf_op jit(solution)/shard_map/ppermute | solution.py:411
  44.2 14.9 %collective-permute-start.10 = (bf16[16,48,128]{2,1,0:T(8,128)(2,1)}, bf16[16,48,128]{2,1,0:T(8,128)(2,1)}, u32[]{:S(2)}, u32[]{:S(2)}) collective-permute-start(bf16[16,48,128]{2,1,0:T(8,128)(2,1)} %get-tuple-element.46), channel_id=1, source_target_pairs={{0,64},{8,72},{16,80},{24,88},{32,96},{40,104},{48,112},{56,120},{... | collective-permute-start | bytes 589832 | tf_op jit(solution)/shard_map/ppermute | solution.py:411
  44.2 14.9 %collective-permute-start.11 = (bf16[16,48,128]{2,1,0:T(8,128)(2,1)}, bf16[16,48,128]{2,1,0:T(8,128)(2,1)}, u32[]{:S(2)}, u32[]{:S(2)}) collective-permute-start(bf16[16,48,128]{2,1,0:T(8,128)(2,1)} %get-tuple-element.47), channel_id=1, source_target_pairs={{0,128},{8,136},{16,144},{24,152},{32,160},{40,168},{48,176},{56,1... | collective-permute-start | bytes 589832 | tf_op jit(solution)/shard_map/ppermute | solution.py:411
  49.0 3.0 %copy-start.5 = (bf16[48,128,128]{2,1,0:T(8,128)(2,1)S(1)}, bf16[48,128,128]{2,1,0:T(8,128)(2,1)}, u32[]{:S(2)}) copy-start(bf16[48,128,128]{2,1,0:T(8,128)(2,1)} %copy-done.4) | copy-start | bytes 4718596
  49.8 5.4 %collective-permute-start.5 = (bf16[8,80,128]{2,1,0:T(8,128)(2,1)S(1)}, bf16[8,80,128]{2,1,0:T(8,128)(2,1)S(1)}, u32[]{:S(2)}, u32[]{:S(2)}) collective-permute-start(bf16[8,80,128]{2,1,0:T(8,128)(2,1)S(1)} %get-tuple-element.39.after_ref), channel_id=1, source_target_pairs={{0,1},{1,2},{2,3},{3,0},{4,5},{5,6},{6,7},{7,4},{8,9},{9,10},{10,1... | collective-permute-start | bytes 491528 | tf_op jit(solution)/shard_map/ppermute | solution.py:402
  50.4 6.5 %collective-permute-start.6 = (bf16[8,80,128]{2,1,0:T(8,128)(2,1)S(1)}, bf16[8,80,128]{2,1,0:T(8,128)(2,1)S(1)}, u32[]{:S(2)}, u32[]{:S(2)}) collective-permute-start(bf16[8,80,128]{2,1,0:T(8,128)(2,1)S(1)} %get-tuple-element.43), channel_id=1, source_target_pairs={{0,3},{1,0},{2,1},{3,2},{4,7},{5,4},{6,5},{7,6},{8,11},{9,8},{10,9... | collective-permute-start | bytes 491528 | tf_op jit(solution)/shard_map/ppermute | solution.py:402
  57.0 10.4 %collective-permute-start.7 = (bf16[16,80,128]{2,1,0:T(8,128)(2,1)S(1)}, bf16[16,80,128]{2,1,0:T(8,128)(2,1)S(1)}, u32[]{:S(2)}, u32[]{:S(2)}) collective-permute-start(bf16[16,80,128]{2,1,0:T(8,128)(2,1)S(1)} %get-tuple-element.44), channel_id=1, source_target_pairs={{0,1},{1,2},{2,3},{3,0},{4,5},{5,6},{6,7},{7,4},{8,9},{9,10},{10,1... | collective-permute-start | bytes 983048 | tf_op jit(solution)/shard_map/ppermute | solution.py:402
  57.3 12.7 %collective-permute-start.8 = (bf16[16,80,128]{2,1,0:T(8,128)(2,1)S(1)}, bf16[16,80,128]{2,1,0:T(8,128)(2,1)S(1)}, u32[]{:S(2)}, u32[]{:S(2)}) collective-permute-start(bf16[16,80,128]{2,1,0:T(8,128)(2,1)S(1)} %get-tuple-element.45), channel_id=1, source_target_pairs={{0,3},{1,0},{2,1},{3,2},{4,7},{5,4},{6,5},{7,6},{8,11},{9,8},{10,9... | collective-permute-start | bytes 983048 | tf_op jit(solution)/shard_map/ppermute | solution.py:402
  59.1 29.6 %copy-start = (bf16[64,128,128]{2,1,0:T(8,128)(2,1)S(1)}, bf16[64,128,128]{2,1,0:T(8,128)(2,1)}, u32[]{:S(2)}) copy-start(bf16[64,128,128]{2,1,0:T(8,128)(2,1)} %w_ref.3) | copy-start | bytes 6291460
  59.1 29.6 %copy-start.3 = (s32[64]{0:T(128)S(1)}, s32[64]{0:T(128)}, u32[]{:S(2)}) copy-start(s32[64]{0:T(128)} %rank_ref.3) | copy-start | bytes 772
  61.0 17.9 %collective-permute-start.12 = (bf16[16,48,128]{2,1,0:T(8,128)(2,1)S(1)}, bf16[16,48,128]{2,1,0:T(8,128)(2,1)S(1)}, u32[]{:S(2)}, u32[]{:S(2)}) collective-permute-start(bf16[16,48,128]{2,1,0:T(8,128)(2,1)S(1)} %get-tuple-element.50), channel_id=1, source_target_pairs={{0,2},{1,3},{2,0},{3,1},{4,6},{5,7},{6,4},{7,5},{8,10},{9,11},{10,... | collective-permute-start | bytes 589832 | tf_op jit(solution)/shard_map/ppermute | solution.py:402
  62.5 16.5 %collective-permute-start.13 = (bf16[16,48,128]{2,1,0:T(8,128)(2,1)S(1)}, bf16[16,48,128]{2,1,0:T(8,128)(2,1)S(1)}, u32[]{:S(2)}, u32[]{:S(2)}) collective-permute-start(bf16[16,48,128]{2,1,0:T(8,128)(2,1)S(1)} %get-tuple-element.51), channel_id=1, source_target_pairs={{0,1},{1,2},{2,3},{3,0},{4,5},{5,6},{6,7},{7,4},{8,9},{9,10},{10,1... | collective-permute-start | bytes 589832 | tf_op jit(solution)/shard_map/ppermute | solution.py:402
  64.3 14.7 %collective-permute-start.14 = (bf16[16,48,128]{2,1,0:T(8,128)(2,1)S(1)}, bf16[16,48,128]{2,1,0:T(8,128)(2,1)S(1)}, u32[]{:S(2)}, u32[]{:S(2)}) collective-permute-start(bf16[16,48,128]{2,1,0:T(8,128)(2,1)S(1)} %get-tuple-element.52), channel_id=1, source_target_pairs={{0,3},{1,0},{2,1},{3,2},{4,7},{5,4},{6,5},{7,6},{8,11},{9,8},{10,9... | collective-permute-start | bytes 589832 | tf_op jit(solution)/shard_map/ppermute | solution.py:402
  70.1 18.6 %collective-permute-start.9 = (bf16[8,80,128]{2,1,0:T(8,128)(2,1)S(1)}, bf16[8,80,128]{2,1,0:T(8,128)(2,1)S(1)}, u32[]{:S(2)}, u32[]{:S(2)}) collective-permute-start(bf16[8,80,128]{2,1,0:T(8,128)(2,1)S(1)} %sum_other.2), channel_id=1, source_target_pairs={{0,4},{1,5},{2,6},{3,7},{4,0},{5,1},{6,2},{7,3},{8,12},{9,13},{10,... | collective-permute-start | bytes 491528 | tf_op jit(solution)/shard_map/ppermute | solution.py:407
  79.0 9.7 %collective-permute-start.15 = (bf16[8,48,128]{2,1,0:T(8,128)(2,1)S(1)}, bf16[8,48,128]{2,1,0:T(8,128)(2,1)S(1)}, u32[]{:S(2)}, u32[]{:S(2)}) collective-permute-start(bf16[8,48,128]{2,1,0:T(8,128)(2,1)S(1)} %sum_other.3), channel_id=1, source_target_pairs={{0,4},{1,5},{2,6},{3,7},{4,0},{5,1},{6,2},{7,3},{8,12},{9,13},{10,... | collective-permute-start | bytes 294920 | tf_op jit(solution)/shard_map/ppermute | solution.py:407
  (1 other events, 1.2 us)

commit v9 on v8

--- a/solution.py
+++ b/solution.py
@@ -439,12 +439,13 @@
             stepped_rows, for_planes(), N_PLANE, PIECE, pieces, HINT_PLANES, [far_factors]
         )
     )
+    sent = planes[1]
     for k in range(1, EARLY):
         planes[k] = across_row(planes[k], k, 0, 0)
 
     first, second = mid_part(
         far_kernel, "mid_far", straight_rows, [STEP, STEP], me, ranks, regrouped, far_factors,
-        planes[0],
+        sent,
     )
     right, left, own = mid_part(
         near_kernel, "mid_near", straight_rows, [N_Z * STEP] * 3, me, ranks, regrouped,

time: 90.7 us -> 90.7 us (level)
  no operation moved by 1% of the time
where the time goes in v9:
time: 90.7 us; the launch traced here: 90.5 us
  starting transfers between devices  40.1 us (44%)
  waiting for transfers between devices  36.1 us (40%)
  Pallas kernels  12.8 us (14%)
  local copies, waits for them, and re-layouts  1.21 us (1%)
    ppermute x7, waiting for transfers between devices, across_row(): lax.ppermute(value, 'row', [(r, r ^ flip(k, m, e)) for r in range(N_PLANE...  20.3 us
    ppermute x7, starting transfers between devices, across_row(): lax.ppermute(value, 'row', [(r, r ^ flip(k, m, e)) for r in range(N_PLANE...  13 us
    ppermute x2, starting transfers between devices, across_z(): lax.ppermute(value, 'col', [(i, (i + half) % (2 * half)) for i in range(2...  11.9 us
    ppermute x7, waiting for transfers between devices, around_x(): return lax.ppermute(value, 'col', pairs)  9.27 us
    ppermute x7, starting transfers between devices, around_x(): return lax.ppermute(value, 'col', pairs)  7.69 us
    all_to_all x1, starting transfers between devices, shards(): lax.all_to_all(middle, 'row', split_axis=0, concat_axis=0, tiled=True)  7.45 us
    ppermute x2, waiting for transfers between devices, across_z(): lax.ppermute(value, 'col', [(i, (i + half) % (2 * half)) for i in range(2...  6.6 us
    pallas_call x1, Pallas kernels, col_levels(): pl.pallas_call(col_kernel, out_shape=[jax.ShapeDtypeStruct((PB, straight,...  6.02 us
  transfers between devices with their start and end apart: 17, of which 10 were waited for; matrix products, arithmetic and copies ran while one was open for 0% of the time, Pallas kernels for 6%

profile of v9, /device:TPU:38, one launch (start us, length us, event | category | flops | bytes accessed | tf_op | source)
XLA Modules:
  0.0 90.5 jit_solution(109637132428498261)
XLA Ops:
  0.0 6.0 %col_levels.1 = (bf16[64,80,128]{2,1,0:T(8,128)(2,1)}, bf16[16,48,128]{2,1,0:T(8,128)(2,1)}, bf16[24,48,128]{2,1,0:T(8,128)(2,1)}, bf16[24,48,128]{2,1,0:T(8,128)(2,1)}) custom-call(s32[1]{0:T(128)} %bitcast.2.row_ref, s32[1]{0:T(128)} %bitcast.me_ref, s32[64]{0:T(128)} %bitcast.9, s32[2,64]{1,0:T(2,128)} %rank_ref.2, bf16[64,128,128]{2,1,0:T(8,128)(2,1)} %z_ref.1, ...), custom_call_target="tpu_custom_call" | custom-call | flops 536870912 | bytes 8388608 | tf_op jit(solution)/shard_map/col_levels/pallas_call | solution.py:120
  6.0 2.0 %collective-permute-start = (bf16[16,48,128]{2,1,0:T(8,128)(2,1)}, bf16[16,48,128]{2,1,0:T(8,128)(2,1)S(1)}, u32[]{:S(2)}, u32[]{:S(2)}) collective-permute-start(bf16[16,48,128]{2,1,0:T(8,128)(2,1)} %get-tuple-element.33), channel_id=1, source_target_pairs={{0,192},{8,200},{16,208},{24,216},{32,224},{40,232},{48,240},{56,2... | collective-permute-start | bytes 589832 | tf_op jit(solution)/shard_map/ppermute | solution.py:411
  8.0 7.4 %all-to-all-start = ((bf16[64,80,128]{2,1,0:T(8,128)(2,1)}), bf16[64,80,128]{2,1,0:T(8,128)(2,1)S(1)}, u32[]{:S(2)}, u32[]{:S(2)}) async-start(bf16[64,80,128]{2,1,0:T(8,128)(2,1)} %get-tuple-element.29), calls=%async_computation | async-start | bytes 2621440 | tf_op jit(solution)/shard_map/all_to_all | solution.py:428
  15.5 2.8 %collective-permute-done.refs_1_ = bf16[16,48,128]{2,1,0:T(8,128)(2,1)S(1)} collective-permute-done((bf16[16,48,128]{2,1,0:T(8,128)(2,1)}, bf16[16,48,128]{2,1,0:T(8,128)(2,1)S(1)}, u32[]{:S(2)}, u32[]{:S(2)}) %collective-permute-start) | collective-permute-done | bytes 196640 | tf_op jit(solution)/shard_map/ppermute | solution.py:411
  18.4 1.7 %collective-permute-done.1.refs_2_ = bf16[32,48,128]{2,1,0:T(8,128)(2,1)S(1)} collective-permute-done((bf16[32,48,128]{2,1,0:T(8,128)(2,1)S(1)}, bf16[32,48,128]{2,1,0:T(8,128)(2,1)S(1)}, u32[]{:S(2)}, u32[]{:S(2)}) %collective-permute-start.1) | collective-permute-done | bytes 393248 | tf_op jit(solution)/shard_map/ppermute | solution.py:411
  20.2 1.4 %collective-permute-start.2 = (bf16[16,48,128]{2,1,0:T(8,128)(2,1)S(1)}, bf16[16,48,128]{2,1,0:T(8,128)(2,1)S(1)}, u32[]{:S(2)}, u32[]{:S(2)}) collective-permute-start(bf16[16,48,128]{2,1,0:T(8,128)(2,1)S(1)} %get-tuple-element.35), channel_id=1, source_target_pairs={{0,16},{8,24},{16,0},{24,8},{32,48},{40,56},{48,32},{56,40},{64,80... | collective-permute-start | bytes 589832 | tf_op jit(solution)/shard_map/ppermute | solution.py:411
  21.6 4.7 %collective-permute-start.3 = (bf16[16,48,128]{2,1,0:T(8,128)(2,1)S(1)}, bf16[16,48,128]{2,1,0:T(8,128)(2,1)S(1)}, u32[]{:S(2)}, u32[]{:S(2)}) collective-permute-start(bf16[16,48,128]{2,1,0:T(8,128)(2,1)S(1)} %get-tuple-element.36), channel_id=1, source_target_pairs={{0,32},{8,40},{16,48},{24,56},{32,0},{40,8},{48,16},{56,24},{64,96... | collective-permute-start | bytes 589832 | tf_op jit(solution)/shard_map/ppermute | solution.py:411
  27.6 4.0 %collective-permute-done.2.refs_3_ = bf16[16,48,128]{2,1,0:T(8,128)(2,1)S(1)} collective-permute-done((bf16[16,48,128]{2,1,0:T(8,128)(2,1)S(1)}, bf16[16,48,128]{2,1,0:T(8,128)(2,1)S(1)}, u32[]{:S(2)}, u32[]{:S(2)}) %collective-permute-start.2) | collective-permute-done | bytes 196640 | tf_op jit(solution)/shard_map/ppermute | solution.py:411
  31.6 10.8 %collective-permute-done.3.refs_4_ = bf16[16,48,128]{2,1,0:T(8,128)(2,1)S(1)} collective-permute-done((bf16[16,48,128]{2,1,0:T(8,128)(2,1)S(1)}, bf16[16,48,128]{2,1,0:T(8,128)(2,1)S(1)}, u32[]{:S(2)}, u32[]{:S(2)}) %collective-permute-start.3) | collective-permute-done | bytes 196640 | tf_op jit(solution)/shard_map/ppermute | solution.py:411
  44.2 4.8 %collective-permute-start.11 = (bf16[16,48,128]{2,1,0:T(8,128)(2,1)}, bf16[16,48,128]{2,1,0:T(8,128)(2,1)}, u32[]{:S(2)}, u32[]{:S(2)}) collective-permute-start(bf16[16,48,128]{2,1,0:T(8,128)(2,1)} %get-tuple-element.47), channel_id=1, source_target_pairs={{0,128},{8,136},{16,144},{24,152},{32,160},{40,168},{48,176},{56,1... | collective-permute-start | bytes 589832 | tf_op jit(solution)/shard_map/ppermute | solution.py:411
  50.4 1.5 %collective-permute-start.6 = (bf16[8,80,128]{2,1,0:T(8,128)(2,1)S(1)}, bf16[8,80,128]{2,1,0:T(8,128)(2,1)S(1)}, u32[]{:S(2)}, u32[]{:S(2)}) collective-permute-start(bf16[8,80,128]{2,1,0:T(8,128)(2,1)S(1)} %get-tuple-element.43), channel_id=1, source_target_pairs={{0,3},{1,0},{2,1},{3,2},{4,7},{5,4},{6,5},{7,6},{8,11},{9,8},{10,9... | collective-permute-start | bytes 491528 | tf_op jit(solution)/shard_map/ppermute | solution.py:402
  51.9 1.2 %mid_near.1 = (bf16[16,80,128]{2,1,0:T(8,128)(2,1)S(1)}, bf16[16,80,128]{2,1,0:T(8,128)(2,1)S(1)}, bf16[16,80,128]{2,1,0:T(8,128)(2,1)S(1)}) custom-call(s32[1]{0:T(128)} %bitcast.me_ref, s32[64]{0:T(128)S(1)} %bitcast.7, bf16[64,80,128]{2,1,0:T(8,128)(2,1)S(1)} %all-to-all-done.z_ref, bf16[48,128,128]{2,1,0:T(8,128)(2,1)S(1)} %copy-done.5, ...), custom_call_target="tpu_custom_call" | custom-call | flops 100125827072 | bytes 3538944 | tf_op jit(solution)/shard_map/mid_near/pallas_call | solution.py:253
  53.2 2.1 %collective-permute-done.5.from_left_ref = bf16[8,80,128]{2,1,0:T(8,128)(2,1)S(1)} collective-permute-done((bf16[8,80,128]{2,1,0:T(8,128)(2,1)S(1)}, bf16[8,80,128]{2,1,0:T(8,128)(2,1)S(1)}, u32[]{:S(2)}, u32[]{:S(2)}) %collective-permute-start.5) | collective-permute-done | bytes 163872 | tf_op jit(solution)/shard_map/ppermute | solution.py:402
  55.2 1.7 %collective-permute-done.6.from_right_ref = bf16[8,80,128]{2,1,0:T(8,128)(2,1)S(1)} collective-permute-done((bf16[8,80,128]{2,1,0:T(8,128)(2,1)S(1)}, bf16[8,80,128]{2,1,0:T(8,128)(2,1)S(1)}, u32[]{:S(2)}, u32[]{:S(2)}) %collective-permute-start.6) | collective-permute-done | bytes 163872 | tf_op jit(solution)/shard_map/ppermute | solution.py:402
  57.3 1.8 %collective-permute-start.8 = (bf16[16,80,128]{2,1,0:T(8,128)(2,1)S(1)}, bf16[16,80,128]{2,1,0:T(8,128)(2,1)S(1)}, u32[]{:S(2)}, u32[]{:S(2)}) collective-permute-start(bf16[16,80,128]{2,1,0:T(8,128)(2,1)S(1)} %get-tuple-element.45), channel_id=1, source_target_pairs={{0,3},{1,0},{2,1},{3,2},{4,7},{5,4},{6,5},{7,6},{8,11},{9,8},{10,9... | collective-permute-start | bytes 983048 | tf_op jit(solution)/shard_map/ppermute | solution.py:402
  59.1 1.9 %mid_stepped.1 = (bf16[16,48,128]{2,1,0:T(8,128)(2,1)S(1)}, bf16[16,48,128]{2,1,0:T(8,128)(2,1)S(1)}, bf16[16,48,128]{2,1,0:T(8,128)(2,1)S(1)}, bf16[16,48,128]{2,1,0:T(8,128)(2,1)S(1)}) custom-call(s32[1]{0:T(128)} %bitcast.2.row_ref, s32[1]{0:T(128)} %bitcast.me_ref, s32[64]{0:T(128)S(1)} %bitcast.8, ...), custom_call_target="tpu_custom_call" | custom-call | flops 100100661248 | bytes 3670016 | tf_op jit(solution)/shard_map/mid_stepped/pallas_call | solution.py:318
  61.0 1.5 %collective-permute-start.12 = (bf16[16,48,128]{2,1,0:T(8,128)(2,1)S(1)}, bf16[16,48,128]{2,1,0:T(8,128)(2,1)S(1)}, u32[]{:S(2)}, u32[]{:S(2)}) collective-permute-start(bf16[16,48,128]{2,1,0:T(8,128)(2,1)S(1)} %get-tuple-element.50), channel_id=1, source_target_pairs={{0,2},{1,3},{2,0},{3,1},{4,6},{5,7},{6,4},{7,5},{8,10},{9,11},{10,... | collective-permute-start | bytes 589832 | tf_op jit(solution)/shard_map/ppermute | solution.py:402
  62.5 1.8 %collective-permute-start.13 = (bf16[16,48,128]{2,1,0:T(8,128)(2,1)S(1)}, bf16[16,48,128]{2,1,0:T(8,128)(2,1)S(1)}, u32[]{:S(2)}, u32[]{:S(2)}) collective-permute-start(bf16[16,48,128]{2,1,0:T(8,128)(2,1)S(1)} %get-tuple-element.51), channel_id=1, source_target_pairs={{0,1},{1,2},{2,3},{3,0},{4,5},{5,6},{6,7},{7,4},{8,9},{9,10},{10,1... | collective-permute-start | bytes 589832 | tf_op jit(solution)/shard_map/ppermute | solution.py:402
  64.5 2.8 %collective-permute-done.7.refs_1_ = bf16[16,80,128]{2,1,0:T(8,128)(2,1)S(1)} collective-permute-done((bf16[16,80,128]{2,1,0:T(8,128)(2,1)S(1)}, bf16[16,80,128]{2,1,0:T(8,128)(2,1)S(1)}, u32[]{:S(2)}, u32[]{:S(2)}) %collective-permute-start.7) | collective-permute-done | bytes 327712 | tf_op jit(solution)/shard_map/ppermute | solution.py:402
  67.3 2.7 %collective-permute-done.8.refs_2_ = bf16[16,80,128]{2,1,0:T(8,128)(2,1)S(1)} collective-permute-done((bf16[16,80,128]{2,1,0:T(8,128)(2,1)S(1)}, bf16[16,80,128]{2,1,0:T(8,128)(2,1)S(1)}, u32[]{:S(2)}, u32[]{:S(2)}) %collective-permute-start.8) | collective-permute-done | bytes 327712 | tf_op jit(solution)/shard_map/ppermute | solution.py:402
  70.1 8.9 %collective-permute-start.9 = (bf16[8,80,128]{2,1,0:T(8,128)(2,1)S(1)}, bf16[8,80,128]{2,1,0:T(8,128)(2,1)S(1)}, u32[]{:S(2)}, u32[]{:S(2)}) collective-permute-start(bf16[8,80,128]{2,1,0:T(8,128)(2,1)S(1)} %sum_other.2), channel_id=1, source_target_pairs={{0,4},{1,5},{2,6},{3,7},{4,0},{5,1},{6,2},{7,3},{8,12},{9,13},{10,... | collective-permute-start | bytes 491528 | tf_op jit(solution)/shard_map/ppermute | solution.py:407
  79.1 3.1 %collective-permute-start.15 = (bf16[8,48,128]{2,1,0:T(8,128)(2,1)S(1)}, bf16[8,48,128]{2,1,0:T(8,128)(2,1)S(1)}, u32[]{:S(2)}, u32[]{:S(2)}) collective-permute-start(bf16[8,48,128]{2,1,0:T(8,128)(2,1)S(1)} %sum_other.3), channel_id=1, source_target_pairs={{0,4},{1,5},{2,6},{3,7},{4,0},{5,1},{6,2},{7,3},{8,12},{9,13},{10,... | collective-permute-start | bytes 294920 | tf_op jit(solution)/shard_map/ppermute | solution.py:407
  82.1 6.6 %collective-permute-done.15.refs_8_ = bf16[8,48,128]{2,1,0:T(8,128)(2,1)S(1)} collective-permute-done((bf16[8,48,128]{2,1,0:T(8,128)(2,1)S(1)}, bf16[8,48,128]{2,1,0:T(8,128)(2,1)S(1)}, u32[]{:S(2)}, u32[]{:S(2)}) %collective-permute-start.15) | collective-permute-done | bytes 98336 | tf_op jit(solution)/shard_map/ppermute | solution.py:407
  88.7 1.6 %row_level.1 = bf16[8,128,128]{2,1,0:T(8,128)(2,1)} custom-call(s32[1]{0:T(128)} %bitcast.me_ref, s32[64]{0:T(128)S(1)} %copy-done.3, bf16[64,128,128]{2,1,0:T(8,128)(2,1)S(1)} %copy-done, bf16[16,80,128]{2,1,0:T(8,128)(2,1)S(1)} %get-tuple-element.40.refs_0_, bf16[16,80,128]{2,1,0:T(8,128)(2,1)S(1)} %collective-permute-done.7.refs_1_, ...), custom_call_target="tpu_custom_call" | custom-call | flops 33554432 | bytes 1048576 | tf_op jit(solution)/shard_map/row_level/pallas_call | solution.py:383
  (38 shorter events, 5.5 us)
Async XLA Ops:
  6.0 12.3 %copy-start.6 = (bf16[24,48,128]{2,1,0:T(8,128)(2,1)S(1)}, bf16[24,48,128]{2,1,0:T(8,128)(2,1)}, u32[]{:S(2)}) copy-start(bf16[24,48,128]{2,1,0:T(8,128)(2,1)} %get-tuple-element.34.refs_0_) | copy-start | bytes 884740
  6.0 12.2 %collective-permute-start = (bf16[16,48,128]{2,1,0:T(8,128)(2,1)}, bf16[16,48,128]{2,1,0:T(8,128)(2,1)S(1)}, u32[]{:S(2)}, u32[]{:S(2)}) collective-permute-start(bf16[16,48,128]{2,1,0:T(8,128)(2,1)} %get-tuple-element.33), channel_id=1, source_target_pairs={{0,192},{8,200},{16,208},{24,216},{32,224},{40,232},{48,240},{56,2... | collective-permute-start | bytes 589832 | tf_op jit(solution)/shard_map/ppermute | solution.py:411
  8.0 40.9 %all-to-all-start = ((bf16[64,80,128]{2,1,0:T(8,128)(2,1)}), bf16[64,80,128]{2,1,0:T(8,128)(2,1)S(1)}, u32[]{:S(2)}, u32[]{:S(2)}) async-start(bf16[64,80,128]{2,1,0:T(8,128)(2,1)} %get-tuple-element.29), calls=%async_computation | async-start | bytes 2621440 | tf_op jit(solution)/shard_map/all_to_all | solution.py:428
  18.3 1.8 %copy-start.2 = (bf16[24,48,128]{2,1,0:T(8,128)(2,1)S(1)}, bf16[24,48,128]{2,1,0:T(8,128)(2,1)}, u32[]{:S(2)}) copy-start(bf16[24,48,128]{2,1,0:T(8,128)(2,1)} %get-tuple-element.32.refs_0_) | copy-start | bytes 884740
  18.3 8.0 %copy-start.1 = (bf16[1,64,128,128]{3,2,1,0:T(8,128)(2,1)S(1)}, bf16[1,64,128,128]{3,2,1,0:T(8,128)(2,1)}, u32[]{:S(2)}) copy-start(bf16[1,64,128,128]{3,2,1,0:T(8,128)(2,1)} %param.12) | copy-start | bytes 6291460
  18.3 1.8 %collective-permute-start.1 = (bf16[32,48,128]{2,1,0:T(8,128)(2,1)S(1)}, bf16[32,48,128]{2,1,0:T(8,128)(2,1)S(1)}, u32[]{:S(2)}, u32[]{:S(2)}) collective-permute-start(bf16[32,48,128]{2,1,0:T(8,128)(2,1)S(1)} %regroup.3), channel_id=1, source_target_pairs={{0,8},{8,0},{16,24},{24,16},{32,40},{40,32},{48,56},{56,48},{64,72... | collective-permute-start | bytes 1179656 | tf_op jit(solution)/shard_map/ppermute | solution.py:411
  20.2 28.8 %copy-start.7 = (s32[1,64]{1,0:T(1,128)S(1)}, s32[1,64]{1,0:T(1,128)}, u32[]{:S(2)}) copy-start(s32[1,64]{1,0:T(1,128)} %param.13) | copy-start | bytes 772
  20.2 11.4 %collective-permute-start.2 = (bf16[16,48,128]{2,1,0:T(8,128)(2,1)S(1)}, bf16[16,48,128]{2,1,0:T(8,128)(2,1)S(1)}, u32[]{:S(2)}, u32[]{:S(2)}) collective-permute-start(bf16[16,48,128]{2,1,0:T(8,128)(2,1)S(1)} %get-tuple-element.35), channel_id=1, source_target_pairs={{0,16},{8,24},{16,0},{24,8},{32,48},{40,56},{48,32},{56,40},{64,80... | collective-permute-start | bytes 589832 | tf_op jit(solution)/shard_map/ppermute | solution.py:411
  21.6 20.8 %collective-permute-start.3 = (bf16[16,48,128]{2,1,0:T(8,128)(2,1)S(1)}, bf16[16,48,128]{2,1,0:T(8,128)(2,1)S(1)}, u32[]{:S(2)}, u32[]{:S(2)}) collective-permute-start(bf16[16,48,128]{2,1,0:T(8,128)(2,1)S(1)} %get-tuple-element.36), channel_id=1, source_target_pairs={{0,32},{8,40},{16,48},{24,56},{32,0},{40,8},{48,16},{56,24},{64,96... | collective-permute-start | bytes 589832 | tf_op jit(solution)/shard_map/ppermute | solution.py:411
  26.3 17.1 %collective-permute-start.4 = (bf16[16,48,128]{2,1,0:T(8,128)(2,1)S(1)}, bf16[16,48,128]{2,1,0:T(8,128)(2,1)S(1)}, u32[]{:S(2)}, u32[]{:S(2)}) collective-permute-start(bf16[16,48,128]{2,1,0:T(8,128)(2,1)S(1)} %get-tuple-element.37), channel_id=1, source_target_pairs={{0,48},{8,56},{16,32},{24,40},{32,16},{40,24},{48,0},{56,8},{64,11... | collective-permute-start | bytes 589832 | tf_op jit(solution)/shard_map/ppermute | solution.py:411
  44.2 14.9 %collective-permute-start.10 = (bf16[16,48,128]{2,1,0:T(8,128)(2,1)}, bf16[16,48,128]{2,1,0:T(8,128)(2,1)}, u32[]{:S(2)}, u32[]{:S(2)}) collective-permute-start(bf16[16,48,128]{2,1,0:T(8,128)(2,1)} %get-tuple-element.38.after_ref), channel_id=1, source_target_pairs={{0,64},{8,72},{16,80},{24,88},{32,96},{40,104},{48,112},{56,120},{... | collective-permute-start | bytes 589832 | tf_op jit(solution)/shard_map/ppermute | solution.py:411
  44.2 14.9 %collective-permute-start.11 = (bf16[16,48,128]{2,1,0:T(8,128)(2,1)}, bf16[16,48,128]{2,1,0:T(8,128)(2,1)}, u32[]{:S(2)}, u32[]{:S(2)}) collective-permute-start(bf16[16,48,128]{2,1,0:T(8,128)(2,1)} %get-tuple-element.47), channel_id=1, source_target_pairs={{0,128},{8,136},{16,144},{24,152},{32,160},{40,168},{48,176},{56,1... | collective-permute-start | bytes 589832 | tf_op jit(solution)/shard_map/ppermute | solution.py:411
  49.0 3.0 %copy-start.5 = (bf16[48,128,128]{2,1,0:T(8,128)(2,1)S(1)}, bf16[48,128,128]{2,1,0:T(8,128)(2,1)}, u32[]{:S(2)}) copy-start(bf16[48,128,128]{2,1,0:T(8,128)(2,1)} %copy-done.4) | copy-start | bytes 4718596
  49.8 5.4 %collective-permute-start.5 = (bf16[8,80,128]{2,1,0:T(8,128)(2,1)S(1)}, bf16[8,80,128]{2,1,0:T(8,128)(2,1)S(1)}, u32[]{:S(2)}, u32[]{:S(2)}) collective-permute-start(bf16[8,80,128]{2,1,0:T(8,128)(2,1)S(1)} %get-tuple-element.39.after_ref), channel_id=1, source_target_pairs={{0,1},{1,2},{2,3},{3,0},{4,5},{5,6},{6,7},{7,4},{8,9},{9,10},{10,1... | collective-permute-start | bytes 491528 | tf_op jit(solution)/shard_map/ppermute | solution.py:402
  50.4 6.5 %collective-permute-start.6 = (bf16[8,80,128]{2,1,0:T(8,128)(2,1)S(1)}, bf16[8,80,128]{2,1,0:T(8,128)(2,1)S(1)}, u32[]{:S(2)}, u32[]{:S(2)}) collective-permute-start(bf16[8,80,128]{2,1,0:T(8,128)(2,1)S(1)} %get-tuple-element.43), channel_id=1, source_target_pairs={{0,3},{1,0},{2,1},{3,2},{4,7},{5,4},{6,5},{7,6},{8,11},{9,8},{10,9... | collective-permute-start | bytes 491528 | tf_op jit(solution)/shard_map/ppermute | solution.py:402
  57.0 10.3 %collective-permute-start.7 = (bf16[16,80,128]{2,1,0:T(8,128)(2,1)S(1)}, bf16[16,80,128]{2,1,0:T(8,128)(2,1)S(1)}, u32[]{:S(2)}, u32[]{:S(2)}) collective-permute-start(bf16[16,80,128]{2,1,0:T(8,128)(2,1)S(1)} %get-tuple-element.44), channel_id=1, source_target_pairs={{0,1},{1,2},{2,3},{3,0},{4,5},{5,6},{6,7},{7,4},{8,9},{9,10},{10,1... | collective-permute-start | bytes 983048 | tf_op jit(solution)/shard_map/ppermute | solution.py:402
  57.3 12.7 %collective-permute-start.8 = (bf16[16,80,128]{2,1,0:T(8,128)(2,1)S(1)}, bf16[16,80,128]{2,1,0:T(8,128)(2,1)S(1)}, u32[]{:S(2)}, u32[]{:S(2)}) collective-permute-start(bf16[16,80,128]{2,1,0:T(8,128)(2,1)S(1)} %get-tuple-element.45), channel_id=1, source_target_pairs={{0,3},{1,0},{2,1},{3,2},{4,7},{5,4},{6,5},{7,6},{8,11},{9,8},{10,9... | collective-permute-start | bytes 983048 | tf_op jit(solution)/shard_map/ppermute | solution.py:402
  59.1 29.6 %copy-start = (bf16[64,128,128]{2,1,0:T(8,128)(2,1)S(1)}, bf16[64,128,128]{2,1,0:T(8,128)(2,1)}, u32[]{:S(2)}) copy-start(bf16[64,128,128]{2,1,0:T(8,128)(2,1)} %w_ref.3) | copy-start | bytes 6291460
  59.1 29.6 %copy-start.3 = (s32[64]{0:T(128)S(1)}, s32[64]{0:T(128)}, u32[]{:S(2)}) copy-start(s32[64]{0:T(128)} %rank_ref.3) | copy-start | bytes 772
  61.0 17.9 %collective-permute-start.12 = (bf16[16,48,128]{2,1,0:T(8,128)(2,1)S(1)}, bf16[16,48,128]{2,1,0:T(8,128)(2,1)S(1)}, u32[]{:S(2)}, u32[]{:S(2)}) collective-permute-start(bf16[16,48,128]{2,1,0:T(8,128)(2,1)S(1)} %get-tuple-element.50), channel_id=1, source_target_pairs={{0,2},{1,3},{2,0},{3,1},{4,6},{5,7},{6,4},{7,5},{8,10},{9,11},{10,... | collective-permute-start | bytes 589832 | tf_op jit(solution)/shard_map/ppermute | solution.py:402
  62.5 16.5 %collective-permute-start.13 = (bf16[16,48,128]{2,1,0:T(8,128)(2,1)S(1)}, bf16[16,48,128]{2,1,0:T(8,128)(2,1)S(1)}, u32[]{:S(2)}, u32[]{:S(2)}) collective-permute-start(bf16[16,48,128]{2,1,0:T(8,128)(2,1)S(1)} %get-tuple-element.51), channel_id=1, source_target_pairs={{0,1},{1,2},{2,3},{3,0},{4,5},{5,6},{6,7},{7,4},{8,9},{9,10},{10,1... | collective-permute-start | bytes 589832 | tf_op jit(solution)/shard_map/ppermute | solution.py:402
  64.3 14.7 %collective-permute-start.14 = (bf16[16,48,128]{2,1,0:T(8,128)(2,1)S(1)}, bf16[16,48,128]{2,1,0:T(8,128)(2,1)S(1)}, u32[]{:S(2)}, u32[]{:S(2)}) collective-permute-start(bf16[16,48,128]{2,1,0:T(8,128)(2,1)S(1)} %get-tuple-element.52), channel_id=1, source_target_pairs={{0,3},{1,0},{2,1},{3,2},{4,7},{5,4},{6,5},{7,6},{8,11},{9,8},{10,9... | collective-permute-start | bytes 589832 | tf_op jit(solution)/shard_map/ppermute | solution.py:402
  70.1 18.6 %collective-permute-start.9 = (bf16[8,80,128]{2,1,0:T(8,128)(2,1)S(1)}, bf16[8,80,128]{2,1,0:T(8,128)(2,1)S(1)}, u32[]{:S(2)}, u32[]{:S(2)}) collective-permute-start(bf16[8,80,128]{2,1,0:T(8,128)(2,1)S(1)} %sum_other.2), channel_id=1, source_target_pairs={{0,4},{1,5},{2,6},{3,7},{4,0},{5,1},{6,2},{7,3},{8,12},{9,13},{10,... | collective-permute-start | bytes 491528 | tf_op jit(solution)/shard_map/ppermute | solution.py:407
  79.1 9.7 %collective-permute-start.15 = (bf16[8,48,128]{2,1,0:T(8,128)(2,1)S(1)}, bf16[8,48,128]{2,1,0:T(8,128)(2,1)S(1)}, u32[]{:S(2)}, u32[]{:S(2)}) collective-permute-start(bf16[8,48,128]{2,1,0:T(8,128)(2,1)S(1)} %sum_other.3), channel_id=1, source_target_pairs={{0,4},{1,5},{2,6},{3,7},{4,0},{5,1},{6,2},{7,3},{8,12},{9,13},{10,... | collective-permute-start | bytes 294920 | tf_op jit(solution)/shard_map/ppermute | solution.py:407
  (1 other events, 1.2 us)
